TPU v7x, 256 devices: a whole 4x4x8 slice. The times are simulated.
256 devices in a mesh: batch: 4 (over y), seq: 64 (over x, z, core).
Axes of the slice: x: 4, y: 4, z: 8, core: 2. Of those that a mesh axis runs over, the one named last changes fastest.
Arguments:
- query: bfloat16 [4, 8192, 1024], P('batch', 'seq'), may hold values from -6 to 6
- key: bfloat16 [4, 8192, 1024], P('batch', 'seq'), may hold values from -6 to 6
- value: bfloat16 [4, 8192, 1024], P('batch', 'seq'), may hold values from -6 to 6
- grad_attn: bfloat16 [4, 8192, 1024], P('batch', 'seq'), may hold values from -6 to 6
- scale_ids: int32 [4, 8192], P('batch', 'seq'), may hold values from 0 to 12, never falling along the last dimension, each value on 1 to 3276 neighbouring positions
Outputs:
- attn_out: bfloat16 [4, 8192, 1024], P('batch', 'seq')
- query_grad: bfloat16 [4, 8192, 1024], P('batch', 'seq')
- key_grad: bfloat16 [4, 8192, 1024], P('batch', 'seq')
- value_grad: bfloat16 [4, 8192, 1024], P('batch', 'seq')
Inputs may be any that keep to these rules, and one draw needn't show every extreme that they name: `scale_ids`: along each image's positions the scale id never falls; every id occurs; no scale has more than 3276 positions and one has exactly that many.
All inputs are finite; a program needn't handle non-finite values.
Results may differ from a plain program's by a relative error of at most 0.03.
Values may be sent and summed in bfloat16 or wider, within the bound.
No kernel may reach another device: no remote copies, remote signals or barrier semaphores. Data moves between devices by JAX's collectives and lax.ppermute only.
A program may use at most 128 MiB of HBM per device.

v0:
```python
import jax
import jax.numpy as jnp
from jax import lax
from jax.sharding import PartitionSpec as P

HEADS = 8
HDIM = 128


def local(query, key, value, grad_attn, scale_ids):
    rows = query.shape[1]
    width = query.shape[2]
    devices = lax.axis_size("seq")
    groups = devices // HEADS
    share = rows // groups
    member = lax.axis_index("seq") % groups
    inv_root = HDIM ** (-0.5)
    own_scale = scale_ids[0].astype(jnp.bfloat16)

    def by_share(arr):
        return (
            arr.reshape(groups, share, HEADS, HDIM)
            .transpose(2, 0, 1, 3)
            .reshape(devices, share, HDIM)
        )

    def by_head(arr):
        heads = arr.reshape(rows, HEADS, HDIM).transpose(1, 0, 2)
        return jnp.broadcast_to(heads[:, None], (HEADS, groups, rows, HDIM)).reshape(
            devices, rows, HDIM
        )

    def to_rows(arr):
        return arr.reshape(HEADS, groups, share, HDIM).transpose(1, 2, 0, 3).reshape(rows, width)

    scale_rows = jnp.broadcast_to(own_scale[None, :], (devices, rows))
    q_in, do_in, k_in, v_in, s_in = (
        lax.all_to_all(by_share(query[0]), "seq", split_axis=0, concat_axis=0, tiled=True),
        lax.all_to_all(by_share(grad_attn[0]), "seq", split_axis=0, concat_axis=0, tiled=True),
        lax.all_to_all(by_head(key[0]), "seq", split_axis=0, concat_axis=0, tiled=True),
        lax.all_to_all(by_head(value[0]), "seq", split_axis=0, concat_axis=0, tiled=True),
        lax.all_to_all(scale_rows, "seq", split_axis=0, concat_axis=0, tiled=True),
    )
    keys = k_in.reshape(devices * rows, HDIM)
    values = v_in.reshape(devices * rows, HDIM)
    key_scale = s_in.reshape(devices * rows).astype(jnp.float32)
    q_scale = (
        lax.dynamic_slice_in_dim(s_in, member * share, share, 1)
        .reshape(devices * share)
        .astype(jnp.float32)
    )
    q_all = q_in.reshape(devices * share, HDIM)
    do_all = do_in.reshape(devices * share, HDIM)
    count = q_all.shape[0]
    block = min(512, count)
    total = keys.shape[0]

    def step(carry, index):
        start = index * block
        q_block = lax.dynamic_slice_in_dim(q_all, start, block, 0)
        do_block = lax.dynamic_slice_in_dim(do_all, start, block, 0)
        qs_block = lax.dynamic_slice_in_dim(q_scale, start, block, 0)
        scores = (
            jnp.einsum("qd,kd->qk", q_block, keys, preferred_element_type=jnp.float32) * inv_root
        )
        scores = jnp.where(key_scale[None, :] <= qs_block[:, None], scores, -1e30)
        top = jnp.max(scores, axis=1, keepdims=True)
        lse = top + jnp.log(jnp.sum(jnp.exp(scores - top), axis=1, keepdims=True))
        probs = jnp.exp(scores - lse)
        weights = probs.astype(jnp.bfloat16)
        attn = jnp.dot(weights, values, preferred_element_type=jnp.float32).astype(jnp.bfloat16)
        delta = jnp.sum(
            do_block.astype(jnp.float32) * attn.astype(jnp.float32), axis=1, keepdims=True
        )
        dprobs = jnp.einsum("qd,kd->qk", do_block, values, preferred_element_type=jnp.float32)
        dscores = (probs * (dprobs - delta) * inv_root).astype(jnp.bfloat16)
        q_grad = jnp.dot(dscores, keys, preferred_element_type=jnp.float32).astype(jnp.bfloat16)
        key_next = carry[0] + jnp.einsum(
            "qk,qd->kd", dscores, q_block, preferred_element_type=jnp.float32
        )
        value_next = carry[1] + jnp.einsum(
            "qk,qd->kd", weights, do_block, preferred_element_type=jnp.float32
        )
        return ((key_next, value_next), (attn, q_grad))

    zeros = jnp.zeros((total, HDIM), jnp.float32)
    (key_acc, value_acc), (attn_blocks, qgrad_blocks) = lax.scan(
        step, (zeros, zeros), jnp.arange(count // block)
    )
    attn_back, qgrad_back = (
        lax.all_to_all(
            attn_blocks.reshape(devices, share, HDIM),
            "seq",
            split_axis=0,
            concat_axis=0,
            tiled=True,
        ),
        lax.all_to_all(
            qgrad_blocks.reshape(devices, share, HDIM),
            "seq",
            split_axis=0,
            concat_axis=0,
            tiled=True,
        ),
    )
    attn_out = to_rows(attn_back)
    query_grad = to_rows(qgrad_back)
    key_in, value_in = (
        lax.all_to_all(
            key_acc.reshape(devices, rows, HDIM).astype(jnp.bfloat16),
            "seq",
            split_axis=0,
            concat_axis=0,
            tiled=True,
        ).astype(jnp.float32),
        lax.all_to_all(
            value_acc.reshape(devices, rows, HDIM).astype(jnp.bfloat16),
            "seq",
            split_axis=0,
            concat_axis=0,
            tiled=True,
        ).astype(jnp.float32),
    )
    key_sum = (
        key_in.reshape(HEADS, groups, rows, HDIM)
        .sum(axis=1)
        .transpose(1, 0, 2)
        .reshape(rows, width)
    )
    value_sum = (
        value_in.reshape(HEADS, groups, rows, HDIM)
        .sum(axis=1)
        .transpose(1, 0, 2)
        .reshape(rows, width)
    )
    key_grad = key_sum.astype(jnp.bfloat16)
    value_grad = value_sum.astype(jnp.bfloat16)
    return (attn_out[None], query_grad[None], key_grad[None], value_grad[None])


def solution(mesh):
    in_specs = (
        P("batch", "seq", None),
        P("batch", "seq", None),
        P("batch", "seq", None),
        P("batch", "seq", None),
        P("batch", "seq"),
    )
    out_specs = (
        P("batch", "seq", None),
        P("batch", "seq", None),
        P("batch", "seq", None),
        P("batch", "seq", None),
    )
    return jax.shard_map(local, mesh=mesh, in_specs=in_specs, out_specs=out_specs, check_vma=False)
```

profile of v0, /device:TPU:16, one launch (start us, length us, event | category | flops | bytes accessed | tf_op | source)
XLA Modules:
  0.0 444.3 jit_solution(10812819749352126272)
XLA Ops:
  2.0 11.9 %all-to-all-start = ((bf16[64,1,128]{2,1,0:T(2,128)(2,1)}), bf16[64,1,128]{2,1,0:T(2,128)(2,1)S(1)}, u32[]{:S(2)}, u32[]{:S(2)}) async-start(bf16[64,1,128]{2,1,0:T(2,128)(2,1)} %broadcast_in_dim.19), calls=%async_computation | async-start | bytes 65536 | tf_op jit(solution)/shard_map/all_to_all | solution.py:42
  15.7 7.6 %all-to-all-done = bf16[64,1,128]{2,1,0:T(2,128)(2,1)S(1)} async-done(((bf16[64,1,128]{2,1,0:T(2,128)(2,1)}), bf16[64,1,128]{2,1,0:T(2,128)(2,1)S(1)}, u32[]{:S(2)}, u32[]{:S(2)}) %all-to-all-start) | async-done | bytes 16416 | tf_op jit(solution)/shard_map/all_to_all | solution.py:42
  23.3 4.6 %all-to-all-start.1 = ((bf16[64,16,128]{2,1,0:T(8,128)(2,1)}), bf16[64,16,128]{2,1,0:T(8,128)(2,1)S(1)}, u32[]{:S(2)}, u32[]{:S(2)}) async-start(bf16[64,16,128]{2,1,0:T(8,128)(2,1)} %bitcast.3), calls=%async_computation.1 | async-start | bytes 524288 | tf_op jit(solution)/shard_map/all_to_all | solution.py:38
  29.7 10.2 %all-to-all-done.1 = bf16[64,16,128]{2,1,0:T(8,128)(2,1)S(1)} async-done(((bf16[64,16,128]{2,1,0:T(8,128)(2,1)}), bf16[64,16,128]{2,1,0:T(8,128)(2,1)S(1)}, u32[]{:S(2)}, u32[]{:S(2)}) %all-to-all-start.1) | async-done | bytes 262176 | tf_op jit(solution)/shard_map/all_to_all | solution.py:38
  40.0 6.0 %all-to-all-start.3 = ((bf16[64,16,128]{2,1,0:T(8,128)(2,1)}), bf16[64,16,128]{2,1,0:T(8,128)(2,1)S(1)}, u32[]{:S(2)}, u32[]{:S(2)}) async-start(bf16[64,16,128]{2,1,0:T(8,128)(2,1)} %bitcast.9), calls=%async_computation.3 | async-start | bytes 524288 | tf_op jit(solution)/shard_map/all_to_all | solution.py:39
  47.1 10.9 %all-to-all-done.3 = bf16[64,16,128]{2,1,0:T(8,128)(2,1)S(1)} async-done(((bf16[64,16,128]{2,1,0:T(8,128)(2,1)}), bf16[64,16,128]{2,1,0:T(8,128)(2,1)S(1)}, u32[]{:S(2)}, u32[]{:S(2)}) %all-to-all-start.3) | async-done | bytes 262176 | tf_op jit(solution)/shard_map/all_to_all | solution.py:39
  59.9 6.0 %all-to-all-start.4 = ((bf16[64,128,128]{2,1,0:T(8,128)(2,1)}), bf16[64,128,128]{2,1,0:T(8,128)(2,1)S(1)}, u32[]{:S(2)}, u32[]{:S(2)}) async-start(bf16[64,128,128]{2,1,0:T(8,128)(2,1)} %bitcast.96), calls=%async_computation.4 | async-start | bytes 4194304 | tf_op jit(solution)/shard_map/all_to_all | solution.py:41
  66.0 51.1 %all-to-all-done.4 = bf16[64,128,128]{2,1,0:T(8,128)(2,1)S(1)} async-done(((bf16[64,128,128]{2,1,0:T(8,128)(2,1)}), bf16[64,128,128]{2,1,0:T(8,128)(2,1)S(1)}, u32[]{:S(2)}, u32[]{:S(2)}) %all-to-all-start.4) | async-done | bytes 2097184 | tf_op jit(solution)/shard_map/all_to_all | solution.py:41
  119.0 6.1 %all-to-all-start.2 = ((bf16[64,128,128]{2,1,0:T(8,128)(2,1)}), bf16[64,128,128]{2,1,0:T(8,128)(2,1)}, u32[]{:S(2)}, u32[]{:S(2)}) async-start(bf16[64,128,128]{2,1,0:T(8,128)(2,1)} %bitcast.95), calls=%async_computation.2 | async-start | bytes 4194304 | tf_op jit(solution)/shard_map/all_to_all | solution.py:40
  125.4 50.7 %all-to-all-done.2 = bf16[64,128,128]{2,1,0:T(8,128)(2,1)} async-done(((bf16[64,128,128]{2,1,0:T(8,128)(2,1)}), bf16[64,128,128]{2,1,0:T(8,128)(2,1)}, u32[]{:S(2)}, u32[]{:S(2)}) %all-to-all-start.2) | async-done | bytes 2097184 | tf_op jit(solution)/shard_map/all_to_all | solution.py:40
  176.1 115.1 %while.17 = (s32[]{:T(128)}, f32[8192,128]{1,0:T(8,128)}, f32[8192,128]{1,0:T(8,128)}, bf16[2,512,128]{2,1,0:T(8,128)(2,1)}, bf16[2,512,128]{2,1,0:T(8,128)(2,1)...) while((s32[]{:T(128)}, f32[8192,128]{1,0:T(8,128)}, ...), condition=%wide.region_4.5_spmd.clone, body=%wide.region_0.4_spmd.clone.sunk | while | flops 6509952000 | bytes 169799984 | solution.py:87
  177.6 8.8 %fusion.40 = (f32[512]{0:T(512)S(1)}, f32[512,8192]{1,0:T(8,128)}) fusion(bf16[8192,128]{1,0:T(8,128)(2,1)} %get-tuple-element.326, bf16[1024,128]{1,0:T(8,128)(2,1)S(1)} %get-tuple-element.325, s32[]{:T(128)S(6)} %select_n.25, f32[512]{0:T(512)S(1)} %dynamic_slice.38, f32[8192]{0:T(1024)S(1)} %get-tuple-element.322), kind=kOutput, calls=%fused_computation.24.clone.1 | convolution fusion | flops 1090518528 | bytes 19042308 | tf_op jit(solution)/shard_map/while/body/eval_jaxpr/qd,kd->qk/dot_general | solution.py:64
  186.4 8.1 %exponential_reduce_fusion.2 = f32[512]{0:T(512)S(1)} fusion(f32[512,8192]{1,0:T(8,128)} %get-tuple-element.281, f32[512]{0:T(512)S(1)} %get-tuple-element.282), kind=kLoop, calls=%fused_computation.2.clone.1 | loop fusion | flops 8388096 | bytes 16781312 | tf_op jit(solution)/shard_map/while/body/eval_jaxpr/reduce_sum | solution.py:68
  194.5 8.8 %multiply_reduce_fusion.2 = (f32[512]{0:T(512)S(1)}, bf16[512,128]{0,1:T(8,128)(2,1)S(1)}) fusion(bf16[512,128]{0,1:T(8,128)(2,1)S(1)} %copy.63, bf16[8192,128]{1,0:T(8,128)(2,1)S(1)} %get-tuple-element.328, f32[512,8192]{1,0:T(8,128)} %get-tuple-element.281, f32[512]{0:T(512)S(1)} %log_add_fusion.2), kind=kOutput, calls=%fused_computation.11.clone.1 | convolution fusion | flops 1082457600 | bytes 19140608 | tf_op jit(solution)/shard_map/while/body/eval_jaxpr/dot_general | solution.py:71
  204.1 11.0 %convolution_add_fusion.5 = f32[8192,128]{1,0:T(8,128)} fusion(bf16[512,128]{1,0:T(8,128)(2,1)S(1)} %constant_dynamic-slice_fusion.2, f32[8192,128]{1,0:T(8,128)} %get-tuple-element.303, pred[]{:T(512)S(6)} %compare.4, f32[512,8192]{1,0:T(8,128)} %get-tuple-element.281, f32[512]{0:T(512)S(1)} %log_add_fusion.2), kind=kOutput, calls=%fused_computation.5.clone.1 | convolution fusion | flops 1084227584 | bytes 25298944 | tf_op jit(solution)/shard_map/while/body/eval_jaxpr/qk,qd->kd/dot_general | solution.py:81
  215.1 8.0 %multiply_convert_fusion.2 = bf16[512,8192]{1,0:T(8,128)(2,1)S(1)} fusion(f32[512,8192]{1,0:T(8,128)} %get-tuple-element.281, bf16[512,128]{1,0:T(8,128)(2,1)S(1)} %constant_dynamic-slice_fusion.2, bf16[8192,128]{1,0:T(8,128)(2,1)S(1)} %get-tuple-element.328, f32[512]{0:T(512)S(1)} %get-tuple-element.283, f32[512]{0:T(512)S(1)} %log_add_fusion.2), kind=kOutput, calls=%fused_computation.clone.1 | convolution fusion | flops 1094713344 | bytes 27398144 | tf_op jit(solution)/shard_map/while/body/eval_jaxpr/qd,kd->qk/dot_general | solution.py:75
  223.2 4.1 fusion.41
  227.3 3.8 convolution_add_fusion.4
  234.5 8.8 %fusion.40 = (f32[512]{0:T(512)S(1)}, f32[512,8192]{1,0:T(8,128)}) fusion(bf16[8192,128]{1,0:T(8,128)(2,1)} %get-tuple-element.326, bf16[1024,128]{1,0:T(8,128)(2,1)S(1)} %get-tuple-element.325, s32[]{:T(128)S(6)} %select_n.25, f32[512]{0:T(512)S(1)} %dynamic_slice.38, f32[8192]{0:T(1024)S(1)} %get-tuple-element.322), kind=kOutput, calls=%fused_computation.24.clone.1 | convolution fusion | flops 1090518528 | bytes 19042308 | tf_op jit(solution)/shard_map/while/body/eval_jaxpr/qd,kd->qk/dot_general | solution.py:64
  243.4 8.1 %exponential_reduce_fusion.2 = f32[512]{0:T(512)S(1)} fusion(f32[512,8192]{1,0:T(8,128)} %get-tuple-element.281, f32[512]{0:T(512)S(1)} %get-tuple-element.282), kind=kLoop, calls=%fused_computation.2.clone.1 | loop fusion | flops 8388096 | bytes 16781312 | tf_op jit(solution)/shard_map/while/body/eval_jaxpr/reduce_sum | solution.py:68
  251.5 8.8 %multiply_reduce_fusion.2 = (f32[512]{0:T(512)S(1)}, bf16[512,128]{0,1:T(8,128)(2,1)S(1)}) fusion(bf16[512,128]{0,1:T(8,128)(2,1)S(1)} %copy.63, bf16[8192,128]{1,0:T(8,128)(2,1)S(1)} %get-tuple-element.328, f32[512,8192]{1,0:T(8,128)} %get-tuple-element.281, f32[512]{0:T(512)S(1)} %log_add_fusion.2), kind=kOutput, calls=%fused_computation.11.clone.1 | convolution fusion | flops 1082457600 | bytes 19140608 | tf_op jit(solution)/shard_map/while/body/eval_jaxpr/dot_general | solution.py:71
  261.1 12.2 %convolution_add_fusion.5 = f32[8192,128]{1,0:T(8,128)} fusion(bf16[512,128]{1,0:T(8,128)(2,1)S(1)} %constant_dynamic-slice_fusion.2, f32[8192,128]{1,0:T(8,128)} %get-tuple-element.303, pred[]{:T(512)S(6)} %compare.4, f32[512,8192]{1,0:T(8,128)} %get-tuple-element.281, f32[512]{0:T(512)S(1)} %log_add_fusion.2), kind=kOutput, calls=%fused_computation.5.clone.1 | convolution fusion | flops 1084227584 | bytes 25298944 | tf_op jit(solution)/shard_map/while/body/eval_jaxpr/qk,qd->kd/dot_general | solution.py:81
  273.2 8.0 %multiply_convert_fusion.2 = bf16[512,8192]{1,0:T(8,128)(2,1)S(1)} fusion(f32[512,8192]{1,0:T(8,128)} %get-tuple-element.281, bf16[512,128]{1,0:T(8,128)(2,1)S(1)} %constant_dynamic-slice_fusion.2, bf16[8192,128]{1,0:T(8,128)(2,1)S(1)} %get-tuple-element.328, f32[512]{0:T(512)S(1)} %get-tuple-element.283, f32[512]{0:T(512)S(1)} %log_add_fusion.2), kind=kOutput, calls=%fused_computation.clone.1 | convolution fusion | flops 1094713344 | bytes 27398144 | tf_op jit(solution)/shard_map/while/body/eval_jaxpr/qd,kd->qk/dot_general | solution.py:75
  281.3 4.1 fusion.41
  285.5 3.8 convolution_add_fusion.4
  291.2 17.7 %all_to_all.46 = bf16[64,16,128]{2,1,0:T(8,128)(2,1)S(1)} all-to-all(bf16[64,16,128]{2,1,0:T(8,128)(2,1)S(1)} %bitcast.113), channel_id=1, replica_groups=mesh['batch'=4,'seq'=64] {'seq'}, dimensions={0} | all-to-all | bytes 524288 | tf_op jit(solution)/shard_map/all_to_all | solution.py:98
  308.9 6.0 %all-to-all-start.5 = ((bf16[64,16,128]{2,1,0:T(8,128)(2,1)}), bf16[64,16,128]{2,1,0:T(8,128)(2,1)S(1)}, u32[]{:S(2)}, u32[]{:S(2)}) async-start(bf16[64,16,128]{2,1,0:T(8,128)(2,1)} %bitcast.14), calls=%async_computation.5 | async-start | bytes 524288 | tf_op jit(solution)/shard_map/all_to_all | solution.py:91
  318.7 8.3 %all-to-all-done.5 = bf16[64,16,128]{2,1,0:T(8,128)(2,1)S(1)} async-done(((bf16[64,16,128]{2,1,0:T(8,128)(2,1)}), bf16[64,16,128]{2,1,0:T(8,128)(2,1)S(1)}, u32[]{:S(2)}, u32[]{:S(2)}) %all-to-all-start.5) | async-done | bytes 262176 | tf_op jit(solution)/shard_map/all_to_all | solution.py:91
  326.9 6.0 %all-to-all-start.7 = ((bf16[64,128,128]{2,1,0:T(8,128)(2,1)}), bf16[64,128,128]{2,1,0:T(8,128)(2,1)S(1)}, u32[]{:S(2)}, u32[]{:S(2)}) async-start(bf16[64,128,128]{2,1,0:T(8,128)(2,1)} %bitcast.20), calls=%async_computation.7 | async-start | bytes 4194304 | tf_op jit(solution)/shard_map/all_to_all | solution.py:109
  336.7 47.5 %all-to-all-done.7 = bf16[64,128,128]{2,1,0:T(8,128)(2,1)S(1)} async-done(((bf16[64,128,128]{2,1,0:T(8,128)(2,1)}), bf16[64,128,128]{2,1,0:T(8,128)(2,1)S(1)}, u32[]{:S(2)}, u32[]{:S(2)}) %all-to-all-start.7) | async-done | bytes 2097184 | tf_op jit(solution)/shard_map/all_to_all | solution.py:109
  384.2 6.1 %all-to-all-start.8 = ((bf16[64,128,128]{2,1,0:T(8,128)(2,1)}), bf16[64,128,128]{2,1,0:T(8,128)(2,1)}, u32[]{:S(2)}, u32[]{:S(2)}) async-start(bf16[64,128,128]{2,1,0:T(8,128)(2,1)} %bitcast.24), calls=%async_computation.8 | async-start | bytes 4194304 | tf_op jit(solution)/shard_map/all_to_all | solution.py:116
  393.7 47.7 %all-to-all-done.8 = bf16[64,128,128]{2,1,0:T(8,128)(2,1)} async-done(((bf16[64,128,128]{2,1,0:T(8,128)(2,1)}), bf16[64,128,128]{2,1,0:T(8,128)(2,1)}, u32[]{:S(2)}, u32[]{:S(2)}) %all-to-all-start.8) | async-done | bytes 2097184 | tf_op jit(solution)/shard_map/all_to_all | solution.py:116
  (57 shorter events, 30.7 us)
Async XLA Ops:
  0.6 65.3 %copy-start.2 = (bf16[1,128,1024]{2,1,0:T(8,128)(2,1)S(1)}, bf16[1,128,1024]{2,1,0:T(8,128)(2,1)}, u32[]{:S(2)}) copy-start(bf16[1,128,1024]{2,1,0:T(8,128)(2,1)} %param.8) | copy-start | bytes 786436
  2.0 21.4 %all-to-all-start = ((bf16[64,1,128]{2,1,0:T(2,128)(2,1)}), bf16[64,1,128]{2,1,0:T(2,128)(2,1)S(1)}, u32[]{:S(2)}, u32[]{:S(2)}) async-start(bf16[64,1,128]{2,1,0:T(2,128)(2,1)} %broadcast_in_dim.19), calls=%async_computation | async-start | bytes 65536 | tf_op jit(solution)/shard_map/all_to_all | solution.py:42
  23.3 16.6 %all-to-all-start.1 = ((bf16[64,16,128]{2,1,0:T(8,128)(2,1)}), bf16[64,16,128]{2,1,0:T(8,128)(2,1)S(1)}, u32[]{:S(2)}, u32[]{:S(2)}) async-start(bf16[64,16,128]{2,1,0:T(8,128)(2,1)} %bitcast.3), calls=%async_computation.1 | async-start | bytes 524288 | tf_op jit(solution)/shard_map/all_to_all | solution.py:38
  40.0 18.0 %all-to-all-start.3 = ((bf16[64,16,128]{2,1,0:T(8,128)(2,1)}), bf16[64,16,128]{2,1,0:T(8,128)(2,1)S(1)}, u32[]{:S(2)}, u32[]{:S(2)}) async-start(bf16[64,16,128]{2,1,0:T(8,128)(2,1)} %bitcast.9), calls=%async_computation.3 | async-start | bytes 524288 | tf_op jit(solution)/shard_map/all_to_all | solution.py:39
  59.9 57.2 %all-to-all-start.4 = ((bf16[64,128,128]{2,1,0:T(8,128)(2,1)}), bf16[64,128,128]{2,1,0:T(8,128)(2,1)S(1)}, u32[]{:S(2)}, u32[]{:S(2)}) async-start(bf16[64,128,128]{2,1,0:T(8,128)(2,1)} %bitcast.96), calls=%async_computation.4 | async-start | bytes 4194304 | tf_op jit(solution)/shard_map/all_to_all | solution.py:41
  119.0 57.2 %all-to-all-start.2 = ((bf16[64,128,128]{2,1,0:T(8,128)(2,1)}), bf16[64,128,128]{2,1,0:T(8,128)(2,1)}, u32[]{:S(2)}, u32[]{:S(2)}) async-start(bf16[64,128,128]{2,1,0:T(8,128)(2,1)} %bitcast.95), calls=%async_computation.2 | async-start | bytes 4194304 | tf_op jit(solution)/shard_map/all_to_all | solution.py:40
  223.1 4.2 copy-start
  231.2 1.9 copy-start.1
  281.3 4.2 copy-start
  289.3 1.9 copy-start.1
  308.9 18.0 %all-to-all-start.5 = ((bf16[64,16,128]{2,1,0:T(8,128)(2,1)}), bf16[64,16,128]{2,1,0:T(8,128)(2,1)S(1)}, u32[]{:S(2)}, u32[]{:S(2)}) async-start(bf16[64,16,128]{2,1,0:T(8,128)(2,1)} %bitcast.14), calls=%async_computation.5 | async-start | bytes 524288 | tf_op jit(solution)/shard_map/all_to_all | solution.py:91
  326.9 57.2 %all-to-all-start.7 = ((bf16[64,128,128]{2,1,0:T(8,128)(2,1)}), bf16[64,128,128]{2,1,0:T(8,128)(2,1)S(1)}, u32[]{:S(2)}, u32[]{:S(2)}) async-start(bf16[64,128,128]{2,1,0:T(8,128)(2,1)} %bitcast.20), calls=%async_computation.7 | async-start | bytes 4194304 | tf_op jit(solution)/shard_map/all_to_all | solution.py:109
  384.2 57.2 %all-to-all-start.8 = ((bf16[64,128,128]{2,1,0:T(8,128)(2,1)}), bf16[64,128,128]{2,1,0:T(8,128)(2,1)}, u32[]{:S(2)}, u32[]{:S(2)}) async-start(bf16[64,128,128]{2,1,0:T(8,128)(2,1)} %bitcast.24), calls=%async_computation.8 | async-start | bytes 4194304 | tf_op jit(solution)/shard_map/all_to_all | solution.py:116
where the time goes:
time: 447 us; the launch traced here: 444 us
  waiting for transfers between devices  234 us (52%)
  matrix products  90.4 us (20%)
  starting transfers between devices  53 us (12%)
  other arithmetic  26.8 us (6%)
  local copies, waits for them, and re-layouts  20.1 us (4%)
  blocking collectives  17.7 us (4%)
    all_to_all x1, waiting for transfers between devices, local(): lax.all_to_all(by_head(value[0]), 'seq', split_axis=0, concat_axis=0, til...  51.1 us
    all_to_all x1, waiting for transfers between devices, local(): lax.all_to_all(by_head(key[0]), 'seq', split_axis=0, concat_axis=0, tiled...  50.7 us
    all_to_all x1, waiting for transfers between devices, local(): lax.all_to_all(value_acc.reshape(devices, rows, HDIM).astype(jnp.bfloat16...  47.7 us
    all_to_all x1, waiting for transfers between devices, local(): lax.all_to_all(key_acc.reshape(devices, rows, HDIM).astype(jnp.bfloat16),...  47.5 us
    dot_general x2, matrix products, step(): jnp.einsum('qk,qd->kd', weights, do_block, preferred_element_type=jnp.flo...  23.2 us
    dot_general x2, matrix products, step(): jnp.einsum('qd,kd->qk', q_block, keys, preferred_element_type=jnp.float32)  17.7 us
    all_to_all x1, blocking collectives, local(): lax.all_to_all(qgrad_blocks.reshape(devices, share, HDIM), 'seq', split_a...  17.7 us
    dot_general x2, matrix products, step(): jnp.dot(weights, values, preferred_element_type=jnp.float32)  17.5 us
  transfers between devices with their start and end apart: 8, of which 8 were waited for; matrix products, arithmetic and copies ran while one was open for 4% of the time, Pallas kernels for 0%

commit v1 on v0

v1 whole, which is shorter than its diff:
```python
import functools

import jax
import jax.numpy as jnp
from jax import lax
from jax.experimental import pallas as pl
from jax.experimental.pallas import tpu as pltpu
from jax.sharding import Mesh, PartitionSpec as P

HEADS = 8
HDIM = 128
ROWS = 128
TILE = 16
XS, ZS, CS = 4, 8, 2
CHUNKS = XS * ZS * CS
QB = 512
KB = 512
STEPS = CHUNKS * ROWS // KB
INV_ROOT = HDIM ** -0.5
LOG2E = 1.4426950408889634
NEG = -1e30

NT = (((1,), (1,)), ((), ()))
TN = (((0,), (0,)), ((), ()))


def dot(a, b, dims=(((1,), (0,)), ((), ()))):
    return lax.dot_general(a, b, dims, preferred_element_type=jnp.float32)


def lanes(fn, tile):
    return jnp.concatenate(
        [fn(i, tile[:, i * 128 : (i + 1) * 128]) for i in range(tile.shape[1] // 128)], axis=1
    )


PIECES = ((0, 0, 8), (3, 0, 8), (1, 0, 8), (2, 0, 4), (2, 4, 4))


def attention_kernel(at_ref, *refs):
    pieces, (qd_a, qd_b), refs = refs[:10], refs[10:12], refs[12:]
    (ad_a, ad_b), grads, refs = refs[:2], refs[2:10], refs[10:]
    kvs_ref, qd_ref, ad_ref, s_scr, e_scr, dk_scr, dv_scr, acc_scr, dq_scr, qs_scr, row_scr, sems, qsems = refs
    x, own_core = at_ref[0], at_ref[1]

    def first_chunk(distance, other):
        core = 1 - own_core if other else own_core
        return (lax.rem(x + distance, XS) * CS + core) * ZS

    copies = [
        pltpu.make_async_copy(qd_a, qd_ref.at[0:4], qsems.at[0]),
        pltpu.make_async_copy(qd_b, qd_ref.at[4:8], qsems.at[1]),
    ]
    for i, (distance, start, count) in enumerate(PIECES):
        for other in (0, 1):
            n = 2 * i + other
            copies.append(
                pltpu.make_async_copy(
                    pieces[n], kvs_ref.at[pl.ds(first_chunk(distance, other) + start, count)], sems.at[n]
                )
            )
    for copy in copies:
        copy.start()
    dk_scr[...] = jnp.zeros_like(dk_scr)
    dv_scr[...] = jnp.zeros_like(dv_scr)
    for copy in copies:
        copy.wait()

    key_scales = kvs_ref[:, 256:272, :].astype(jnp.float32)[:, 0, :]
    chunk = lax.broadcasted_iota(jnp.int32, key_scales.shape, 0)
    lane = lax.broadcasted_iota(jnp.int32, key_scales.shape, 1)
    core = (chunk // ZS) % CS
    parity = chunk % 2
    is_first = (core == 0) & (parity == 0) & (lane == 0)
    is_last = (core == 1) & (parity == 1) & (lane == ROWS - 1)

    def parts(step):
        base = (step // 4) * 16 + 2 * (step % 4)
        return (base, base + 8)

    def rows_of(base, start):
        return kvs_ref[pl.ds(base, 2), start : start + ROWS, :].reshape(2 * ROWS, HDIM)

    def both(step, start):
        a, b = parts(step)
        return jnp.concatenate([rows_of(a, start), rows_of(b, start)], axis=0)

    def one_block(block, _):
        first = block * (QB // ROWS)
        q = qd_ref[pl.ds(first, QB // ROWS), 0:128, :].reshape(QB, HDIM)
        do = qd_ref[pl.ds(first, QB // ROWS), 128:256, :].reshape(QB, HDIM)
        own = qd_ref[pl.ds(first, QB // ROWS), 256:272, :].astype(jnp.float32)[:, 0, :]
        for i in range(QB // ROWS):
            qs_scr[i * ROWS : (i + 1) * ROWS, :] = jnp.broadcast_to(own[i : i + 1, :], (ROWS, ROWS)).T
        low, high = jnp.min(own), jnp.max(own)
        n_steps = jnp.sum(jnp.where(is_first & (key_scales <= high), 1.0, 0.0)).astype(jnp.int32)
        n_full = jnp.sum(jnp.where(is_last & (key_scales <= low), 1.0, 0.0)).astype(jnp.int32)

        def scores(masked, step, _):
            s = dot(q, both(step, 0), NT)
            if masked:
                a, b = parts(step)
                ks = [
                    kvs_ref[c, 256:272, :].astype(jnp.float32)[0:1, :]
                    for c in (a, a + 1, b, b + 1)
                ]
                qs = qs_scr[...]
                s = lanes(lambda i, t: jnp.where(ks[i] <= qs, t, NEG), s)
            s_scr[step] = s
            top = row_scr[...]
            for i in range(KB // 128):
                top = jnp.maximum(top, s[:, i * 128 : (i + 1) * 128])
            row_scr[...] = top
            return 0

        row_scr[...] = jnp.full_like(row_scr, NEG)
        lax.fori_loop(0, n_full, functools.partial(scores, False), 0)
        lax.fori_loop(n_full, n_steps, functools.partial(scores, True), 0)
        top = jnp.max(row_scr[...], axis=1, keepdims=True) * (INV_ROOT * LOG2E)
        row_scr[...] = jnp.broadcast_to(top, row_scr.shape)
        acc_scr[...] = jnp.zeros_like(acc_scr)
        ones = jnp.ones((KB, HDIM), jnp.bfloat16)

        def forward(step, _):
            top = row_scr[...]
            e = lanes(lambda i, t: jnp.exp2(t * (INV_ROOT * LOG2E) - top).astype(jnp.bfloat16), s_scr[step])
            e_scr[step] = e
            acc_scr[...] += dot(e, jnp.concatenate([both(step, 128), ones], axis=1))
            return 0

        lax.fori_loop(0, n_steps, forward, 0)
        inv = 1.0 / acc_scr[:, 128:256]
        attn = acc_scr[:, 0:128] * inv
        for i in range(QB // ROWS):
            ad_ref[first + i, 0:128, :] = attn[i * ROWS : (i + 1) * ROWS, :].astype(jnp.bfloat16)
        do_n = (do.astype(jnp.float32) * inv).astype(jnp.bfloat16)
        delta = jnp.sum(do_n.astype(jnp.float32) * attn, axis=1, keepdims=True)
        row_scr[...] = jnp.broadcast_to(delta, row_scr.shape)
        dq_scr[...] = jnp.zeros_like(dq_scr)

        def backward(step, _):
            delta = row_scr[...]
            e = e_scr[step]
            k = both(step, 0)
            dp = dot(do_n, both(step, 128), NT)
            ds = lanes(
                lambda i, t: (e[:, i * 128 : (i + 1) * 128].astype(jnp.float32) * (t - delta)).astype(jnp.bfloat16),
                dp,
            )
            dq_scr[...] += dot(ds, k)
            dk = dot(ds, q, TN).reshape(4, ROWS, HDIM)
            dv = dot(e, do_n, TN).reshape(4, ROWS, HDIM)
            a, b = parts(step)
            dk_scr[pl.ds(a, 2)] += dk[0:2]
            dk_scr[pl.ds(b, 2)] += dk[2:4]
            dv_scr[pl.ds(a, 2)] += dv[0:2]
            dv_scr[pl.ds(b, 2)] += dv[2:4]
            return 0

        lax.fori_loop(0, n_steps, backward, 0)
        for i in range(QB // ROWS):
            ad_ref[first + i, 128:256, :] = (dq_scr[i * ROWS : (i + 1) * ROWS, :] * INV_ROOT).astype(jnp.bfloat16)
        return 0

    lax.fori_loop(0, ZS * ROWS // QB, one_block, 0)

    ad_a[...] = ad_ref[0:4]
    ad_b[...] = ad_ref[4:8]
    for distance in range(XS):
        for other in (0, 1):
            out = grads[2 * distance + other]
            base = first_chunk(distance, other)
            out[:, 0:128, :] = (dk_scr[pl.ds(base, ZS)] * INV_ROOT).astype(jnp.bfloat16)
            out[:, 128:256, :] = dv_scr[pl.ds(base, ZS)].astype(jnp.bfloat16)


def attention(at, pieces, qds):
    vmem = pl.BlockSpec(memory_space=pltpu.VMEM)
    anywhere = pl.BlockSpec(memory_space=pl.ANY)
    half = jax.ShapeDtypeStruct((ZS // 2, 2 * ROWS, HDIM), jnp.bfloat16)
    whole = jax.ShapeDtypeStruct((ZS, 2 * ROWS, HDIM), jnp.bfloat16)
    outs = (half,) * 2 + (whole,) * 8
    return pl.pallas_call(
        attention_kernel,
        out_shape=outs,
        in_specs=[pl.BlockSpec(memory_space=pltpu.SMEM)] + [anywhere] * 12,
        out_specs=(vmem,) * len(outs),
        scratch_shapes=[
            pltpu.VMEM((CHUNKS, 2 * ROWS + TILE, HDIM), jnp.bfloat16),
            pltpu.VMEM((ZS, 2 * ROWS + TILE, HDIM), jnp.bfloat16),
            pltpu.VMEM((ZS, 2 * ROWS, HDIM), jnp.bfloat16),
            pltpu.VMEM((STEPS, QB, KB), jnp.float32),
            pltpu.VMEM((STEPS, QB, KB), jnp.bfloat16),
            pltpu.VMEM((CHUNKS, ROWS, HDIM), jnp.float32),
            pltpu.VMEM((CHUNKS, ROWS, HDIM), jnp.float32),
            pltpu.VMEM((QB, 2 * HDIM), jnp.float32),
            pltpu.VMEM((QB, HDIM), jnp.float32),
            pltpu.VMEM((QB, HDIM), jnp.float32),
            pltpu.VMEM((QB, HDIM), jnp.float32),
            pltpu.SemaphoreType.DMA((10,)),
            pltpu.SemaphoreType.DMA((2,)),
        ],
        compiler_params=pltpu.CompilerParams(vmem_limit_bytes=56 * 1024 * 1024),
        cost_estimate=pl.CostEstimate(flops=8 * 10**9, bytes_accessed=10 * 2**20, transcendentals=5 * 10**6),
    )(at, *pieces, *qds)


def pack_kernel(a_ref, b_ref, scale_ref, out_ref):
    scales = jnp.broadcast_to(scale_ref[...].astype(jnp.float32), (TILE, ROWS)).astype(jnp.bfloat16)
    for h in range(HEADS):
        out_ref[h, 0:128, :] = a_ref[0, :, h * HDIM : (h + 1) * HDIM]
        out_ref[h, 128:256, :] = b_ref[0, :, h * HDIM : (h + 1) * HDIM]
        out_ref[h, 256:272, :] = scales


def pack(a, b, scale_ids):
    vmem = pl.BlockSpec(memory_space=pltpu.VMEM)
    return pl.pallas_call(
        pack_kernel,
        out_shape=jax.ShapeDtypeStruct((HEADS, 2 * ROWS + TILE, HDIM), jnp.bfloat16),
        in_specs=[vmem] * 3,
        out_specs=vmem,
    )(a, b, scale_ids)


def unpack_kernel(in_ref, a_ref, b_ref):
    for h in range(HEADS):
        a_ref[0, :, h * HDIM : (h + 1) * HDIM] = in_ref[h, 0:128, :]
        b_ref[0, :, h * HDIM : (h + 1) * HDIM] = in_ref[h, 128:256, :]


def unpack(arr):
    vmem = pl.BlockSpec(memory_space=pltpu.VMEM)
    rows = jax.ShapeDtypeStruct((1, ROWS, HEADS * HDIM), jnp.bfloat16)
    return pl.pallas_call(
        unpack_kernel, out_shape=(rows, rows), in_specs=[vmem], out_specs=(vmem, vmem)
    )(arr)


def add(*arrs):
    total = arrs[0].astype(jnp.float32)
    for arr in arrs[1:]:
        total = total + arr.astype(jnp.float32)
    return total.astype(jnp.bfloat16)


def local(query, key, value, grad_attn, scale_ids):
    def over_heads(arr):
        return lax.all_to_all(arr, "z", split_axis=0, concat_axis=0, tiled=True)

    def right(arr):
        return lax.ppermute(arr, "x", [(i, (i + 1) % XS) for i in range(XS)])

    def left(arr):
        return lax.ppermute(arr, "x", [(i, (i + XS - 1) % XS) for i in range(XS)])

    def mirror(arr):
        return lax.ppermute(arr, "x", [(i, XS - 1 - i) for i in range(XS)])

    def twin(arr):
        return lax.ppermute(arr, "core", [(0, 1), (1, 0)])

    half = ZS // 2
    at = jnp.stack([lax.axis_index("x"), lax.axis_index("core")]).astype(jnp.int32)

    kvs = over_heads(pack(key, value, scale_ids))
    from_left, from_right = right(kvs), left(kvs)
    qd = over_heads(pack(query, grad_attn, scale_ids))
    opposite_a, opposite_b = right(from_left[:half]), left(from_right[half:])
    qd_b = mirror(qd[half:])
    pieces = []
    for piece in (kvs, from_left, from_right, opposite_a, opposite_b):
        pieces += [piece, twin(piece)]

    ad_a, ad_b, *grads = attention(at, pieces, (qd[:half], qd_b))

    sums = [None] * XS
    for distance in (2, 1, 3, 0):
        sums[distance] = add(grads[2 * distance], twin(grads[2 * distance + 1]))
    from_a, from_b = right(sums[2][:half]), left(sums[2][half:])
    to_right = jnp.concatenate([add(sums[1][:half], from_a), sums[1][half:]], axis=0)
    to_left = jnp.concatenate([sums[3][:half], add(sums[3][half:], from_b)], axis=0)
    ad_back = over_heads(jnp.concatenate([ad_a, mirror(ad_b)], axis=0))
    dkv_back = over_heads(add(sums[0], right(to_right), left(to_left)))
    return unpack(ad_back) + unpack(dkv_back)


def solution(mesh):
    fine = Mesh(mesh.devices.reshape(mesh.devices.shape[0], XS, ZS, CS), ("batch", "x", "z", "core"))
    seq = ("x", "z", "core")
    rows = P("batch", seq, None)
    return jax.shard_map(
        local,
        mesh=fine,
        in_specs=(rows, rows, rows, rows, P("batch", seq)),
        out_specs=(rows, rows, rows, rows),
        check_vma=False,
    )
```

time: 447 us -> 182 us (0.41)
  waiting for transfers between devices: 234 us -> 79.4 us
  matrix products: 90.4 us -> 0 us
  Pallas kernels: 0 us -> 42.7 us
  other arithmetic: 26.8 us -> 4.13 us
  blocking collectives: 17.7 us -> 0 us
  local copies, waits for them, and re-layouts: 20.1 us -> 4.45 us
    all_to_all x8 -> x4, waiting for transfers between devices: 234 us -> 45.2 us  [over_heads(): return lax.all_to_all(arr, 'z', split_axis=0, concat_axis=0, tiled=True)]
    dot_general x12 -> x0, matrix products: 90.4 us -> none  [the longest x2 23.2 us: step(): jnp.einsum('qk,qd->kd', weights, do_block, preferred_element_type=jnp.flo...]
    pallas_call x0 -> x5, Pallas kernels: none -> 42.7 us  [the longest x1 34.9 us: attention(): pl.pallas_call(attention_kernel, out_shape=outs, in_specs=[pl.BlockSpec(m...]
    ppermute x0 -> x19, waiting for transfers between devices: none -> 34.3 us  [the longest x4 16.9 us: right(): return lax.ppermute(arr, 'x', [(i, (i + 1) % XS) for i in range(XS)])]
    all_to_all x8 -> x4, starting transfers between devices: 53 us -> 22.2 us  [over_heads(): return lax.all_to_all(arr, 'z', split_axis=0, concat_axis=0, tiled=True)]
    ppermute x0 -> x19, starting transfers between devices: none -> 26.7 us  [the longest x2 14.2 us: mirror(): return lax.ppermute(arr, 'x', [(i, XS - 1 - i) for i in range(XS)])]
    reduce_sum x4 -> x0, other arithmetic: 18.5 us -> none  [the longest x2 16.2 us: step(): lse = top + jnp.log(jnp.sum(jnp.exp(scores - top), axis=1, keepdims=True))]
    all_to_all x1 -> x0, blocking collectives: 17.7 us -> none  [local(): lax.all_to_all(qgrad_blocks.reshape(devices, share, HDIM), 'seq', split_a...]
  transfers between devices with their start and end apart: 8 -> 23, of which waited for: 8 -> 11; matrix products, arithmetic and copies ran while one was open for 4% -> 3% of each run, Pallas kernels for 0% -> 2%
where the time goes in v1:
time: 182 us; the launch traced here: 180 us
  waiting for transfers between devices  79.4 us (44%)
  starting transfers between devices  48.8 us (27%)
  Pallas kernels  42.7 us (23%)
  local copies, waits for them, and re-layouts  4.45 us (2%)
  other arithmetic  4.13 us (2%)
    all_to_all x4, waiting for transfers between devices, over_heads(): return lax.all_to_all(arr, 'z', split_axis=0, concat_axis=0, tiled=True)  45.2 us
    pallas_call x1, Pallas kernels, attention(): pl.pallas_call(attention_kernel, out_shape=outs, in_specs=[pl.BlockSpec(m...  34.9 us
    all_to_all x4, starting transfers between devices, over_heads(): return lax.all_to_all(arr, 'z', split_axis=0, concat_axis=0, tiled=True)  22.2 us
    ppermute x4, waiting for transfers between devices, right(): return lax.ppermute(arr, 'x', [(i, (i + 1) % XS) for i in range(XS)])  16.9 us
    ppermute x2, starting transfers between devices, mirror(): return lax.ppermute(arr, 'x', [(i, XS - 1 - i) for i in range(XS)])  14.2 us
    ppermute x2, waiting for transfers between devices, mirror(): return lax.ppermute(arr, 'x', [(i, XS - 1 - i) for i in range(XS)])  12 us
    ppermute x4, starting transfers between devices, left(): return lax.ppermute(arr, 'x', [(i, (i + XS - 1) % XS) for i in range(XS)])  9.9 us
    ppermute x4, waiting for transfers between devices, left(): return lax.ppermute(arr, 'x', [(i, (i + XS - 1) % XS) for i in range(XS)])  4.11 us
  transfers between devices with their start and end apart: 23, of which 11 were waited for; matrix products, arithmetic and copies ran while one was open for 3% of the time, Pallas kernels for 2%

profile of v1, /device:TPU:16, one launch (start us, length us, event | category | flops | bytes accessed | tf_op | source)
XLA Modules:
  0.0 180.4 jit_solution(876640648237522099)
XLA Ops:
  0.6 1.9 %shard_map.84 = bf16[8,272,128]{2,1,0:T(8,128)(2,1)} custom-call(bf16[1,128,1024]{2,1,0:T(8,128)(2,1)} %a_ref.2, bf16[1,128,1024]{2,1,0:T(8,128)(2,1)} %b_ref.2, s32[1,128]{1,0:T(1,128)} %scale_ref.3), custom_call_target="tpu_custom_call" | custom-call | tf_op jit(solution)/shard_map/pallas_call | solution.py:218
  2.6 8.5 %all-to-all-start = ((bf16[8,272,128]{2,1,0:T(8,128)(2,1)}), bf16[8,272,128]{2,1,0:T(8,128)(2,1)S(1)}, u32[]{:S(2)}, u32[]{:S(2)}) async-start(bf16[8,272,128]{2,1,0:T(8,128)(2,1)} %shard_map.84), calls=%async_computation | async-start | bytes 1114112 | tf_op jit(solution)/shard_map/all_to_all | solution.py:249
  11.0 2.0 %shard_map.85 = bf16[8,272,128]{2,1,0:T(8,128)(2,1)} custom-call(bf16[1,128,1024]{2,1,0:T(8,128)(2,1)} %a_ref.3, bf16[1,128,1024]{2,1,0:T(8,128)(2,1)} %b_ref.3, s32[1,128]{1,0:T(1,128)} %scale_ref.3), custom_call_target="tpu_custom_call" | custom-call | tf_op jit(solution)/shard_map/pallas_call | solution.py:218
  13.0 16.2 %all-to-all-done.refs_0_ = bf16[8,272,128]{2,1,0:T(8,128)(2,1)S(1)} async-done(((bf16[8,272,128]{2,1,0:T(8,128)(2,1)}), bf16[8,272,128]{2,1,0:T(8,128)(2,1)S(1)}, u32[]{:S(2)}, u32[]{:S(2)}) %all-to-all-start) | async-done | bytes 557088 | tf_op jit(solution)/shard_map/all_to_all | solution.py:249
  29.2 3.5 %all-to-all-start.1 = ((bf16[8,272,128]{2,1,0:T(8,128)(2,1)}), bf16[8,272,128]{2,1,0:T(8,128)(2,1)S(1)}, u32[]{:S(2)}, u32[]{:S(2)}) async-start(bf16[8,272,128]{2,1,0:T(8,128)(2,1)} %shard_map.85), calls=%async_computation.1 | async-start | bytes 1114112 | tf_op jit(solution)/shard_map/all_to_all | solution.py:249
  32.8 2.8 %collective-permute-start.3 = (bf16[8,272,128]{2,1,0:T(8,128)(2,1)S(1)}, bf16[8,272,128]{2,1,0:T(8,128)(2,1)S(1)}, u32[]{:S(2)}, u32[]{:S(2)}) collective-permute-start(bf16[8,272,128]{2,1,0:T(8,128)(2,1)S(1)} %all-to-all-done.refs_0_), channel_id=1, source_target_pairs={{0,48},{16,0},{32,16},{48,32},{1,49},{17,1},{33,17},{49,33},{2,50}... | collective-permute-start | bytes 1671176 | tf_op jit(solution)/shard_map/ppermute | solution.py:255
  35.6 15.8 %all-to-all-done.1 = bf16[8,272,128]{2,1,0:T(8,128)(2,1)S(1)} async-done(((bf16[8,272,128]{2,1,0:T(8,128)(2,1)}), bf16[8,272,128]{2,1,0:T(8,128)(2,1)S(1)}, u32[]{:S(2)}, u32[]{:S(2)}) %all-to-all-start.1) | async-done | bytes 557088 | tf_op jit(solution)/shard_map/all_to_all | solution.py:249
  51.4 0.8 fusion
  52.2 2.8 %collective-permute-start.9 = (bf16[4,272,128]{2,1,0:T(8,128)(2,1)S(1)}, bf16[4,272,128]{2,1,0:T(8,128)(2,1)S(1)}, u32[]{:S(2)}, u32[]{:S(2)}) collective-permute-start(bf16[4,272,128]{2,1,0:T(8,128)(2,1)S(1)} %get-tuple-element.32), channel_id=1, source_target_pairs={{0,48},{16,32},{32,16},{48,0},{1,49},{17,33},{33,17},{49,1},{2,50}... | collective-permute-start | bytes 835592 | tf_op jit(solution)/shard_map/ppermute | solution.py:258
  55.5 1.6 collective-permute-start.5
  57.2 5.7 %collective-permute-done.9.refs_11_ = bf16[4,272,128]{2,1,0:T(8,128)(2,1)S(1)} collective-permute-done((bf16[4,272,128]{2,1,0:T(8,128)(2,1)S(1)}, bf16[4,272,128]{2,1,0:T(8,128)(2,1)S(1)}, u32[]{:S(2)}, u32[]{:S(2)}) %collective-permute-start.9) | collective-permute-done | bytes 278560 | tf_op jit(solution)/shard_map/ppermute | solution.py:258
  62.9 4.1 %collective-permute-done.7.refs_8_ = bf16[4,272,128]{2,1,0:T(8,128)(2,1)} collective-permute-done((bf16[4,272,128]{2,1,0:T(8,128)(2,1)S(1)}, bf16[4,272,128]{2,1,0:T(8,128)(2,1)}, u32[]{:S(2)}, u32[]{:S(2)}) %collective-permute-start.7) | collective-permute-done | bytes 278560 | tf_op jit(solution)/shard_map/ppermute | solution.py:255
  67.0 1.0 collective-permute-done.5.refs_6_
  68.9 1.0 collective-permute-done.6.refs_7_
  70.0 0.8 copy-done.10
  70.9 34.9 %shard_map.86 = (bf16[4,256,128]{2,1,0:T(8,128)(2,1)}, bf16[4,256,128]{2,1,0:T(8,128)(2,1)}, bf16[8,256,128]{2,1,0:T(8,128)(2,1)}, bf16[8,256,128]{2,1,0:T(8,128...) custom-call(s32[2]{0:T(128)} %pad_add_fusion.at_ref, ...), custom_call_target="tpu_custom_call" | custom-call | flops 8000000000 | bytes 10485760 | tf_op jit(solution)/shard_map/pallas_call | solution.py:183
  106.0 11.5 %collective-permute-start.10 = (bf16[4,256,128]{2,1,0:T(8,128)(2,1)}, bf16[4,256,128]{2,1,0:T(8,128)(2,1)S(1)}, u32[]{:S(2)}, u32[]{:S(2)}) collective-permute-start(bf16[4,256,128]{2,1,0:T(8,128)(2,1)} %get-tuple-element.19), channel_id=1, source_target_pairs={{0,48},{16,32},{32,16},{48,0},{1,49},{17,33},{33,17},{49,1},{2,50}... | collective-permute-start | bytes 786440 | tf_op jit(solution)/shard_map/ppermute | solution.py:258
  118.0 6.3 %collective-permute-done.10 = bf16[4,256,128]{2,1,0:T(8,128)(2,1)S(1)} collective-permute-done((bf16[4,256,128]{2,1,0:T(8,128)(2,1)}, bf16[4,256,128]{2,1,0:T(8,128)(2,1)S(1)}, u32[]{:S(2)}, u32[]{:S(2)}) %collective-permute-start.10) | collective-permute-done | bytes 262176 | tf_op jit(solution)/shard_map/ppermute | solution.py:258
  124.3 1.8 pad_maximum_fusion
  126.1 3.6 %all-to-all-start.2 = ((bf16[8,256,128]{2,1,0:T(8,128)(2,1)}), bf16[8,256,128]{2,1,0:T(8,128)(2,1)S(1)}, u32[]{:S(2)}, u32[]{:S(2)}) async-start(bf16[8,256,128]{2,1,0:T(8,128)(2,1)} %pad_maximum_fusion), calls=%async_computation.2 | async-start | bytes 1048576 | tf_op jit(solution)/shard_map/all_to_all | solution.py:249
  129.9 1.0 copy-done.5
  131.2 3.2 %collective-permute-start.17 = (bf16[4,256,128]{2,1,0:T(8,128)(2,1)S(1)}, bf16[4,256,128]{2,1,0:T(8,128)(2,1)S(1)}, u32[]{:S(2)}, u32[]{:S(2)}) collective-permute-start(bf16[4,256,128]{2,1,0:T(8,128)(2,1)S(1)} %get-tuple-element.35), channel_id=1, source_target_pairs={{0,48},{16,0},{32,16},{48,32},{1,49},{17,1},{33,17},{49,33},{2,50}... | collective-permute-start | bytes 786440 | tf_op jit(solution)/shard_map/ppermute | solution.py:255
  134.6 5.6 %collective-permute-done.14 = bf16[4,256,128]{2,1,0:T(8,128)(2,1)S(1)} collective-permute-done((bf16[4,256,128]{2,1,0:T(8,128)(2,1)S(1)}, bf16[4,256,128]{2,1,0:T(8,128)(2,1)S(1)}, u32[]{:S(2)}, u32[]{:S(2)}) %collective-permute-start.14) | collective-permute-done | bytes 262176 | tf_op jit(solution)/shard_map/ppermute | solution.py:252
  140.6 3.3 %collective-permute-start.18 = (bf16[8,256,128]{2,1,0:T(8,128)(2,1)S(1)}, bf16[8,256,128]{2,1,0:T(8,128)(2,1)S(1)}, u32[]{:S(2)}, u32[]{:S(2)}) collective-permute-start(bf16[8,256,128]{2,1,0:T(8,128)(2,1)S(1)} %pad_maximum_fusion.2), channel_id=1, source_target_pairs={{0,48},{16,0},{32,16},{48,32},{1,49},{17,1},{33,17},{49,33},{2,50}... | collective-permute-start | bytes 1572872 | tf_op jit(solution)/shard_map/ppermute | solution.py:255
  143.9 10.3 %collective-permute-done.15 = bf16[8,256,128]{2,1,0:T(8,128)(2,1)S(1)} collective-permute-done((bf16[8,256,128]{2,1,0:T(8,128)(2,1)S(1)}, bf16[8,256,128]{2,1,0:T(8,128)(2,1)S(1)}, u32[]{:S(2)}, u32[]{:S(2)}) %collective-permute-start.15) | collective-permute-done | bytes 524320 | tf_op jit(solution)/shard_map/ppermute | solution.py:252
  154.1 1.1 add_convert_fusion
  155.2 0.8 copy-done
  156.0 6.5 %all-to-all-start.3 = ((bf16[8,256,128]{2,1,0:T(8,128)(2,1)}), bf16[8,256,128]{2,1,0:T(8,128)(2,1)S(1)}, u32[]{:S(2)}, u32[]{:S(2)}) async-start(bf16[8,256,128]{2,1,0:T(8,128)(2,1)} %add_convert_fusion), calls=%async_computation.3 | async-start | bytes 1048576 | tf_op jit(solution)/shard_map/all_to_all | solution.py:249
  162.5 2.0 %shard_map.87 = (bf16[1,128,1024]{2,1,0:T(8,128)(2,1)}, bf16[1,128,1024]{2,1,0:T(8,128)(2,1)}) custom-call(bf16[8,256,128]{2,1,0:T(8,128)(2,1)} %copy-done), custom_call_target="tpu_custom_call" | custom-call | tf_op jit(solution)/shard_map/pallas_call | solution.py:235
  164.5 13.1 %all-to-all-done.3.in_ref = bf16[8,256,128]{2,1,0:T(8,128)(2,1)S(1)} async-done(((bf16[8,256,128]{2,1,0:T(8,128)(2,1)}), bf16[8,256,128]{2,1,0:T(8,128)(2,1)S(1)}, u32[]{:S(2)}, u32[]{:S(2)}) %all-to-all-start.3) | async-done | bytes 524320 | tf_op jit(solution)/shard_map/all_to_all | solution.py:249
  177.7 0.8 copy-done.1
  178.5 2.0 %shard_map.88 = (bf16[1,128,1024]{2,1,0:T(8,128)(2,1)}, bf16[1,128,1024]{2,1,0:T(8,128)(2,1)}) custom-call(bf16[8,256,128]{2,1,0:T(8,128)(2,1)} %copy-done.1), custom_call_target="tpu_custom_call" | custom-call | tf_op jit(solution)/shard_map/pallas_call | solution.py:235
  (61 shorter events, 3.4 us)
Async XLA Ops:
  2.6 26.7 %all-to-all-start = ((bf16[8,272,128]{2,1,0:T(8,128)(2,1)}), bf16[8,272,128]{2,1,0:T(8,128)(2,1)S(1)}, u32[]{:S(2)}, u32[]{:S(2)}) async-start(bf16[8,272,128]{2,1,0:T(8,128)(2,1)} %shard_map.84), calls=%async_computation | async-start | bytes 1114112 | tf_op jit(solution)/shard_map/all_to_all | solution.py:249
  29.2 25.7 %copy-start.2 = (bf16[8,272,128]{2,1,0:T(8,128)(2,1)}, bf16[8,272,128]{2,1,0:T(8,128)(2,1)S(1)}, u32[]{:S(2)}) copy-start(bf16[8,272,128]{2,1,0:T(8,128)(2,1)S(1)} %all-to-all-done.refs_0_) | copy-start | bytes 1671172
  29.2 22.2 %all-to-all-start.1 = ((bf16[8,272,128]{2,1,0:T(8,128)(2,1)}), bf16[8,272,128]{2,1,0:T(8,128)(2,1)S(1)}, u32[]{:S(2)}, u32[]{:S(2)}) async-start(bf16[8,272,128]{2,1,0:T(8,128)(2,1)} %shard_map.85), calls=%async_computation.1 | async-start | bytes 1114112 | tf_op jit(solution)/shard_map/all_to_all | solution.py:249
  32.8 22.1 %collective-permute-start.3 = (bf16[8,272,128]{2,1,0:T(8,128)(2,1)S(1)}, bf16[8,272,128]{2,1,0:T(8,128)(2,1)S(1)}, u32[]{:S(2)}, u32[]{:S(2)}) collective-permute-start(bf16[8,272,128]{2,1,0:T(8,128)(2,1)S(1)} %all-to-all-done.refs_0_), channel_id=1, source_target_pairs={{0,48},{16,0},{32,16},{48,32},{1,49},{17,1},{33,17},{49,33},{2,50}... | collective-permute-start | bytes 1671176 | tf_op jit(solution)/shard_map/ppermute | solution.py:255
  35.6 19.9 %collective-permute-start.1 = (bf16[8,272,128]{2,1,0:T(8,128)(2,1)S(1)}, bf16[8,272,128]{2,1,0:T(8,128)(2,1)S(1)}, u32[]{:S(2)}, u32[]{:S(2)}) collective-permute-start(bf16[8,272,128]{2,1,0:T(8,128)(2,1)S(1)} %all-to-all-done.refs_0_), channel_id=1, source_target_pairs={{0,16},{16,32},{32,48},{48,0},{1,17},{17,33},{33,49},{49,1},{2,18}... | collective-permute-start | bytes 1671176 | tf_op jit(solution)/shard_map/ppermute | solution.py:252
  52.2 10.7 %collective-permute-start.9 = (bf16[4,272,128]{2,1,0:T(8,128)(2,1)S(1)}, bf16[4,272,128]{2,1,0:T(8,128)(2,1)S(1)}, u32[]{:S(2)}, u32[]{:S(2)}) collective-permute-start(bf16[4,272,128]{2,1,0:T(8,128)(2,1)S(1)} %get-tuple-element.32), channel_id=1, source_target_pairs={{0,48},{16,32},{32,16},{48,0},{1,49},{17,33},{33,17},{49,1},{2,50}... | collective-permute-start | bytes 835592 | tf_op jit(solution)/shard_map/ppermute | solution.py:258
  54.9 13.7 %collective-permute-start = (bf16[8,272,128]{2,1,0:T(8,128)(2,1)S(1)}, bf16[8,272,128]{2,1,0:T(8,128)(2,1)S(1)}, u32[]{:S(2)}, u32[]{:S(2)}) collective-permute-start(bf16[8,272,128]{2,1,0:T(8,128)(2,1)S(1)} %all-to-all-done.refs_0_), channel_id=1, source_target_pairs={{0,1},{1,0},{2,3},{3,2},{4,5},{5,4},{6,7},{7,6},{8,9},{9,8},{10,11... | collective-permute-start | bytes 1671176 | tf_op jit(solution)/shard_map/ppermute | solution.py:261
  54.9 2.2 %copy-start.7 = (bf16[8,272,128]{2,1,0:T(8,128)(2,1)}, bf16[8,272,128]{2,1,0:T(8,128)(2,1)S(1)}, u32[]{:S(2)}) copy-start(bf16[8,272,128]{2,1,0:T(8,128)(2,1)S(1)} %collective-permute-done.3.refs_4_) | copy-start | bytes 1671172
  55.0 12.0 %collective-permute-start.7 = (bf16[4,272,128]{2,1,0:T(8,128)(2,1)S(1)}, bf16[4,272,128]{2,1,0:T(8,128)(2,1)}, u32[]{:S(2)}, u32[]{:S(2)}) collective-permute-start(bf16[4,272,128]{2,1,0:T(8,128)(2,1)S(1)} %slice.41), channel_id=1, source_target_pairs={{0,48},{16,0},{32,16},{48,32},{1,49},{17,1},{33,17},{49,33},{2,50}... | collective-permute-start | bytes 835592 | tf_op jit(solution)/shard_map/ppermute | solution.py:255
  55.5 14.4 %copy-start.8 = (bf16[8,272,128]{2,1,0:T(8,128)(2,1)}, bf16[8,272,128]{2,1,0:T(8,128)(2,1)S(1)}, u32[]{:S(2)}) copy-start(bf16[8,272,128]{2,1,0:T(8,128)(2,1)S(1)} %collective-permute-done.1.refs_2_) | copy-start | bytes 1671172
  55.5 12.5 %collective-permute-start.5 = (bf16[4,272,128]{2,1,0:T(8,128)(2,1)S(1)}, bf16[4,272,128]{2,1,0:T(8,128)(2,1)}, u32[]{:S(2)}, u32[]{:S(2)}) collective-permute-start(bf16[4,272,128]{2,1,0:T(8,128)(2,1)S(1)} %slice.40), channel_id=1, source_target_pairs={{0,16},{16,32},{32,48},{48,0},{1,17},{17,33},{33,49},{49,1},{2,18}... | collective-permute-start | bytes 835592 | tf_op jit(solution)/shard_map/ppermute | solution.py:252
  57.2 12.8 %collective-permute-start.4 = (bf16[8,272,128]{2,1,0:T(8,128)(2,1)S(1)}, bf16[8,272,128]{2,1,0:T(8,128)(2,1)S(1)}, u32[]{:S(2)}, u32[]{:S(2)}) collective-permute-start(bf16[8,272,128]{2,1,0:T(8,128)(2,1)S(1)} %collective-permute-done.3.refs_4_), channel_id=1, source_target_pairs={{0,1},{1,0},{2,3},{3,2},{4,5},{5,4},{6,7},{7,6},{8,9},{9,8},{10,11... | collective-permute-start | bytes 1671176 | tf_op jit(solution)/shard_map/ppermute | solution.py:261
  62.9 5.1 %copy-start.12 = (bf16[4,272,128]{2,1,0:T(8,128)(2,1)}, bf16[4,272,128]{2,1,0:T(8,128)(2,1)S(1)}, u32[]{:S(2)}) copy-start(bf16[4,272,128]{2,1,0:T(8,128)(2,1)S(1)} %collective-permute-done.9.refs_11_) | copy-start | bytes 835588
  62.9 7.1 %collective-permute-start.2 = (bf16[8,272,128]{2,1,0:T(8,128)(2,1)S(1)}, bf16[8,272,128]{2,1,0:T(8,128)(2,1)S(1)}, u32[]{:S(2)}, u32[]{:S(2)}) collective-permute-start(bf16[8,272,128]{2,1,0:T(8,128)(2,1)S(1)} %collective-permute-done.1.refs_2_), channel_id=1, source_target_pairs={{0,1},{1,0},{2,3},{3,2},{4,5},{5,4},{6,7},{7,6},{8,9},{9,8},{10,11... | collective-permute-start | bytes 1671176 | tf_op jit(solution)/shard_map/ppermute | solution.py:261
  67.0 1.9 %collective-permute-start.8 = (bf16[4,272,128]{2,1,0:T(8,128)(2,1)}, bf16[4,272,128]{2,1,0:T(8,128)(2,1)}, u32[]{:S(2)}, u32[]{:S(2)}) collective-permute-start(bf16[4,272,128]{2,1,0:T(8,128)(2,1)} %collective-permute-done.7.refs_8_), channel_id=1, source_target_pairs={{0,1},{1,0},{2,3},{3,2},{4,5},{5,4},{6,7},{7,6},{8,9},{9,8},{10,11... | collective-permute-start | bytes 835592 | tf_op jit(solution)/shard_map/ppermute | solution.py:261
  68.0 1.9 %collective-permute-start.6 = (bf16[4,272,128]{2,1,0:T(8,128)(2,1)}, bf16[4,272,128]{2,1,0:T(8,128)(2,1)}, u32[]{:S(2)}, u32[]{:S(2)}) collective-permute-start(bf16[4,272,128]{2,1,0:T(8,128)(2,1)} %collective-permute-done.5.refs_6_), channel_id=1, source_target_pairs={{0,1},{1,0},{2,3},{3,2},{4,5},{5,4},{6,7},{7,6},{8,9},{9,8},{10,11... | collective-permute-start | bytes 835592 | tf_op jit(solution)/shard_map/ppermute | solution.py:261
  68.6 1.3 copy-start.9
  105.8 23.9 %collective-permute-start.12 = (bf16[8,256,128]{2,1,0:T(8,128)(2,1)}, bf16[8,256,128]{2,1,0:T(8,128)(2,1)S(1)}, u32[]{:S(2)}, u32[]{:S(2)}) collective-permute-start(bf16[8,256,128]{2,1,0:T(8,128)(2,1)} %get-tuple-element.25), channel_id=1, source_target_pairs={{0,1},{1,0},{2,3},{3,2},{4,5},{5,4},{6,7},{7,6},{8,9},{9,8},{10,11... | collective-permute-start | bytes 1572872 | tf_op jit(solution)/shard_map/ppermute | solution.py:261
  106.0 18.2 %collective-permute-start.10 = (bf16[4,256,128]{2,1,0:T(8,128)(2,1)}, bf16[4,256,128]{2,1,0:T(8,128)(2,1)S(1)}, u32[]{:S(2)}, u32[]{:S(2)}) collective-permute-start(bf16[4,256,128]{2,1,0:T(8,128)(2,1)} %get-tuple-element.19), channel_id=1, source_target_pairs={{0,48},{16,32},{32,16},{48,0},{1,49},{17,33},{33,17},{49,1},{2,50}... | collective-permute-start | bytes 786440 | tf_op jit(solution)/shard_map/ppermute | solution.py:258
  117.5 12.4 %collective-permute-start.13 = (bf16[8,256,128]{2,1,0:T(8,128)(2,1)}, bf16[8,256,128]{2,1,0:T(8,128)(2,1)S(1)}, u32[]{:S(2)}, u32[]{:S(2)}) collective-permute-start(bf16[8,256,128]{2,1,0:T(8,128)(2,1)} %get-tuple-element.27), channel_id=1, source_target_pairs={{0,1},{1,0},{2,3},{3,2},{4,5},{5,4},{6,7},{7,6},{8,9},{9,8},{10,11... | collective-permute-start | bytes 1572872 | tf_op jit(solution)/shard_map/ppermute | solution.py:261
  117.5 26.4 %collective-permute-start.11 = (bf16[8,256,128]{2,1,0:T(8,128)(2,1)}, bf16[8,256,128]{2,1,0:T(8,128)(2,1)S(1)}, u32[]{:S(2)}, u32[]{:S(2)}) collective-permute-start(bf16[8,256,128]{2,1,0:T(8,128)(2,1)} %get-tuple-element.23), channel_id=1, source_target_pairs={{0,1},{1,0},{2,3},{3,2},{4,5},{5,4},{6,7},{7,6},{8,9},{9,8},{10,11... | collective-permute-start | bytes 1572872 | tf_op jit(solution)/shard_map/ppermute | solution.py:261
  118.0 16.4 %collective-permute-start.16 = (bf16[8,256,128]{2,1,0:T(8,128)(2,1)}, bf16[8,256,128]{2,1,0:T(8,128)(2,1)S(1)}, u32[]{:S(2)}, u32[]{:S(2)}) collective-permute-start(bf16[8,256,128]{2,1,0:T(8,128)(2,1)} %get-tuple-element.29), channel_id=1, source_target_pairs={{0,1},{1,0},{2,3},{3,2},{4,5},{5,4},{6,7},{7,6},{8,9},{9,8},{10,11... | collective-permute-start | bytes 1572872 | tf_op jit(solution)/shard_map/ppermute | solution.py:261
  126.1 3.6 %copy-start.6 = (bf16[8,256,128]{2,1,0:T(8,128)(2,1)S(1)}, bf16[8,256,128]{2,1,0:T(8,128)(2,1)}, u32[]{:S(2)}) copy-start(bf16[8,256,128]{2,1,0:T(8,128)(2,1)} %get-tuple-element.24) | copy-start | bytes 1572868
  126.1 29.1 %all-to-all-start.2 = ((bf16[8,256,128]{2,1,0:T(8,128)(2,1)}), bf16[8,256,128]{2,1,0:T(8,128)(2,1)S(1)}, u32[]{:S(2)}, u32[]{:S(2)}) async-start(bf16[8,256,128]{2,1,0:T(8,128)(2,1)} %pad_maximum_fusion), calls=%async_computation.2 | async-start | bytes 1048576 | tf_op jit(solution)/shard_map/all_to_all | solution.py:249
  129.9 1.0 copy-start.5
  131.0 3.4 %copy-start.4 = (bf16[8,256,128]{2,1,0:T(8,128)(2,1)S(1)}, bf16[8,256,128]{2,1,0:T(8,128)(2,1)}, u32[]{:S(2)}) copy-start(bf16[8,256,128]{2,1,0:T(8,128)(2,1)} %get-tuple-element.28) | copy-start | bytes 1572868
  131.1 9.1 %collective-permute-start.14 = (bf16[4,256,128]{2,1,0:T(8,128)(2,1)S(1)}, bf16[4,256,128]{2,1,0:T(8,128)(2,1)S(1)}, u32[]{:S(2)}, u32[]{:S(2)}) collective-permute-start(bf16[4,256,128]{2,1,0:T(8,128)(2,1)S(1)} %get-tuple-element.34), channel_id=1, source_target_pairs={{0,16},{16,32},{32,48},{48,0},{1,17},{17,33},{33,49},{49,1},{2,18}... | collective-permute-start | bytes 786440 | tf_op jit(solution)/shard_map/ppermute | solution.py:252
  131.2 9.2 %collective-permute-start.17 = (bf16[4,256,128]{2,1,0:T(8,128)(2,1)S(1)}, bf16[4,256,128]{2,1,0:T(8,128)(2,1)S(1)}, u32[]{:S(2)}, u32[]{:S(2)}) collective-permute-start(bf16[4,256,128]{2,1,0:T(8,128)(2,1)S(1)} %get-tuple-element.35), channel_id=1, source_target_pairs={{0,48},{16,0},{32,16},{48,32},{1,49},{17,1},{33,17},{49,33},{2,50}... | collective-permute-start | bytes 786440 | tf_op jit(solution)/shard_map/ppermute | solution.py:255
  140.3 13.8 %collective-permute-start.15 = (bf16[8,256,128]{2,1,0:T(8,128)(2,1)S(1)}, bf16[8,256,128]{2,1,0:T(8,128)(2,1)S(1)}, u32[]{:S(2)}, u32[]{:S(2)}) collective-permute-start(bf16[8,256,128]{2,1,0:T(8,128)(2,1)S(1)} %pad_maximum_fusion.1), channel_id=1, source_target_pairs={{0,16},{16,32},{32,48},{48,0},{1,17},{17,33},{33,49},{49,1},{2,18}... | collective-permute-start | bytes 1572872 | tf_op jit(solution)/shard_map/ppermute | solution.py:252
  140.5 13.6 %copy-start.3 = (bf16[8,256,128]{2,1,0:T(8,128)(2,1)S(1)}, bf16[8,256,128]{2,1,0:T(8,128)(2,1)}, u32[]{:S(2)}) copy-start(bf16[8,256,128]{2,1,0:T(8,128)(2,1)} %get-tuple-element.22) | copy-start | bytes 1572868
  140.6 13.5 %collective-permute-start.18 = (bf16[8,256,128]{2,1,0:T(8,128)(2,1)S(1)}, bf16[8,256,128]{2,1,0:T(8,128)(2,1)S(1)}, u32[]{:S(2)}, u32[]{:S(2)}) collective-permute-start(bf16[8,256,128]{2,1,0:T(8,128)(2,1)S(1)} %pad_maximum_fusion.2), channel_id=1, source_target_pairs={{0,48},{16,0},{32,16},{48,32},{1,49},{17,1},{33,17},{49,33},{2,50}... | collective-permute-start | bytes 1572872 | tf_op jit(solution)/shard_map/ppermute | solution.py:255
  156.0 21.7 %all-to-all-start.3 = ((bf16[8,256,128]{2,1,0:T(8,128)(2,1)}), bf16[8,256,128]{2,1,0:T(8,128)(2,1)S(1)}, u32[]{:S(2)}, u32[]{:S(2)}) async-start(bf16[8,256,128]{2,1,0:T(8,128)(2,1)} %add_convert_fusion), calls=%async_computation.3 | async-start | bytes 1048576 | tf_op jit(solution)/shard_map/all_to_all | solution.py:249
  (4 other events, 3.4 us)

commit v2 on v1

v2 whole, which is shorter than its diff:
```python
import functools

import jax
import jax.numpy as jnp
from jax import lax
from jax.experimental import pallas as pl
from jax.experimental.pallas import tpu as pltpu
from jax.sharding import Mesh, PartitionSpec as P

HEADS = 8
HDIM = 128
ROWS = 128
TILE = 16
XS, ZS, CS = 4, 8, 2
CHUNKS = XS * ZS * CS
QB = 512
KB = 512
SLAB = 256
GROUP = 32
COLS = tuple(slice(i, i + SLAB) for i in range(0, QB, SLAB))
STEPS = CHUNKS * ROWS // KB
INV_ROOT = HDIM ** -0.5
LOG2E = 1.4426950408889634
NEG = -1e30

NT = (((1,), (1,)), ((), ()))
TN = (((0,), (0,)), ((), ()))


def dot(a, b, dims=(((1,), (0,)), ((), ()))):
    return lax.dot_general(a, b, dims, preferred_element_type=jnp.float32)


PIECES = ((0, 0, 8), (3, 0, 8), (1, 0, 8), (2, 0, 4), (2, 4, 4))


def attention_kernel(at_ref, *refs):
    pieces, qd_in, ad_ref, grads, refs = refs[:10], refs[10], refs[11], refs[12:20], refs[20:]
    kvs_ref, qd_ref, s_scr, e_scr, dk_scr, dv_scr, acc_scr, dq_scr, don_scr, q_scr, ds_scr, top_scr, sum_scr, qs_scr, sems, qsem = refs
    x, own_core = at_ref[0], at_ref[1]

    def first_chunk(distance, other):
        core = 1 - own_core if other else own_core
        return (lax.rem(x + distance, XS) * CS + core) * ZS

    copies = [pltpu.make_async_copy(qd_in, qd_ref, qsem.at[0])]
    for i, (distance, start, count) in enumerate(PIECES):
        for other in (0, 1):
            n = 2 * i + other
            copies.append(
                pltpu.make_async_copy(
                    pieces[n], kvs_ref.at[pl.ds(first_chunk(distance, other) + start, count)], sems.at[n]
                )
            )
    for copy in copies:
        copy.start()
    dk_scr[...] = jnp.zeros_like(dk_scr)
    dv_scr[...] = jnp.zeros_like(dv_scr)
    for copy in copies:
        copy.wait()

    key_scales = kvs_ref[:, 256:272, :].astype(jnp.float32)[:, 0, :]
    chunk = lax.broadcasted_iota(jnp.int32, key_scales.shape, 0)
    lane = lax.broadcasted_iota(jnp.int32, key_scales.shape, 1)
    core = (chunk // ZS) % CS
    parity = chunk % 2
    is_first = (core == 0) & (parity == 0) & (lane == 0)
    is_last = (core == 1) & (parity == 1) & (lane == ROWS - 1)

    def parts(step):
        base = (step // 4) * 16 + 2 * (step % 4)
        return (base, base + 8)

    def slab(step, half, start):
        return kvs_ref[pl.ds(parts(step)[half], 2), start : start + ROWS, :].reshape(SLAB, HDIM)

    def down(row):
        return jnp.broadcast_to(row, (ROWS, ROWS)).T

    def fold(tile, op):
        return op(tile.reshape(tile.shape[0] // 8, 8, tile.shape[1]), axis=0)

    def one_block(block, _):
        first = block * (QB // ROWS)

        def rows(start):
            return qd_ref[pl.ds(first, QB // ROWS), start : start + ROWS, :].reshape(QB, HDIM)

        own = qd_ref[pl.ds(first, QB // ROWS), 256:272, :].astype(jnp.float32)[:, 0, :]
        for i in range(QB // ROWS):
            qs_scr[:, i * ROWS : (i + 1) * ROWS] = jnp.broadcast_to(own[i : i + 1, :], (8, ROWS))
        low, high = jnp.min(own), jnp.max(own)
        n_steps = jnp.sum(jnp.where(is_first & (key_scales <= high), 1.0, 0.0)).astype(jnp.int32)
        n_full = jnp.sum(jnp.where(is_last & (key_scales <= low), 1.0, 0.0)).astype(jnp.int32)

        def scores(masked, step, _):
            for half in range(KB // SLAB):
                k = slab(step, half, 0)
                if masked:
                    ks = [
                        down(kvs_ref[parts(step)[half] + i, 256:272, :].astype(jnp.float32)[0:1, :])
                        for i in range(SLAB // ROWS)
                    ]
                for cols in COLS:
                    s = dot(k, q_scr[cols, :], NT)
                    top = top_scr[:, cols]
                    for r in range(0, SLAB, GROUP):
                        tile = s[r : r + GROUP, :]
                        if masked:
                            own_ks = ks[r // ROWS][r % ROWS : r % ROWS + GROUP, :]
                            tile = jnp.concatenate(
                                [
                                    jnp.where(
                                        own_ks <= qs_scr[0:1, cols.start + j : cols.start + j + ROWS],
                                        tile[:, j : j + ROWS],
                                        NEG,
                                    )
                                    for j in range(0, SLAB, ROWS)
                                ],
                                axis=1,
                            )
                        s_scr[step, half * SLAB + r : half * SLAB + r + GROUP, cols] = tile
                        top = jnp.maximum(top, fold(tile, jnp.max))
                    top_scr[:, cols] = top
            return 0

        q_scr[...] = rows(0)
        top_scr[...] = jnp.full_like(top_scr, NEG)
        lax.fori_loop(0, n_full, functools.partial(scores, False), 0)
        lax.fori_loop(n_full, n_steps, functools.partial(scores, True), 0)
        top = jnp.max(top_scr[...], axis=0, keepdims=True) * (INV_ROOT * LOG2E)
        top_scr[...] = jnp.broadcast_to(top, top_scr.shape)
        sum_scr[...] = jnp.zeros_like(sum_scr)
        acc_scr[...] = jnp.zeros_like(acc_scr)

        def forward(step, _):
            for half in range(KB // SLAB):
                total = sum_scr[...]
                for r in range(half * SLAB, (half + 1) * SLAB, GROUP):
                    e = jnp.exp2(s_scr[step, r : r + GROUP, :] * (INV_ROOT * LOG2E) - top_scr[0:1, :])
                    total = total + fold(e, jnp.sum)
                    e_scr[step, r : r + GROUP, :] = e.astype(jnp.bfloat16)
                sum_scr[...] = total
                acc_scr[...] += dot(slab(step, half, 128), e_scr[step, half * SLAB : (half + 1) * SLAB, :], TN)
            return 0

        lax.fori_loop(0, n_steps, forward, 0)
        inv = 1.0 / jnp.sum(sum_scr[...], axis=0, keepdims=True)
        attn = (acc_scr[...] * inv).T
        inv_rows = jnp.broadcast_to(inv, (HDIM, QB)).T
        for i in range(QB // ROWS):
            ad_ref[first + i, 0:128, :] = attn[i * ROWS : (i + 1) * ROWS, :].astype(jnp.bfloat16)
        do_n = (rows(128).astype(jnp.float32) * inv_rows).astype(jnp.bfloat16)
        don_scr[...] = do_n
        delta = jnp.sum(do_n.astype(jnp.float32) * attn, axis=1, keepdims=True)
        top_scr[...] = jnp.broadcast_to(delta, (QB, HDIM)).T[0:8, :]
        dq_scr[...] = jnp.zeros_like(dq_scr)

        def backward(step, _):
            for half in range(KB // SLAB):
                own = slice(half * SLAB, (half + 1) * SLAB)
                v = slab(step, half, 128)
                for cols in COLS:
                    dp = dot(v, don_scr[cols, :], NT)
                    for r in range(0, SLAB, GROUP):
                        e = e_scr[step, half * SLAB + r : half * SLAB + r + GROUP, cols].astype(jnp.float32)
                        ds = e * (dp[r : r + GROUP, :] - top_scr[0:1, cols])
                        ds_scr[half, r : r + GROUP, cols] = ds.astype(jnp.bfloat16)
                dv = dot(e_scr[step, own, :], don_scr[...])
                dk = dot(ds_scr[half], q_scr[...])
                at_chunks = pl.ds(parts(step)[half], 2)
                dv_scr[at_chunks] += dv.reshape(2, ROWS, HDIM)
                dk_scr[at_chunks] += dk.reshape(2, ROWS, HDIM)
                dq_scr[...] += dot(slab(step, half, 0), ds_scr[half], TN)
            return 0

        lax.fori_loop(0, n_steps, backward, 0)
        dq = (dq_scr[...] * INV_ROOT).T.astype(jnp.bfloat16)
        for i in range(QB // ROWS):
            ad_ref[first + i, 128:256, :] = dq[i * ROWS : (i + 1) * ROWS, :]
        return 0

    lax.fori_loop(0, ZS * ROWS // QB, one_block, 0)

    for distance in range(XS):
        for other in (0, 1):
            out = grads[2 * distance + other]
            base = first_chunk(distance, other)
            out[:, 0:128, :] = (dk_scr[pl.ds(base, ZS)] * INV_ROOT).astype(jnp.bfloat16)
            out[:, 128:256, :] = dv_scr[pl.ds(base, ZS)].astype(jnp.bfloat16)


def attention(at, pieces, qd):
    vmem = pl.BlockSpec(memory_space=pltpu.VMEM)
    outs = (jax.ShapeDtypeStruct((ZS, 2 * ROWS, HDIM), jnp.bfloat16),) * 9
    return pl.pallas_call(
        attention_kernel,
        out_shape=outs,
        in_specs=[pl.BlockSpec(memory_space=pltpu.SMEM)] + [vmem] * 11,
        out_specs=(vmem,) * len(outs),
        scratch_shapes=[
            pltpu.VMEM((CHUNKS, 2 * ROWS + TILE, HDIM), jnp.bfloat16),
            pltpu.VMEM((ZS, 2 * ROWS + TILE, HDIM), jnp.bfloat16),
            pltpu.VMEM((STEPS, KB, QB), jnp.float32),
            pltpu.VMEM((STEPS, KB, QB), jnp.bfloat16),
            pltpu.VMEM((CHUNKS, ROWS, HDIM), jnp.float32),
            pltpu.VMEM((CHUNKS, ROWS, HDIM), jnp.float32),
            pltpu.VMEM((HDIM, QB), jnp.float32),
            pltpu.VMEM((HDIM, QB), jnp.float32),
            pltpu.VMEM((QB, HDIM), jnp.bfloat16),
            pltpu.VMEM((QB, HDIM), jnp.bfloat16),
            pltpu.VMEM((KB // SLAB, SLAB, QB), jnp.bfloat16),
            pltpu.VMEM((8, QB), jnp.float32),
            pltpu.VMEM((8, QB), jnp.float32),
            pltpu.VMEM((8, QB), jnp.float32),
            pltpu.SemaphoreType.DMA((10,)),
            pltpu.SemaphoreType.DMA((1,)),
        ],
        compiler_params=pltpu.CompilerParams(vmem_limit_bytes=42 * 1024 * 1024),
        cost_estimate=pl.CostEstimate(flops=8 * 10**9, bytes_accessed=10 * 2**20, transcendentals=5 * 10**6),
    )(at, *pieces, qd)


def pack_kernel(a_ref, b_ref, scale_ref, out_ref):
    scales = jnp.broadcast_to(scale_ref[...].astype(jnp.float32), (TILE, ROWS)).astype(jnp.bfloat16)
    for h in range(HEADS):
        out_ref[h, 0:128, :] = a_ref[0, :, h * HDIM : (h + 1) * HDIM]
        out_ref[h, 128:256, :] = b_ref[0, :, h * HDIM : (h + 1) * HDIM]
        out_ref[h, 256:272, :] = scales


def pack(a, b, scale_ids):
    vmem = pl.BlockSpec(memory_space=pltpu.VMEM)
    return pl.pallas_call(
        pack_kernel,
        out_shape=jax.ShapeDtypeStruct((HEADS, 2 * ROWS + TILE, HDIM), jnp.bfloat16),
        in_specs=[vmem] * 3,
        out_specs=vmem,
    )(a, b, scale_ids)


def unpack_kernel(in_ref, *outs):
    for h in range(HEADS):
        for i, out in enumerate(outs):
            out[0, :, h * HDIM : (h + 1) * HDIM] = in_ref[h, i * ROWS : (i + 1) * ROWS, :]


def unpack(arr):
    vmem = pl.BlockSpec(memory_space=pltpu.VMEM)
    rows = jax.ShapeDtypeStruct((1, ROWS, HEADS * HDIM), jnp.bfloat16)
    n = arr.shape[1] // ROWS
    return pl.pallas_call(unpack_kernel, out_shape=(rows,) * n, in_specs=[vmem], out_specs=(vmem,) * n)(arr)


def add(*arrs):
    total = arrs[0].astype(jnp.float32)
    for arr in arrs[1:]:
        total = total + arr.astype(jnp.float32)
    return total.astype(jnp.bfloat16)


def local(query, key, value, grad_attn, scale_ids):
    def over_heads(arr):
        return lax.all_to_all(arr, "z", split_axis=0, concat_axis=0, tiled=True)

    def right(arr):
        return lax.ppermute(arr, "x", [(i, (i + 1) % XS) for i in range(XS)])

    def left(arr):
        return lax.ppermute(arr, "x", [(i, (i + XS - 1) % XS) for i in range(XS)])

    def swap(arr):
        pairs = [
            (x * ZS + z, (XS - 1 - x if z >= ZS // 2 else x) * ZS + z) for x in range(XS) for z in range(ZS)
        ]
        return lax.ppermute(arr, ("x", "z"), pairs)

    def twin(arr):
        return lax.ppermute(arr, "core", [(0, 1), (1, 0)])

    half = ZS // 2
    at = jnp.stack([lax.axis_index("x"), lax.axis_index("core")]).astype(jnp.int32)

    kvs = over_heads(pack(key, value, scale_ids))
    swapped = swap(pack(query, grad_attn, scale_ids))
    kvs, swapped = lax.optimization_barrier((kvs, swapped))
    from_left, from_right = right(kvs), left(kvs)
    qd = over_heads(swapped)
    opposite_a, opposite_b = right(from_left[:half]), left(from_right[half:])
    pieces = []
    for piece in (kvs, from_left, from_right, opposite_a, opposite_b):
        pieces += [piece, twin(piece)]

    ad, *grads = attention(at, pieces, qd)

    far = add(grads[4], twin(grads[5]))
    far, *grads = lax.optimization_barrier((far, *grads))
    sums = {distance: add(grads[2 * distance], twin(grads[2 * distance + 1])) for distance in (3, 1, 0)}
    ad, sums[1], sums[3] = lax.optimization_barrier((ad, sums[1], sums[3]))
    ad_back = over_heads(ad)
    k, v = slice(0, ROWS), slice(ROWS, 2 * ROWS)
    key_left = left(sums[3][:, k])
    key_right = right(add(sums[1][:, k], right(far[:, k])))
    value_left = left(add(sums[3][:, v], left(far[:, v])))
    value_right = right(sums[1][:, v])
    key_sum = add(sums[0][:, k], key_right, key_left)
    value_sum = add(sums[0][:, v], value_right, value_left)
    value_sum, ad_back = lax.optimization_barrier((value_sum, ad_back))
    return (
        *unpack(swap(ad_back)),
        *unpack(over_heads(key_sum)),
        *unpack(over_heads(value_sum)),
    )


def solution(mesh):
    fine = Mesh(mesh.devices.reshape(mesh.devices.shape[0], XS, ZS, CS), ("batch", "x", "z", "core"))
    seq = ("x", "z", "core")
    rows = P("batch", seq, None)
    return jax.shard_map(
        local,
        mesh=fine,
        in_specs=(rows, rows, rows, rows, P("batch", seq)),
        out_specs=(rows, rows, rows, rows),
        check_vma=False,
    )
```

time: 182 us -> 166 us (0.912)
  waiting for transfers between devices: 79.4 us -> 56.2 us
  starting transfers between devices: 48.8 us -> 61.3 us
  Pallas kernels: 42.7 us -> 38.7 us
  other arithmetic: 4.13 us -> 1.79 us
    all_to_all x4 -> x5, waiting for transfers between devices: 45.2 us -> 28.9 us  [over_heads(): return lax.all_to_all(arr, 'z', split_axis=0, concat_axis=0, tiled=True)]
    ppermute x4 -> x5, waiting for transfers between devices: 4.11 us -> 16.1 us  [left(): return lax.ppermute(arr, 'x', [(i, (i + XS - 1) % XS) for i in range(XS)])]
    ppermute x2, waiting for transfers between devices: 12 us -> 0.01 us  [swap(): return lax.ppermute(arr, ('x', 'z'), pairs)]
    all_to_all x4 -> x5, starting transfers between devices: 22.2 us -> 32.4 us  [over_heads(): return lax.all_to_all(arr, 'z', split_axis=0, concat_axis=0, tiled=True)]
    ppermute x4 -> x5, waiting for transfers between devices: 16.9 us -> 7.86 us  [right(): return lax.ppermute(arr, 'x', [(i, (i + 1) % XS) for i in range(XS)])]
    ppermute x2, starting transfers between devices: 14.2 us -> 6.52 us  [swap(): return lax.ppermute(arr, ('x', 'z'), pairs)]
    ppermute x4 -> x5, starting transfers between devices: 9.9 us -> 17.1 us  [left(): return lax.ppermute(arr, 'x', [(i, (i + XS - 1) % XS) for i in range(XS)])]
    pallas_call x1, Pallas kernels: 34.9 us -> 29.4 us  [attention(): pl.pallas_call(attention_kernel, out_shape=outs, in_specs=[pl.BlockSpec(m...]
  transfers between devices with their start and end apart: 23 -> 26, of which waited for: 11 -> 12; matrix products, arithmetic and copies ran while one was open for 3% -> 2% of each run, Pallas kernels for 2% -> 3%
where the time goes in v2:
time: 166 us; the launch traced here: 164 us
  starting transfers between devices  61.3 us (37%)
  waiting for transfers between devices  56.2 us (34%)
  Pallas kernels  38.7 us (23%)
  local copies, waits for them, and re-layouts  5.48 us (3%)
  other arithmetic  1.79 us (1%)
    all_to_all x5, starting transfers between devices, over_heads(): return lax.all_to_all(arr, 'z', split_axis=0, concat_axis=0, tiled=True)  32.4 us
    pallas_call x1, Pallas kernels, attention(): pl.pallas_call(attention_kernel, out_shape=outs, in_specs=[pl.BlockSpec(m...  29.4 us
    all_to_all x5, waiting for transfers between devices, over_heads(): return lax.all_to_all(arr, 'z', split_axis=0, concat_axis=0, tiled=True)  28.9 us
    ppermute x5, starting transfers between devices, left(): return lax.ppermute(arr, 'x', [(i, (i + XS - 1) % XS) for i in range(XS)])  17.1 us
    ppermute x5, waiting for transfers between devices, left(): return lax.ppermute(arr, 'x', [(i, (i + XS - 1) % XS) for i in range(XS)])  16.1 us
    ppermute x5, waiting for transfers between devices, right(): return lax.ppermute(arr, 'x', [(i, (i + 1) % XS) for i in range(XS)])  7.86 us
    ppermute x2, starting transfers between devices, swap(): return lax.ppermute(arr, ('x', 'z'), pairs)  6.52 us
    pallas_call x3, Pallas kernels, unpack(): pl.pallas_call(unpack_kernel, out_shape=(rows,) * n, in_specs=[vmem], out...  5.42 us
  transfers between devices with their start and end apart: 26, of which 12 were waited for; matrix products, arithmetic and copies ran while one was open for 2% of the time, Pallas kernels for 3%

profile of v2, /device:TPU:16, one launch (start us, length us, event | category | flops | bytes accessed | tf_op | source)
XLA Modules:
  0.0 164.2 jit_solution(9915226262629024873)
XLA Ops:
  0.6 1.9 %shard_map.84 = bf16[8,272,128]{2,1,0:T(8,128)(2,1)} custom-call(bf16[1,128,1024]{2,1,0:T(8,128)(2,1)} %a_ref.2, bf16[1,128,1024]{2,1,0:T(8,128)(2,1)} %b_ref.2, s32[1,128]{1,0:T(1,128)} %scale_ref.3), custom_call_target="tpu_custom_call" | custom-call | tf_op jit(solution)/shard_map/pallas_call | solution.py:234
  2.6 8.5 %all-to-all-start = ((bf16[8,272,128]{2,1,0:T(8,128)(2,1)}), bf16[8,272,128]{2,1,0:T(8,128)(2,1)S(1)}, u32[]{:S(2)}, u32[]{:S(2)}) async-start(bf16[8,272,128]{2,1,0:T(8,128)(2,1)} %shard_map.84), calls=%async_computation | async-start | bytes 1114112 | tf_op jit(solution)/shard_map/all_to_all | solution.py:264
  11.0 2.0 %shard_map.85 = bf16[8,272,128]{2,1,0:T(8,128)(2,1)} custom-call(bf16[1,128,1024]{2,1,0:T(8,128)(2,1)} %a_ref.3, bf16[1,128,1024]{2,1,0:T(8,128)(2,1)} %b_ref.3, s32[1,128]{1,0:T(1,128)} %scale_ref.3), custom_call_target="tpu_custom_call" | custom-call | tf_op jit(solution)/shard_map/pallas_call | solution.py:234
  13.0 5.8 %collective-permute-start = (bf16[8,272,128]{2,1,0:T(8,128)(2,1)}, bf16[8,272,128]{2,1,0:T(8,128)(2,1)}, u32[]{:S(2)}, u32[]{:S(2)}) collective-permute-start(bf16[8,272,128]{2,1,0:T(8,128)(2,1)} %shard_map.85), channel_id=1, source_target_pairs={{0,0},{2,2},{4,4},{6,6},{8,56},{10,58},{12,60},{14,62},{16,16},{18... | collective-permute-start | bytes 1671176 | tf_op jit(solution)/shard_map/ppermute | solution.py:276
  18.8 10.4 %all-to-all-done.refs_0_ = bf16[8,272,128]{2,1,0:T(8,128)(2,1)S(1)} async-done(((bf16[8,272,128]{2,1,0:T(8,128)(2,1)}), bf16[8,272,128]{2,1,0:T(8,128)(2,1)S(1)}, u32[]{:S(2)}, u32[]{:S(2)}) %all-to-all-start) | async-done | bytes 557088 | tf_op jit(solution)/shard_map/all_to_all | solution.py:264
  29.2 2.8 %collective-permute-start.4 = (bf16[8,272,128]{2,1,0:T(8,128)(2,1)S(1)}, bf16[8,272,128]{2,1,0:T(8,128)(2,1)S(1)}, u32[]{:S(2)}, u32[]{:S(2)}) collective-permute-start(bf16[8,272,128]{2,1,0:T(8,128)(2,1)S(1)} %all-to-all-done.refs_0_), channel_id=1, source_target_pairs={{0,48},{16,0},{32,16},{48,32},{1,49},{17,1},{33,17},{49,33},{2,50}... | collective-permute-start | bytes 1671176 | tf_op jit(solution)/shard_map/ppermute | solution.py:270
  32.0 8.2 %all-to-all-start.1 = ((bf16[8,272,128]{2,1,0:T(8,128)(2,1)}), bf16[8,272,128]{2,1,0:T(8,128)(2,1)S(1)}, u32[]{:S(2)}, u32[]{:S(2)}) async-start(bf16[8,272,128]{2,1,0:T(8,128)(2,1)} %collective-permute-done), calls=%async_computation.1 | async-start | bytes 1114112 | tf_op jit(solution)/shard_map/all_to_all | solution.py:264
  40.2 3.9 %collective-permute-done.4.refs_4_ = bf16[8,272,128]{2,1,0:T(8,128)(2,1)S(1)} collective-permute-done((bf16[8,272,128]{2,1,0:T(8,128)(2,1)S(1)}, bf16[8,272,128]{2,1,0:T(8,128)(2,1)S(1)}, u32[]{:S(2)}, u32[]{:S(2)}) %collective-permute-start.4) | collective-permute-done | bytes 557088 | tf_op jit(solution)/shard_map/ppermute | solution.py:270
  44.1 3.8 %collective-permute-start.8 = (bf16[4,272,128]{2,1,0:T(8,128)(2,1)S(1)}, bf16[4,272,128]{2,1,0:T(8,128)(2,1)S(1)}, u32[]{:S(2)}, u32[]{:S(2)}) collective-permute-start(bf16[4,272,128]{2,1,0:T(8,128)(2,1)S(1)} %slice.41), channel_id=1, source_target_pairs={{0,48},{16,0},{32,16},{48,32},{1,49},{17,1},{33,17},{49,33},{2,50}... | collective-permute-start | bytes 835592 | tf_op jit(solution)/shard_map/ppermute | solution.py:270
  48.6 4.5 %collective-permute-done.8.refs_8_ = bf16[4,272,128]{2,1,0:T(8,128)(2,1)S(1)} collective-permute-done((bf16[4,272,128]{2,1,0:T(8,128)(2,1)S(1)}, bf16[4,272,128]{2,1,0:T(8,128)(2,1)S(1)}, u32[]{:S(2)}, u32[]{:S(2)}) %collective-permute-start.8) | collective-permute-done | bytes 278560 | tf_op jit(solution)/shard_map/ppermute | solution.py:270
  53.8 2.9 %collective-permute-done.6.refs_6_ = bf16[4,272,128]{2,1,0:T(8,128)(2,1)} collective-permute-done((bf16[4,272,128]{2,1,0:T(8,128)(2,1)S(1)}, bf16[4,272,128]{2,1,0:T(8,128)(2,1)}, u32[]{:S(2)}, u32[]{:S(2)}) %collective-permute-start.6) | collective-permute-done | bytes 278560 | tf_op jit(solution)/shard_map/ppermute | solution.py:267
  56.8 1.8 %collective-permute-done.7.refs_7_ = bf16[4,272,128]{2,1,0:T(8,128)(2,1)} collective-permute-done((bf16[4,272,128]{2,1,0:T(8,128)(2,1)}, bf16[4,272,128]{2,1,0:T(8,128)(2,1)}, u32[]{:S(2)}, u32[]{:S(2)}) %collective-permute-start.7) | collective-permute-done | bytes 278560 | tf_op jit(solution)/shard_map/ppermute | solution.py:279
  58.6 1.0 copy-done.1
  59.6 29.4 %shard_map.86 = (bf16[8,256,128]{2,1,0:T(8,128)(2,1)}, bf16[8,256,128]{2,1,0:T(8,128)(2,1)S(1)}, bf16[8,256,128]{2,1,0:T(8,128)(2,1)}, bf16[8,256,128]{2,1,0:T(8...) custom-call(s32[2]{0:T(128)S(1)} %pad_add_fusion.at_ref, ...), custom_call_target="tpu_custom_call" | custom-call | flops 8000000000 | bytes 10485760 | tf_op jit(solution)/shard_map/pallas_call | solution.py:196
  89.0 1.5 collective-permute-start.10
  90.5 1.5 collective-permute-done.10
  94.2 3.2 %collective-permute-start.15 = (bf16[8,128,128]{2,1,0:T(8,128)(2,1)}, bf16[8,128,128]{2,1,0:T(8,128)(2,1)S(1)}, u32[]{:S(2)}, u32[]{:S(2)}) collective-permute-start(bf16[8,128,128]{2,1,0:T(8,128)(2,1)} %get-tuple-element.57), channel_id=1, source_target_pairs={{0,48},{16,0},{32,16},{48,32},{1,49},{17,1},{33,17},{49,33},{2,50}... | collective-permute-start | bytes 786440 | tf_op jit(solution)/shard_map/ppermute | solution.py:270
  98.6 5.4 %all-to-all-start.2 = ((bf16[8,256,128]{2,1,0:T(8,128)(2,1)}), bf16[8,256,128]{2,1,0:T(8,128)(2,1)S(1)}, u32[]{:S(2)}, u32[]{:S(2)}) async-start(bf16[8,256,128]{2,1,0:T(8,128)(2,1)} %get-tuple-element.49), calls=%async_computation.2 | async-start | bytes 1048576 | tf_op jit(solution)/shard_map/all_to_all | solution.py:264
  103.9 5.3 %collective-permute-start.20 = (bf16[8,128,128]{2,1,0:T(8,128)(2,1)}, bf16[8,128,128]{2,1,0:T(8,128)(2,1)S(1)}, u32[]{:S(2)}, u32[]{:S(2)}) collective-permute-start(bf16[8,128,128]{2,1,0:T(8,128)(2,1)} %slice.39), channel_id=1, source_target_pairs={{0,48},{16,0},{32,16},{48,32},{1,49},{17,1},{33,17},{49,33},{2,50}... | collective-permute-start | bytes 786440 | tf_op jit(solution)/shard_map/ppermute | solution.py:270
  109.3 2.0 %collective-permute-start.16 = (bf16[8,128,128]{2,1,0:T(8,128)(2,1)S(1)}, bf16[8,128,128]{2,1,0:T(8,128)(2,1)S(1)}, u32[]{:S(2)}, u32[]{:S(2)}) collective-permute-start(bf16[8,128,128]{2,1,0:T(8,128)(2,1)S(1)} %add_convert_fusion.7), channel_id=1, source_target_pairs={{0,48},{16,0},{32,16},{48,32},{1,49},{17,1},{33,17},{49,33},{2,50}... | collective-permute-start | bytes 786440 | tf_op jit(solution)/shard_map/ppermute | solution.py:270
  111.5 1.8 %collective-permute-start.19 = (bf16[8,128,128]{2,1,0:T(8,128)(2,1)S(1)}, bf16[8,128,128]{2,1,0:T(8,128)(2,1)S(1)}, u32[]{:S(2)}, u32[]{:S(2)}) collective-permute-start(bf16[8,128,128]{2,1,0:T(8,128)(2,1)S(1)} %add_convert_fusion.5), channel_id=1, source_target_pairs={{0,16},{16,32},{32,48},{48,0},{1,17},{17,33},{33,49},{49,1},{2,18}... | collective-permute-start | bytes 786440 | tf_op jit(solution)/shard_map/ppermute | solution.py:267
  113.4 2.8 %collective-permute-done.20 = bf16[8,128,128]{2,1,0:T(8,128)(2,1)S(1)} collective-permute-done((bf16[8,128,128]{2,1,0:T(8,128)(2,1)}, bf16[8,128,128]{2,1,0:T(8,128)(2,1)S(1)}, u32[]{:S(2)}, u32[]{:S(2)}) %collective-permute-start.20) | collective-permute-done | bytes 262176 | tf_op jit(solution)/shard_map/ppermute | solution.py:270
  116.2 4.9 %collective-permute-done.16 = bf16[8,128,128]{2,1,0:T(8,128)(2,1)S(1)} collective-permute-done((bf16[8,128,128]{2,1,0:T(8,128)(2,1)S(1)}, bf16[8,128,128]{2,1,0:T(8,128)(2,1)S(1)}, u32[]{:S(2)}, u32[]{:S(2)}) %collective-permute-start.16) | collective-permute-done | bytes 262176 | tf_op jit(solution)/shard_map/ppermute | solution.py:270
  121.7 4.3 %collective-permute-done.19 = bf16[8,128,128]{2,1,0:T(8,128)(2,1)S(1)} collective-permute-done((bf16[8,128,128]{2,1,0:T(8,128)(2,1)S(1)}, bf16[8,128,128]{2,1,0:T(8,128)(2,1)S(1)}, u32[]{:S(2)}, u32[]{:S(2)}) %collective-permute-start.19) | collective-permute-done | bytes 262176 | tf_op jit(solution)/shard_map/ppermute | solution.py:267
  126.0 1.0 add_convert_fusion.4
  127.0 6.9 %all-to-all-start.3 = ((bf16[8,128,128]{2,1,0:T(8,128)(2,1)}), bf16[8,128,128]{2,1,0:T(8,128)(2,1)S(1)}, u32[]{:S(2)}, u32[]{:S(2)}) async-start(bf16[8,128,128]{2,1,0:T(8,128)(2,1)} %get-tuple-element.54), calls=%async_computation.3 | async-start | bytes 524288 | tf_op jit(solution)/shard_map/all_to_all | solution.py:264
  134.7 9.8 %all-to-all-done.3.in_ref = bf16[8,128,128]{2,1,0:T(8,128)(2,1)S(1)} async-done(((bf16[8,128,128]{2,1,0:T(8,128)(2,1)}), bf16[8,128,128]{2,1,0:T(8,128)(2,1)S(1)}, u32[]{:S(2)}, u32[]{:S(2)}) %all-to-all-start.3) | async-done | bytes 262176 | tf_op jit(solution)/shard_map/all_to_all | solution.py:264
  145.2 3.4 %all-to-all-start.4 = ((bf16[8,128,128]{2,1,0:T(8,128)(2,1)}), bf16[8,128,128]{2,1,0:T(8,128)(2,1)S(1)}, u32[]{:S(2)}, u32[]{:S(2)}) async-start(bf16[8,128,128]{2,1,0:T(8,128)(2,1)} %get-tuple-element.53), calls=%async_computation.4 | async-start | bytes 524288 | tf_op jit(solution)/shard_map/all_to_all | solution.py:264
  148.6 1.7 %shard_map.88 = bf16[1,128,1024]{2,1,0:T(8,128)(2,1)} custom-call(bf16[8,128,128]{2,1,0:T(8,128)(2,1)} %copy-done.2), custom_call_target="tpu_custom_call" | custom-call | tf_op jit(solution)/shard_map/pallas_call | solution.py:252
  150.3 8.7 %all-to-all-done.4.in_ref = bf16[8,128,128]{2,1,0:T(8,128)(2,1)S(1)} async-done(((bf16[8,128,128]{2,1,0:T(8,128)(2,1)}), bf16[8,128,128]{2,1,0:T(8,128)(2,1)S(1)}, u32[]{:S(2)}, u32[]{:S(2)}) %all-to-all-start.4) | async-done | bytes 262176 | tf_op jit(solution)/shard_map/all_to_all | solution.py:264
  159.7 1.7 %shard_map.89 = bf16[1,128,1024]{2,1,0:T(8,128)(2,1)} custom-call(bf16[8,128,128]{2,1,0:T(8,128)(2,1)} %copy-done.3), custom_call_target="tpu_custom_call" | custom-call | tf_op jit(solution)/shard_map/pallas_call | solution.py:252
  162.2 2.0 %shard_map.87 = (bf16[1,128,1024]{2,1,0:T(8,128)(2,1)}, bf16[1,128,1024]{2,1,0:T(8,128)(2,1)}) custom-call(bf16[8,256,128]{2,1,0:T(8,128)(2,1)} %copy-done.4), custom_call_target="tpu_custom_call" | custom-call | tf_op jit(solution)/shard_map/pallas_call | solution.py:252
  (49 shorter events, 8.7 us)
Async XLA Ops:
  2.6 26.7 %all-to-all-start = ((bf16[8,272,128]{2,1,0:T(8,128)(2,1)}), bf16[8,272,128]{2,1,0:T(8,128)(2,1)S(1)}, u32[]{:S(2)}, u32[]{:S(2)}) async-start(bf16[8,272,128]{2,1,0:T(8,128)(2,1)} %shard_map.84), calls=%async_computation | async-start | bytes 1114112 | tf_op jit(solution)/shard_map/all_to_all | solution.py:264
  13.0 5.8 %collective-permute-start = (bf16[8,272,128]{2,1,0:T(8,128)(2,1)}, bf16[8,272,128]{2,1,0:T(8,128)(2,1)}, u32[]{:S(2)}, u32[]{:S(2)}) collective-permute-start(bf16[8,272,128]{2,1,0:T(8,128)(2,1)} %shard_map.85), channel_id=1, source_target_pairs={{0,0},{2,2},{4,4},{6,6},{8,56},{10,58},{12,60},{14,62},{16,16},{18... | collective-permute-start | bytes 1671176 | tf_op jit(solution)/shard_map/ppermute | solution.py:276
  29.2 14.8 %collective-permute-start.4 = (bf16[8,272,128]{2,1,0:T(8,128)(2,1)S(1)}, bf16[8,272,128]{2,1,0:T(8,128)(2,1)S(1)}, u32[]{:S(2)}, u32[]{:S(2)}) collective-permute-start(bf16[8,272,128]{2,1,0:T(8,128)(2,1)S(1)} %all-to-all-done.refs_0_), channel_id=1, source_target_pairs={{0,48},{16,0},{32,16},{48,32},{1,49},{17,1},{33,17},{49,33},{2,50}... | collective-permute-start | bytes 1671176 | tf_op jit(solution)/shard_map/ppermute | solution.py:270
  32.0 15.9 %collective-permute-start.2 = (bf16[8,272,128]{2,1,0:T(8,128)(2,1)S(1)}, bf16[8,272,128]{2,1,0:T(8,128)(2,1)S(1)}, u32[]{:S(2)}, u32[]{:S(2)}) collective-permute-start(bf16[8,272,128]{2,1,0:T(8,128)(2,1)S(1)} %all-to-all-done.refs_0_), channel_id=1, source_target_pairs={{0,16},{16,32},{32,48},{48,0},{1,17},{17,33},{33,49},{49,1},{2,18}... | collective-permute-start | bytes 1671176 | tf_op jit(solution)/shard_map/ppermute | solution.py:267
  32.0 24.8 %all-to-all-start.1 = ((bf16[8,272,128]{2,1,0:T(8,128)(2,1)}), bf16[8,272,128]{2,1,0:T(8,128)(2,1)S(1)}, u32[]{:S(2)}, u32[]{:S(2)}) async-start(bf16[8,272,128]{2,1,0:T(8,128)(2,1)} %collective-permute-done), calls=%async_computation.1 | async-start | bytes 1114112 | tf_op jit(solution)/shard_map/all_to_all | solution.py:264
  40.2 16.6 %collective-permute-start.1 = (bf16[8,272,128]{2,1,0:T(8,128)(2,1)S(1)}, bf16[8,272,128]{2,1,0:T(8,128)(2,1)S(1)}, u32[]{:S(2)}, u32[]{:S(2)}) collective-permute-start(bf16[8,272,128]{2,1,0:T(8,128)(2,1)S(1)} %all-to-all-done.refs_0_), channel_id=1, source_target_pairs={{0,1},{1,0},{2,3},{3,2},{4,5},{5,4},{6,7},{7,6},{8,9},{9,8},{10,11... | collective-permute-start | bytes 1671176 | tf_op jit(solution)/shard_map/ppermute | solution.py:279
  44.1 9.0 %collective-permute-start.8 = (bf16[4,272,128]{2,1,0:T(8,128)(2,1)S(1)}, bf16[4,272,128]{2,1,0:T(8,128)(2,1)S(1)}, u32[]{:S(2)}, u32[]{:S(2)}) collective-permute-start(bf16[4,272,128]{2,1,0:T(8,128)(2,1)S(1)} %slice.41), channel_id=1, source_target_pairs={{0,48},{16,0},{32,16},{48,32},{1,49},{17,1},{33,17},{49,33},{2,50}... | collective-permute-start | bytes 835592 | tf_op jit(solution)/shard_map/ppermute | solution.py:270
  47.9 8.8 %collective-permute-start.6 = (bf16[4,272,128]{2,1,0:T(8,128)(2,1)S(1)}, bf16[4,272,128]{2,1,0:T(8,128)(2,1)}, u32[]{:S(2)}, u32[]{:S(2)}) collective-permute-start(bf16[4,272,128]{2,1,0:T(8,128)(2,1)S(1)} %slice.40), channel_id=1, source_target_pairs={{0,16},{16,32},{32,48},{48,0},{1,17},{17,33},{33,49},{49,1},{2,18}... | collective-permute-start | bytes 835592 | tf_op jit(solution)/shard_map/ppermute | solution.py:267
  48.0 10.7 %collective-permute-start.5 = (bf16[8,272,128]{2,1,0:T(8,128)(2,1)S(1)}, bf16[8,272,128]{2,1,0:T(8,128)(2,1)}, u32[]{:S(2)}, u32[]{:S(2)}) collective-permute-start(bf16[8,272,128]{2,1,0:T(8,128)(2,1)S(1)} %collective-permute-done.4.refs_4_), channel_id=1, source_target_pairs={{0,1},{1,0},{2,3},{3,2},{4,5},{5,4},{6,7},{7,6},{8,9},{9,8},{10,11... | collective-permute-start | bytes 1671176 | tf_op jit(solution)/shard_map/ppermute | solution.py:279
  48.1 10.6 %collective-permute-start.3 = (bf16[8,272,128]{2,1,0:T(8,128)(2,1)S(1)}, bf16[8,272,128]{2,1,0:T(8,128)(2,1)}, u32[]{:S(2)}, u32[]{:S(2)}) collective-permute-start(bf16[8,272,128]{2,1,0:T(8,128)(2,1)S(1)} %collective-permute-done.2.refs_2_), channel_id=1, source_target_pairs={{0,1},{1,0},{2,3},{3,2},{4,5},{5,4},{6,7},{7,6},{8,9},{9,8},{10,11... | collective-permute-start | bytes 1671176 | tf_op jit(solution)/shard_map/ppermute | solution.py:279
  53.1 3.7 %collective-permute-start.9 = (bf16[4,272,128]{2,1,0:T(8,128)(2,1)S(1)}, bf16[4,272,128]{2,1,0:T(8,128)(2,1)}, u32[]{:S(2)}, u32[]{:S(2)}) collective-permute-start(bf16[4,272,128]{2,1,0:T(8,128)(2,1)S(1)} %collective-permute-done.8.refs_8_), channel_id=1, source_target_pairs={{0,1},{1,0},{2,3},{3,2},{4,5},{5,4},{6,7},{7,6},{8,9},{9,8},{10,11... | collective-permute-start | bytes 835592 | tf_op jit(solution)/shard_map/ppermute | solution.py:279
  53.1 0.7 copy-start
  56.7 1.9 %collective-permute-start.7 = (bf16[4,272,128]{2,1,0:T(8,128)(2,1)}, bf16[4,272,128]{2,1,0:T(8,128)(2,1)}, u32[]{:S(2)}, u32[]{:S(2)}) collective-permute-start(bf16[4,272,128]{2,1,0:T(8,128)(2,1)} %collective-permute-done.6.refs_6_), channel_id=1, source_target_pairs={{0,1},{1,0},{2,3},{3,2},{4,5},{5,4},{6,7},{7,6},{8,9},{9,8},{10,11... | collective-permute-start | bytes 835592 | tf_op jit(solution)/shard_map/ppermute | solution.py:279
  58.6 1.0 copy-start.1
  89.0 3.1 %collective-permute-start.10 = (bf16[8,256,128]{2,1,0:T(8,128)(2,1)S(1)}, bf16[8,256,128]{2,1,0:T(8,128)(2,1)S(1)}, u32[]{:S(2)}, u32[]{:S(2)}) collective-permute-start(bf16[8,256,128]{2,1,0:T(8,128)(2,1)S(1)} %get-tuple-element.32), channel_id=1, source_target_pairs={{0,1},{1,0},{2,3},{3,2},{4,5},{5,4},{6,7},{7,6},{8,9},{9,8},{10,11... | collective-permute-start | bytes 1572872 | tf_op jit(solution)/shard_map/ppermute | solution.py:279
  92.2 5.3 %collective-permute-start.12 = (bf16[8,256,128]{2,1,0:T(8,128)(2,1)S(1)}, bf16[8,256,128]{2,1,0:T(8,128)(2,1)S(1)}, u32[]{:S(2)}, u32[]{:S(2)}) collective-permute-start(bf16[8,256,128]{2,1,0:T(8,128)(2,1)S(1)} %get-tuple-element.43), channel_id=1, source_target_pairs={{0,1},{1,0},{2,3},{3,2},{4,5},{5,4},{6,7},{7,6},{8,9},{9,8},{10,11... | collective-permute-start | bytes 1572872 | tf_op jit(solution)/shard_map/ppermute | solution.py:279
  92.6 5.0 %collective-permute-start.13 = (bf16[8,256,128]{2,1,0:T(8,128)(2,1)S(1)}, bf16[8,256,128]{2,1,0:T(8,128)(2,1)S(1)}, u32[]{:S(2)}, u32[]{:S(2)}) collective-permute-start(bf16[8,256,128]{2,1,0:T(8,128)(2,1)S(1)} %get-tuple-element.45), channel_id=1, source_target_pairs={{0,1},{1,0},{2,3},{3,2},{4,5},{5,4},{6,7},{7,6},{8,9},{9,8},{10,11... | collective-permute-start | bytes 1572872 | tf_op jit(solution)/shard_map/ppermute | solution.py:279
  93.6 17.8 %collective-permute-start.18 = (bf16[8,128,128]{2,1,0:T(8,128)(2,1)}, bf16[8,128,128]{2,1,0:T(8,128)(2,1)S(1)}, u32[]{:S(2)}, u32[]{:S(2)}) collective-permute-start(bf16[8,128,128]{2,1,0:T(8,128)(2,1)} %get-tuple-element.56), channel_id=1, source_target_pairs={{0,16},{16,32},{32,48},{48,0},{1,17},{17,33},{33,49},{49,1},{2,18}... | collective-permute-start | bytes 786440 | tf_op jit(solution)/shard_map/ppermute | solution.py:267
  94.2 15.0 %collective-permute-start.15 = (bf16[8,128,128]{2,1,0:T(8,128)(2,1)}, bf16[8,128,128]{2,1,0:T(8,128)(2,1)S(1)}, u32[]{:S(2)}, u32[]{:S(2)}) collective-permute-start(bf16[8,128,128]{2,1,0:T(8,128)(2,1)} %get-tuple-element.57), channel_id=1, source_target_pairs={{0,48},{16,0},{32,16},{48,32},{1,49},{17,1},{33,17},{49,33},{2,50}... | collective-permute-start | bytes 786440 | tf_op jit(solution)/shard_map/ppermute | solution.py:270
  97.4 15.8 %collective-permute-start.11 = (bf16[8,256,128]{2,1,0:T(8,128)(2,1)}, bf16[8,256,128]{2,1,0:T(8,128)(2,1)S(1)}, u32[]{:S(2)}, u32[]{:S(2)}) collective-permute-start(bf16[8,256,128]{2,1,0:T(8,128)(2,1)} %get-tuple-element.40), channel_id=1, source_target_pairs={{0,1},{1,0},{2,3},{3,2},{4,5},{5,4},{6,7},{7,6},{8,9},{9,8},{10,11... | collective-permute-start | bytes 1572872 | tf_op jit(solution)/shard_map/ppermute | solution.py:279
  98.6 28.5 %all-to-all-start.2 = ((bf16[8,256,128]{2,1,0:T(8,128)(2,1)}), bf16[8,256,128]{2,1,0:T(8,128)(2,1)S(1)}, u32[]{:S(2)}, u32[]{:S(2)}) async-start(bf16[8,256,128]{2,1,0:T(8,128)(2,1)} %get-tuple-element.49), calls=%async_computation.2 | async-start | bytes 1048576 | tf_op jit(solution)/shard_map/all_to_all | solution.py:264
  103.9 12.3 %collective-permute-start.20 = (bf16[8,128,128]{2,1,0:T(8,128)(2,1)}, bf16[8,128,128]{2,1,0:T(8,128)(2,1)S(1)}, u32[]{:S(2)}, u32[]{:S(2)}) collective-permute-start(bf16[8,128,128]{2,1,0:T(8,128)(2,1)} %slice.39), channel_id=1, source_target_pairs={{0,48},{16,0},{32,16},{48,32},{1,49},{17,1},{33,17},{49,33},{2,50}... | collective-permute-start | bytes 786440 | tf_op jit(solution)/shard_map/ppermute | solution.py:270
  109.3 11.8 %collective-permute-start.16 = (bf16[8,128,128]{2,1,0:T(8,128)(2,1)S(1)}, bf16[8,128,128]{2,1,0:T(8,128)(2,1)S(1)}, u32[]{:S(2)}, u32[]{:S(2)}) collective-permute-start(bf16[8,128,128]{2,1,0:T(8,128)(2,1)S(1)} %add_convert_fusion.7), channel_id=1, source_target_pairs={{0,48},{16,0},{32,16},{48,32},{1,49},{17,1},{33,17},{49,33},{2,50}... | collective-permute-start | bytes 786440 | tf_op jit(solution)/shard_map/ppermute | solution.py:270
  111.3 10.4 %collective-permute-start.14 = (bf16[8,128,128]{2,1,0:T(8,128)(2,1)S(1)}, bf16[8,128,128]{2,1,0:T(8,128)(2,1)S(1)}, u32[]{:S(2)}, u32[]{:S(2)}) collective-permute-start(bf16[8,128,128]{2,1,0:T(8,128)(2,1)S(1)} %slice.33), channel_id=1, source_target_pairs={{0,16},{16,32},{32,48},{48,0},{1,17},{17,33},{33,49},{49,1},{2,18}... | collective-permute-start | bytes 786440 | tf_op jit(solution)/shard_map/ppermute | solution.py:267
  111.5 14.5 %collective-permute-start.19 = (bf16[8,128,128]{2,1,0:T(8,128)(2,1)S(1)}, bf16[8,128,128]{2,1,0:T(8,128)(2,1)S(1)}, u32[]{:S(2)}, u32[]{:S(2)}) collective-permute-start(bf16[8,128,128]{2,1,0:T(8,128)(2,1)S(1)} %add_convert_fusion.5), channel_id=1, source_target_pairs={{0,16},{16,32},{32,48},{48,0},{1,17},{17,33},{33,49},{49,1},{2,18}... | collective-permute-start | bytes 786440 | tf_op jit(solution)/shard_map/ppermute | solution.py:267
  127.0 17.4 %all-to-all-start.3 = ((bf16[8,128,128]{2,1,0:T(8,128)(2,1)}), bf16[8,128,128]{2,1,0:T(8,128)(2,1)S(1)}, u32[]{:S(2)}, u32[]{:S(2)}) async-start(bf16[8,128,128]{2,1,0:T(8,128)(2,1)} %get-tuple-element.54), calls=%async_computation.3 | async-start | bytes 524288 | tf_op jit(solution)/shard_map/all_to_all | solution.py:264
  134.0 27.4 %collective-permute-start.17 = (bf16[8,256,128]{2,1,0:T(8,128)(2,1)S(1)}, bf16[8,256,128]{2,1,0:T(8,128)(2,1)S(1)}, u32[]{:S(2)}, u32[]{:S(2)}) collective-permute-start(bf16[8,256,128]{2,1,0:T(8,128)(2,1)S(1)} %all-to-all-done.2), channel_id=1, source_target_pairs={{0,0},{2,2},{4,4},{6,6},{8,56},{10,58},{12,60},{14,62},{16,16},{18... | collective-permute-start | bytes 1572872 | tf_op jit(solution)/shard_map/ppermute | solution.py:276
  144.5 0.7 copy-start.2
  145.2 13.8 %all-to-all-start.4 = ((bf16[8,128,128]{2,1,0:T(8,128)(2,1)}), bf16[8,128,128]{2,1,0:T(8,128)(2,1)S(1)}, u32[]{:S(2)}, u32[]{:S(2)}) async-start(bf16[8,128,128]{2,1,0:T(8,128)(2,1)} %get-tuple-element.53), calls=%async_computation.4 | async-start | bytes 524288 | tf_op jit(solution)/shard_map/all_to_all | solution.py:264
  159.0 0.7 copy-start.3
  161.4 0.8 copy-start.4

commit v3 on v2

--- a/solution.py
+++ b/solution.py
@@ -32,11 +32,14 @@
 
 
 PIECES = ((0, 0, 8), (3, 0, 8), (1, 0, 8), (2, 0, 4), (2, 4, 4))
+N_PIECES = 2 * len(PIECES)
 
 
 def attention_kernel(at_ref, *refs):
-    pieces, qd_in, ad_ref, grads, refs = refs[:10], refs[10], refs[11], refs[12:20], refs[20:]
-    kvs_ref, qd_ref, s_scr, e_scr, dk_scr, dv_scr, acc_scr, dq_scr, don_scr, q_scr, ds_scr, top_scr, sum_scr, qs_scr, sems, qsem = refs
+    pieces, qd_in, ad_ref, grads, refs = (
+        refs[:N_PIECES], refs[N_PIECES], refs[N_PIECES + 1], refs[N_PIECES + 2 : N_PIECES + 10], refs[N_PIECES + 10 :],
+    )
+    kvs_ref, qd_ref, s_scr, e_scr, dk_scr, dv_scr, acc_scr, dq_scr, don_scr, q_scr, ds_scr, now_scr, dp_scr, top_scr, tops_scr, delta_scr, sum_scr, qs_scr, sems, qsem = refs
     x, own_core = at_ref[0], at_ref[1]
 
     def first_chunk(distance, other):
@@ -91,9 +94,10 @@
             qs_scr[:, i * ROWS : (i + 1) * ROWS] = jnp.broadcast_to(own[i : i + 1, :], (8, ROWS))
         low, high = jnp.min(own), jnp.max(own)
         n_steps = jnp.sum(jnp.where(is_first & (key_scales <= high), 1.0, 0.0)).astype(jnp.int32)
+        n_steps = jnp.maximum(n_steps, 2)
         n_full = jnp.sum(jnp.where(is_last & (key_scales <= low), 1.0, 0.0)).astype(jnp.int32)
 
-        def scores(masked, step, _):
+        def scores(masked, step):
             for half in range(KB // SLAB):
                 k = slab(step, half, 0)
                 if masked:
@@ -103,7 +107,6 @@
                     ]
                 for cols in COLS:
                     s = dot(k, q_scr[cols, :], NT)
-                    top = top_scr[:, cols]
                     for r in range(0, SLAB, GROUP):
                         tile = s[r : r + GROUP, :]
                         if masked:
@@ -119,32 +122,52 @@
                                 ],
                                 axis=1,
                             )
-                        s_scr[step, half * SLAB + r : half * SLAB + r + GROUP, cols] = tile
-                        top = jnp.maximum(top, fold(tile, jnp.max))
-                    top_scr[:, cols] = top
-            return 0
+                        s_scr[half * SLAB + r : half * SLAB + r + GROUP, cols] = tile
 
         q_scr[...] = rows(0)
         top_scr[...] = jnp.full_like(top_scr, NEG)
-        lax.fori_loop(0, n_full, functools.partial(scores, False), 0)
-        lax.fori_loop(n_full, n_steps, functools.partial(scores, True), 0)
-        top = jnp.max(top_scr[...], axis=0, keepdims=True) * (INV_ROOT * LOG2E)
-        top_scr[...] = jnp.broadcast_to(top, top_scr.shape)
         sum_scr[...] = jnp.zeros_like(sum_scr)
         acc_scr[...] = jnp.zeros_like(acc_scr)
 
-        def forward(step, _):
-            for half in range(KB // SLAB):
-                total = sum_scr[...]
-                for r in range(half * SLAB, (half + 1) * SLAB, GROUP):
-                    e = jnp.exp2(s_scr[step, r : r + GROUP, :] * (INV_ROOT * LOG2E) - top_scr[0:1, :])
-                    total = total + fold(e, jnp.sum)
-                    e_scr[step, r : r + GROUP, :] = e.astype(jnp.bfloat16)
-                sum_scr[...] = total
-                acc_scr[...] += dot(slab(step, half, 128), e_scr[step, half * SLAB : (half + 1) * SLAB, :], TN)
+        def weigh(step):
+            for half in range(KB // SLAB):
+                own = slice(half * SLAB, (half + 1) * SLAB)
+                acc_scr[...] += dot(slab(step, half, 128), now_scr[own, :], TN)
+
+        def exponentials(step):
+            top = fold(s_scr[0:GROUP, :], jnp.max)
+            for r in range(GROUP, KB, GROUP):
+                top = jnp.maximum(top, fold(s_scr[r : r + GROUP, :], jnp.max))
+            top = jnp.ceil(jnp.max(top, axis=0, keepdims=True) * (INV_ROOT * LOG2E))
+            top = jnp.maximum(top_scr[0:1, :], top)
+            drop = jnp.exp2(top_scr[0:1, :] - top)
+            top_scr[...] = jnp.broadcast_to(top, top_scr.shape)
+            tops_scr[step] = jnp.broadcast_to(top, top_scr.shape)
+            acc_scr[...] = acc_scr[...] * drop
+            total = sum_scr[...] * drop
+            for r in range(0, KB, GROUP):
+                e = jnp.exp2(s_scr[r : r + GROUP, :] * (INV_ROOT * LOG2E) - top)
+                total = total + fold(e, jnp.sum)
+                e = e.astype(jnp.bfloat16)
+                now_scr[r : r + GROUP, :] = e
+                e_scr[step, r : r + GROUP, :] = e
+            sum_scr[...] = total
+
+        def forward(masked, step, _):
+            weigh(step - 1)
+            exponentials(step)
+            scores(masked, step + 1)
             return 0
 
-        lax.fori_loop(0, n_steps, forward, 0)
+        scores(True, 0)
+        exponentials(0)
+        scores(True, 1)
+        n_open = jnp.maximum(n_full - 1, 1)
+        lax.fori_loop(1, n_open, functools.partial(forward, False), 0)
+        lax.fori_loop(n_open, n_steps - 1, functools.partial(forward, True), 0)
+        weigh(n_steps - 2)
+        exponentials(n_steps - 1)
+        weigh(n_steps - 1)
         inv = 1.0 / jnp.sum(sum_scr[...], axis=0, keepdims=True)
         attn = (acc_scr[...] * inv).T
         inv_rows = jnp.broadcast_to(inv, (HDIM, QB)).T
@@ -153,27 +176,33 @@
         do_n = (rows(128).astype(jnp.float32) * inv_rows).astype(jnp.bfloat16)
         don_scr[...] = do_n
         delta = jnp.sum(do_n.astype(jnp.float32) * attn, axis=1, keepdims=True)
-        top_scr[...] = jnp.broadcast_to(delta, (QB, HDIM)).T[0:8, :]
+        delta_scr[...] = jnp.broadcast_to(delta, (QB, HDIM)).T[0:8, :]
         dq_scr[...] = jnp.zeros_like(dq_scr)
 
-        def backward(step, _):
-            for half in range(KB // SLAB):
-                own = slice(half * SLAB, (half + 1) * SLAB)
+        def dprobs(step):
+            for half in range(KB // SLAB):
                 v = slab(step, half, 128)
                 for cols in COLS:
-                    dp = dot(v, don_scr[cols, :], NT)
-                    for r in range(0, SLAB, GROUP):
-                        e = e_scr[step, half * SLAB + r : half * SLAB + r + GROUP, cols].astype(jnp.float32)
-                        ds = e * (dp[r : r + GROUP, :] - top_scr[0:1, cols])
-                        ds_scr[half, r : r + GROUP, cols] = ds.astype(jnp.bfloat16)
-                dv = dot(e_scr[step, own, :], don_scr[...])
-                dk = dot(ds_scr[half], q_scr[...])
-                at_chunks = pl.ds(parts(step)[half], 2)
-                dv_scr[at_chunks] += dv.reshape(2, ROWS, HDIM)
-                dk_scr[at_chunks] += dk.reshape(2, ROWS, HDIM)
-                dq_scr[...] += dot(slab(step, half, 0), ds_scr[half], TN)
+                    dp_scr[half * SLAB : (half + 1) * SLAB, cols] = dot(v, don_scr[cols, :], NT)
+
+        def backward(step, _):
+            drop = jnp.exp2(tops_scr[step, 0:1, :] - top_scr[0:1, :])
+            delta = delta_scr[0:1, :]
+            for r in range(0, KB, GROUP):
+                e = e_scr[step, r : r + GROUP, :].astype(jnp.float32) * drop
+                now_scr[r : r + GROUP, :] = e.astype(jnp.bfloat16)
+                ds_scr[r : r + GROUP, :] = (e * (dp_scr[r : r + GROUP, :] - delta)).astype(jnp.bfloat16)
+            for half in range(KB // SLAB):
+                dv = dot(now_scr[half * SLAB : (half + 1) * SLAB, :], don_scr[...])
+                dv_scr[pl.ds(parts(step)[half], 2)] += dv.reshape(2, ROWS, HDIM)
+            dprobs(jnp.minimum(step + 1, STEPS - 1))
+            for half in range(KB // SLAB):
+                own = slice(half * SLAB, (half + 1) * SLAB)
+                dk_scr[pl.ds(parts(step)[half], 2)] += dot(ds_scr[own, :], q_scr[...]).reshape(2, ROWS, HDIM)
+                dq_scr[...] += dot(slab(step, half, 0), ds_scr[own, :], TN)
             return 0
 
+        dprobs(0)
         lax.fori_loop(0, n_steps, backward, 0)
         dq = (dq_scr[...] * INV_ROOT).T.astype(jnp.bfloat16)
         for i in range(QB // ROWS):
@@ -196,12 +225,12 @@
     return pl.pallas_call(
         attention_kernel,
         out_shape=outs,
-        in_specs=[pl.BlockSpec(memory_space=pltpu.SMEM)] + [vmem] * 11,
+        in_specs=[pl.BlockSpec(memory_space=pltpu.SMEM)] + [vmem] * (N_PIECES + 1),
         out_specs=(vmem,) * len(outs),
         scratch_shapes=[
             pltpu.VMEM((CHUNKS, 2 * ROWS + TILE, HDIM), jnp.bfloat16),
             pltpu.VMEM((ZS, 2 * ROWS + TILE, HDIM), jnp.bfloat16),
-            pltpu.VMEM((STEPS, KB, QB), jnp.float32),
+            pltpu.VMEM((KB, QB), jnp.float32),
             pltpu.VMEM((STEPS, KB, QB), jnp.bfloat16),
             pltpu.VMEM((CHUNKS, ROWS, HDIM), jnp.float32),
             pltpu.VMEM((CHUNKS, ROWS, HDIM), jnp.float32),
@@ -209,14 +238,18 @@
             pltpu.VMEM((HDIM, QB), jnp.float32),
             pltpu.VMEM((QB, HDIM), jnp.bfloat16),
             pltpu.VMEM((QB, HDIM), jnp.bfloat16),
-            pltpu.VMEM((KB // SLAB, SLAB, QB), jnp.bfloat16),
+            pltpu.VMEM((KB, QB), jnp.bfloat16),
+            pltpu.VMEM((KB, QB), jnp.bfloat16),
+            pltpu.VMEM((KB, QB), jnp.float32),
+            pltpu.VMEM((8, QB), jnp.float32),
+            pltpu.VMEM((STEPS, 8, QB), jnp.float32),
             pltpu.VMEM((8, QB), jnp.float32),
             pltpu.VMEM((8, QB), jnp.float32),
             pltpu.VMEM((8, QB), jnp.float32),
-            pltpu.SemaphoreType.DMA((10,)),
+            pltpu.SemaphoreType.DMA((N_PIECES,)),
             pltpu.SemaphoreType.DMA((1,)),
         ],
-        compiler_params=pltpu.CompilerParams(vmem_limit_bytes=42 * 1024 * 1024),
+        compiler_params=pltpu.CompilerParams(vmem_limit_bytes=38 * 1024 * 1024),
         cost_estimate=pl.CostEstimate(flops=8 * 10**9, bytes_accessed=10 * 2**20, transcendentals=5 * 10**6),
     )(at, *pieces, qd)
 
@@ -296,21 +329,19 @@
     far = add(grads[4], twin(grads[5]))
     far, *grads = lax.optimization_barrier((far, *grads))
     sums = {distance: add(grads[2 * distance], twin(grads[2 * distance + 1])) for distance in (3, 1, 0)}
-    ad, sums[1], sums[3] = lax.optimization_barrier((ad, sums[1], sums[3]))
-    ad_back = over_heads(ad)
     k, v = slice(0, ROWS), slice(ROWS, 2 * ROWS)
     key_left = left(sums[3][:, k])
-    key_right = right(add(sums[1][:, k], right(far[:, k])))
-    value_left = left(add(sums[3][:, v], left(far[:, v])))
+    key_relay = add(sums[1][:, k], right(far[:, k]))
+    value_relay = add(sums[3][:, v], left(far[:, v]))
+    ad, key_relay, value_relay = lax.optimization_barrier((ad, key_relay, value_relay))
+    ad_back = over_heads(ad)
+    key_right, value_left = right(key_relay), left(value_relay)
     value_right = right(sums[1][:, v])
     key_sum = add(sums[0][:, k], key_right, key_left)
     value_sum = add(sums[0][:, v], value_right, value_left)
-    value_sum, ad_back = lax.optimization_barrier((value_sum, ad_back))
-    return (
-        *unpack(swap(ad_back)),
-        *unpack(over_heads(key_sum)),
-        *unpack(over_heads(value_sum)),
-    )
+    sums = jnp.concatenate([key_sum, value_sum], axis=1)
+    sums, ad_back = lax.optimization_barrier((sums, ad_back))
+    return (*unpack(swap(ad_back)), *unpack(over_heads(sums)))
 
 
 def solution(mesh):

time: 166 us -> 156 us (0.940)
  starting transfers between devices: 61.3 us -> 55.3 us
  Pallas kernels: 38.7 us -> 35.8 us
  local copies, waits for them, and re-layouts: 5.48 us -> 3.35 us
    ppermute x5, waiting for transfers between devices: 7.86 us -> 20.6 us  [right(): return lax.ppermute(arr, 'x', [(i, (i + 1) % XS) for i in range(XS)])]
    ppermute x5, waiting for transfers between devices: 16.1 us -> 8.41 us  [left(): return lax.ppermute(arr, 'x', [(i, (i + XS - 1) % XS) for i in range(XS)])]
    all_to_all x5 -> x4, starting transfers between devices: 32.4 us -> 27.2 us  [over_heads(): return lax.all_to_all(arr, 'z', split_axis=0, concat_axis=0, tiled=True)]
    all_to_all x5 -> x4, waiting for transfers between devices: 28.9 us -> 24 us  [over_heads(): return lax.all_to_all(arr, 'z', split_axis=0, concat_axis=0, tiled=True)]
    ppermute x5, starting transfers between devices: 17.1 us -> 19.6 us  [left(): return lax.ppermute(arr, 'x', [(i, (i + XS - 1) % XS) for i in range(XS)])]
    ppermute x5, starting transfers between devices: 2.54 us -> 0.26 us  [right(): return lax.ppermute(arr, 'x', [(i, (i + 1) % XS) for i in range(XS)])]
    pallas_call x3 -> x2, Pallas kernels: 5.42 us -> 3.95 us  [unpack(): pl.pallas_call(unpack_kernel, out_shape=(rows,) * n, in_specs=[vmem], out...]
    unnamed x10 -> x8, local copies, waits for them, and re-layouts: 3.86 us -> 3.24 us
  transfers between devices with their start and end apart: 26 -> 25, of which waited for: 12 -> 11; matrix products, arithmetic and copies ran while one was open for 2% -> 1% of each run, Pallas kernels for 3% -> 3%
where the time goes in v3:
time: 156 us; the launch traced here: 154 us
  waiting for transfers between devices  56.7 us (36%)
  starting transfers between devices  55.3 us (35%)
  Pallas kernels  35.8 us (23%)
  local copies, waits for them, and re-layouts  3.35 us (2%)
  other arithmetic  1.83 us (1%)
    pallas_call x1, Pallas kernels, attention(): pl.pallas_call(attention_kernel, out_shape=outs, in_specs=[pl.BlockSpec(m...  28 us
    all_to_all x4, starting transfers between devices, over_heads(): return lax.all_to_all(arr, 'z', split_axis=0, concat_axis=0, tiled=True)  27.2 us
    all_to_all x4, waiting for transfers between devices, over_heads(): return lax.all_to_all(arr, 'z', split_axis=0, concat_axis=0, tiled=True)  24 us
    ppermute x5, waiting for transfers between devices, right(): return lax.ppermute(arr, 'x', [(i, (i + 1) % XS) for i in range(XS)])  20.6 us
    ppermute x5, starting transfers between devices, left(): return lax.ppermute(arr, 'x', [(i, (i + XS - 1) % XS) for i in range(XS)])  19.6 us
    ppermute x5, waiting for transfers between devices, left(): return lax.ppermute(arr, 'x', [(i, (i + XS - 1) % XS) for i in range(XS)])  8.41 us
    ppermute x2, starting transfers between devices, swap(): return lax.ppermute(arr, ('x', 'z'), pairs)  6.52 us
    pallas_call x2, Pallas kernels, unpack(): pl.pallas_call(unpack_kernel, out_shape=(rows,) * n, in_specs=[vmem], out...  3.95 us
  transfers between devices with their start and end apart: 25, of which 11 were waited for; matrix products, arithmetic and copies ran while one was open for 1% of the time, Pallas kernels for 3%

profile of v3, /device:TPU:16, one launch (start us, length us, event | category | flops | bytes accessed | tf_op | source)
XLA Modules:
  0.0 153.8 jit_solution(16380168321153318419)
XLA Ops:
  0.6 1.9 %shard_map.84 = bf16[8,272,128]{2,1,0:T(8,128)(2,1)} custom-call(bf16[1,128,1024]{2,1,0:T(8,128)(2,1)} %a_ref.2, bf16[1,128,1024]{2,1,0:T(8,128)(2,1)} %b_ref.2, s32[1,128]{1,0:T(1,128)} %scale_ref.3), custom_call_target="tpu_custom_call" | custom-call | tf_op jit(solution)/shard_map/pallas_call | solution.py:267
  2.6 8.5 %all-to-all-start = ((bf16[8,272,128]{2,1,0:T(8,128)(2,1)}), bf16[8,272,128]{2,1,0:T(8,128)(2,1)S(1)}, u32[]{:S(2)}, u32[]{:S(2)}) async-start(bf16[8,272,128]{2,1,0:T(8,128)(2,1)} %shard_map.84), calls=%async_computation | async-start | bytes 1114112 | tf_op jit(solution)/shard_map/all_to_all | solution.py:297
  11.0 2.0 %shard_map.85 = bf16[8,272,128]{2,1,0:T(8,128)(2,1)} custom-call(bf16[1,128,1024]{2,1,0:T(8,128)(2,1)} %a_ref.3, bf16[1,128,1024]{2,1,0:T(8,128)(2,1)} %b_ref.3, s32[1,128]{1,0:T(1,128)} %scale_ref.3), custom_call_target="tpu_custom_call" | custom-call | tf_op jit(solution)/shard_map/pallas_call | solution.py:267
  13.0 5.8 %collective-permute-start = (bf16[8,272,128]{2,1,0:T(8,128)(2,1)}, bf16[8,272,128]{2,1,0:T(8,128)(2,1)}, u32[]{:S(2)}, u32[]{:S(2)}) collective-permute-start(bf16[8,272,128]{2,1,0:T(8,128)(2,1)} %shard_map.85), channel_id=1, source_target_pairs={{0,0},{2,2},{4,4},{6,6},{8,56},{10,58},{12,60},{14,62},{16,16},{18... | collective-permute-start | bytes 1671176 | tf_op jit(solution)/shard_map/ppermute | solution.py:309
  18.8 10.4 %all-to-all-done.refs_0_ = bf16[8,272,128]{2,1,0:T(8,128)(2,1)S(1)} async-done(((bf16[8,272,128]{2,1,0:T(8,128)(2,1)}), bf16[8,272,128]{2,1,0:T(8,128)(2,1)S(1)}, u32[]{:S(2)}, u32[]{:S(2)}) %all-to-all-start) | async-done | bytes 557088 | tf_op jit(solution)/shard_map/all_to_all | solution.py:297
  29.2 2.8 %collective-permute-start.4 = (bf16[8,272,128]{2,1,0:T(8,128)(2,1)S(1)}, bf16[8,272,128]{2,1,0:T(8,128)(2,1)S(1)}, u32[]{:S(2)}, u32[]{:S(2)}) collective-permute-start(bf16[8,272,128]{2,1,0:T(8,128)(2,1)S(1)} %all-to-all-done.refs_0_), channel_id=1, source_target_pairs={{0,48},{16,0},{32,16},{48,32},{1,49},{17,1},{33,17},{49,33},{2,50}... | collective-permute-start | bytes 1671176 | tf_op jit(solution)/shard_map/ppermute | solution.py:303
  32.0 8.2 %all-to-all-start.1 = ((bf16[8,272,128]{2,1,0:T(8,128)(2,1)}), bf16[8,272,128]{2,1,0:T(8,128)(2,1)S(1)}, u32[]{:S(2)}, u32[]{:S(2)}) async-start(bf16[8,272,128]{2,1,0:T(8,128)(2,1)} %collective-permute-done), calls=%async_computation.1 | async-start | bytes 1114112 | tf_op jit(solution)/shard_map/all_to_all | solution.py:297
  40.2 3.9 %collective-permute-done.4.refs_4_ = bf16[8,272,128]{2,1,0:T(8,128)(2,1)S(1)} collective-permute-done((bf16[8,272,128]{2,1,0:T(8,128)(2,1)S(1)}, bf16[8,272,128]{2,1,0:T(8,128)(2,1)S(1)}, u32[]{:S(2)}, u32[]{:S(2)}) %collective-permute-start.4) | collective-permute-done | bytes 557088 | tf_op jit(solution)/shard_map/ppermute | solution.py:303
  44.1 3.8 %collective-permute-start.8 = (bf16[4,272,128]{2,1,0:T(8,128)(2,1)S(1)}, bf16[4,272,128]{2,1,0:T(8,128)(2,1)S(1)}, u32[]{:S(2)}, u32[]{:S(2)}) collective-permute-start(bf16[4,272,128]{2,1,0:T(8,128)(2,1)S(1)} %slice.41), channel_id=1, source_target_pairs={{0,48},{16,0},{32,16},{48,32},{1,49},{17,1},{33,17},{49,33},{2,50}... | collective-permute-start | bytes 835592 | tf_op jit(solution)/shard_map/ppermute | solution.py:303
  48.6 4.5 %collective-permute-done.8.refs_8_ = bf16[4,272,128]{2,1,0:T(8,128)(2,1)S(1)} collective-permute-done((bf16[4,272,128]{2,1,0:T(8,128)(2,1)S(1)}, bf16[4,272,128]{2,1,0:T(8,128)(2,1)S(1)}, u32[]{:S(2)}, u32[]{:S(2)}) %collective-permute-start.8) | collective-permute-done | bytes 278560 | tf_op jit(solution)/shard_map/ppermute | solution.py:303
  53.1 0.7 copy-done
  53.8 2.9 %collective-permute-done.6.refs_6_ = bf16[4,272,128]{2,1,0:T(8,128)(2,1)} collective-permute-done((bf16[4,272,128]{2,1,0:T(8,128)(2,1)S(1)}, bf16[4,272,128]{2,1,0:T(8,128)(2,1)}, u32[]{:S(2)}, u32[]{:S(2)}) %collective-permute-start.6) | collective-permute-done | bytes 278560 | tf_op jit(solution)/shard_map/ppermute | solution.py:300
  56.8 1.8 %collective-permute-done.7.refs_7_ = bf16[4,272,128]{2,1,0:T(8,128)(2,1)} collective-permute-done((bf16[4,272,128]{2,1,0:T(8,128)(2,1)}, bf16[4,272,128]{2,1,0:T(8,128)(2,1)}, u32[]{:S(2)}, u32[]{:S(2)}) %collective-permute-start.7) | collective-permute-done | bytes 278560 | tf_op jit(solution)/shard_map/ppermute | solution.py:312
  58.6 1.0 copy-done.1
  59.6 28.0 %shard_map.86 = (bf16[8,256,128]{2,1,0:T(8,128)(2,1)}, bf16[8,256,128]{2,1,0:T(8,128)(2,1)S(1)}, bf16[8,256,128]{2,1,0:T(8,128)(2,1)}, bf16[8,256,128]{2,1,0:T(8...) custom-call(s32[2]{0:T(128)S(1)} %pad_add_fusion.at_ref, ...), custom_call_target="tpu_custom_call" | custom-call | flops 8000000000 | bytes 10485760 | tf_op jit(solution)/shard_map/pallas_call | solution.py:225
  87.8 1.8 %collective-permute-done.10 = bf16[8,256,128]{2,1,0:T(8,128)(2,1)S(1)} collective-permute-done((bf16[8,256,128]{2,1,0:T(8,128)(2,1)S(1)}, bf16[8,256,128]{2,1,0:T(8,128)(2,1)S(1)}, u32[]{:S(2)}, u32[]{:S(2)}) %collective-permute-start.10) | collective-permute-done | bytes 524320 | tf_op jit(solution)/shard_map/ppermute | solution.py:312
  90.6 7.9 %collective-permute-start.15 = (bf16[8,128,128]{2,1,0:T(8,128)(2,1)S(1)}, bf16[8,128,128]{2,1,0:T(8,128)(2,1)S(1)}, u32[]{:S(2)}, u32[]{:S(2)}) collective-permute-start(bf16[8,128,128]{2,1,0:T(8,128)(2,1)S(1)} %get-tuple-element.60), channel_id=1, source_target_pairs={{0,48},{16,0},{32,16},{48,32},{1,49},{17,1},{33,17},{49,33},{2,50}... | collective-permute-start | bytes 786440 | tf_op jit(solution)/shard_map/ppermute | solution.py:303
  98.9 9.1 %collective-permute-done.13 = bf16[8,128,128]{2,1,0:T(8,128)(2,1)S(1)} collective-permute-done((bf16[8,128,128]{2,1,0:T(8,128)(2,1)S(1)}, bf16[8,128,128]{2,1,0:T(8,128)(2,1)S(1)}, u32[]{:S(2)}, u32[]{:S(2)}) %collective-permute-start.13) | collective-permute-done | bytes 262176 | tf_op jit(solution)/shard_map/ppermute | solution.py:300
  108.1 5.4 %all-to-all-start.2 = ((bf16[8,256,128]{2,1,0:T(8,128)(2,1)}), bf16[8,256,128]{2,1,0:T(8,128)(2,1)S(1)}, u32[]{:S(2)}, u32[]{:S(2)}) async-start(bf16[8,256,128]{2,1,0:T(8,128)(2,1)} %get-tuple-element.51), calls=%async_computation.2 | async-start | bytes 1048576 | tf_op jit(solution)/shard_map/all_to_all | solution.py:297
  113.7 3.2 %collective-permute-start.19 = (bf16[8,128,128]{2,1,0:T(8,128)(2,1)S(1)}, bf16[8,128,128]{2,1,0:T(8,128)(2,1)S(1)}, u32[]{:S(2)}, u32[]{:S(2)}) collective-permute-start(bf16[8,128,128]{2,1,0:T(8,128)(2,1)S(1)} %add_convert_fusion.6), channel_id=1, source_target_pairs={{0,48},{16,0},{32,16},{48,32},{1,49},{17,1},{33,17},{49,33},{2,50}... | collective-permute-start | bytes 786440 | tf_op jit(solution)/shard_map/ppermute | solution.py:303
  116.9 1.9 %collective-permute-start.17 = (bf16[8,128,128]{2,1,0:T(8,128)(2,1)S(1)}, bf16[8,128,128]{2,1,0:T(8,128)(2,1)S(1)}, u32[]{:S(2)}, u32[]{:S(2)}) collective-permute-start(bf16[8,128,128]{2,1,0:T(8,128)(2,1)S(1)} %slice.45), channel_id=1, source_target_pairs={{0,48},{16,0},{32,16},{48,32},{1,49},{17,1},{33,17},{49,33},{2,50}... | collective-permute-start | bytes 786440 | tf_op jit(solution)/shard_map/ppermute | solution.py:303
  119.0 5.0 %collective-permute-done.18 = bf16[8,128,128]{2,1,0:T(8,128)(2,1)S(1)} collective-permute-done((bf16[8,128,128]{2,1,0:T(8,128)(2,1)S(1)}, bf16[8,128,128]{2,1,0:T(8,128)(2,1)S(1)}, u32[]{:S(2)}, u32[]{:S(2)}) %collective-permute-start.18) | collective-permute-done | bytes 262176 | tf_op jit(solution)/shard_map/ppermute | solution.py:300
  124.1 3.5 %collective-permute-done.16 = bf16[8,128,128]{2,1,0:T(8,128)(2,1)S(1)} collective-permute-done((bf16[8,128,128]{2,1,0:T(8,128)(2,1)S(1)}, bf16[8,128,128]{2,1,0:T(8,128)(2,1)S(1)}, u32[]{:S(2)}, u32[]{:S(2)}) %collective-permute-start.16) | collective-permute-done | bytes 262176 | tf_op jit(solution)/shard_map/ppermute | solution.py:300
  127.8 0.8 pad_maximum_fusion
  128.7 1.7 %all-to-all-done.2 = bf16[8,256,128]{2,1,0:T(8,128)(2,1)S(1)} async-done(((bf16[8,256,128]{2,1,0:T(8,128)(2,1)}), bf16[8,256,128]{2,1,0:T(8,128)(2,1)S(1)}, u32[]{:S(2)}, u32[]{:S(2)}) %all-to-all-start.2) | async-done | bytes 524320 | tf_op jit(solution)/shard_map/all_to_all | solution.py:297
  130.4 5.2 %all-to-all-start.3 = ((bf16[8,256,128]{2,1,0:T(8,128)(2,1)}), bf16[8,256,128]{2,1,0:T(8,128)(2,1)S(1)}, u32[]{:S(2)}, u32[]{:S(2)}) async-start(bf16[8,256,128]{2,1,0:T(8,128)(2,1)} %pad_maximum_fusion), calls=%async_computation.3 | async-start | bytes 1048576 | tf_op jit(solution)/shard_map/all_to_all | solution.py:297
  135.6 0.7 collective-permute-start.20
  136.3 0.8 copy-done.3
  137.1 2.0 %shard_map.87 = (bf16[1,128,1024]{2,1,0:T(8,128)(2,1)}, bf16[1,128,1024]{2,1,0:T(8,128)(2,1)}) custom-call(bf16[8,256,128]{2,1,0:T(8,128)(2,1)} %copy-done.3), custom_call_target="tpu_custom_call" | custom-call | tf_op jit(solution)/shard_map/pallas_call | solution.py:285
  139.1 11.9 %all-to-all-done.3.in_ref = bf16[8,256,128]{2,1,0:T(8,128)(2,1)S(1)} async-done(((bf16[8,256,128]{2,1,0:T(8,128)(2,1)}), bf16[8,256,128]{2,1,0:T(8,128)(2,1)S(1)}, u32[]{:S(2)}, u32[]{:S(2)}) %all-to-all-start.3) | async-done | bytes 524320 | tf_op jit(solution)/shard_map/all_to_all | solution.py:297
  151.0 0.8 copy-done.2
  151.8 2.0 %shard_map.88 = (bf16[1,128,1024]{2,1,0:T(8,128)(2,1)}, bf16[1,128,1024]{2,1,0:T(8,128)(2,1)}) custom-call(bf16[8,256,128]{2,1,0:T(8,128)(2,1)} %copy-done.2), custom_call_target="tpu_custom_call" | custom-call | tf_op jit(solution)/shard_map/pallas_call | solution.py:285
  (45 shorter events, 3.1 us)
Async XLA Ops:
  2.6 26.7 %all-to-all-start = ((bf16[8,272,128]{2,1,0:T(8,128)(2,1)}), bf16[8,272,128]{2,1,0:T(8,128)(2,1)S(1)}, u32[]{:S(2)}, u32[]{:S(2)}) async-start(bf16[8,272,128]{2,1,0:T(8,128)(2,1)} %shard_map.84), calls=%async_computation | async-start | bytes 1114112 | tf_op jit(solution)/shard_map/all_to_all | solution.py:297
  13.0 5.8 %collective-permute-start = (bf16[8,272,128]{2,1,0:T(8,128)(2,1)}, bf16[8,272,128]{2,1,0:T(8,128)(2,1)}, u32[]{:S(2)}, u32[]{:S(2)}) collective-permute-start(bf16[8,272,128]{2,1,0:T(8,128)(2,1)} %shard_map.85), channel_id=1, source_target_pairs={{0,0},{2,2},{4,4},{6,6},{8,56},{10,58},{12,60},{14,62},{16,16},{18... | collective-permute-start | bytes 1671176 | tf_op jit(solution)/shard_map/ppermute | solution.py:309
  29.2 14.8 %collective-permute-start.4 = (bf16[8,272,128]{2,1,0:T(8,128)(2,1)S(1)}, bf16[8,272,128]{2,1,0:T(8,128)(2,1)S(1)}, u32[]{:S(2)}, u32[]{:S(2)}) collective-permute-start(bf16[8,272,128]{2,1,0:T(8,128)(2,1)S(1)} %all-to-all-done.refs_0_), channel_id=1, source_target_pairs={{0,48},{16,0},{32,16},{48,32},{1,49},{17,1},{33,17},{49,33},{2,50}... | collective-permute-start | bytes 1671176 | tf_op jit(solution)/shard_map/ppermute | solution.py:303
  32.0 15.9 %collective-permute-start.2 = (bf16[8,272,128]{2,1,0:T(8,128)(2,1)S(1)}, bf16[8,272,128]{2,1,0:T(8,128)(2,1)S(1)}, u32[]{:S(2)}, u32[]{:S(2)}) collective-permute-start(bf16[8,272,128]{2,1,0:T(8,128)(2,1)S(1)} %all-to-all-done.refs_0_), channel_id=1, source_target_pairs={{0,16},{16,32},{32,48},{48,0},{1,17},{17,33},{33,49},{49,1},{2,18}... | collective-permute-start | bytes 1671176 | tf_op jit(solution)/shard_map/ppermute | solution.py:300
  32.0 24.8 %all-to-all-start.1 = ((bf16[8,272,128]{2,1,0:T(8,128)(2,1)}), bf16[8,272,128]{2,1,0:T(8,128)(2,1)S(1)}, u32[]{:S(2)}, u32[]{:S(2)}) async-start(bf16[8,272,128]{2,1,0:T(8,128)(2,1)} %collective-permute-done), calls=%async_computation.1 | async-start | bytes 1114112 | tf_op jit(solution)/shard_map/all_to_all | solution.py:297
  40.2 16.6 %collective-permute-start.1 = (bf16[8,272,128]{2,1,0:T(8,128)(2,1)S(1)}, bf16[8,272,128]{2,1,0:T(8,128)(2,1)S(1)}, u32[]{:S(2)}, u32[]{:S(2)}) collective-permute-start(bf16[8,272,128]{2,1,0:T(8,128)(2,1)S(1)} %all-to-all-done.refs_0_), channel_id=1, source_target_pairs={{0,1},{1,0},{2,3},{3,2},{4,5},{5,4},{6,7},{7,6},{8,9},{9,8},{10,11... | collective-permute-start | bytes 1671176 | tf_op jit(solution)/shard_map/ppermute | solution.py:312
  44.1 9.0 %collective-permute-start.8 = (bf16[4,272,128]{2,1,0:T(8,128)(2,1)S(1)}, bf16[4,272,128]{2,1,0:T(8,128)(2,1)S(1)}, u32[]{:S(2)}, u32[]{:S(2)}) collective-permute-start(bf16[4,272,128]{2,1,0:T(8,128)(2,1)S(1)} %slice.41), channel_id=1, source_target_pairs={{0,48},{16,0},{32,16},{48,32},{1,49},{17,1},{33,17},{49,33},{2,50}... | collective-permute-start | bytes 835592 | tf_op jit(solution)/shard_map/ppermute | solution.py:303
  47.9 8.8 %collective-permute-start.6 = (bf16[4,272,128]{2,1,0:T(8,128)(2,1)S(1)}, bf16[4,272,128]{2,1,0:T(8,128)(2,1)}, u32[]{:S(2)}, u32[]{:S(2)}) collective-permute-start(bf16[4,272,128]{2,1,0:T(8,128)(2,1)S(1)} %slice.40), channel_id=1, source_target_pairs={{0,16},{16,32},{32,48},{48,0},{1,17},{17,33},{33,49},{49,1},{2,18}... | collective-permute-start | bytes 835592 | tf_op jit(solution)/shard_map/ppermute | solution.py:300
  48.0 10.7 %collective-permute-start.5 = (bf16[8,272,128]{2,1,0:T(8,128)(2,1)S(1)}, bf16[8,272,128]{2,1,0:T(8,128)(2,1)}, u32[]{:S(2)}, u32[]{:S(2)}) collective-permute-start(bf16[8,272,128]{2,1,0:T(8,128)(2,1)S(1)} %collective-permute-done.4.refs_4_), channel_id=1, source_target_pairs={{0,1},{1,0},{2,3},{3,2},{4,5},{5,4},{6,7},{7,6},{8,9},{9,8},{10,11... | collective-permute-start | bytes 1671176 | tf_op jit(solution)/shard_map/ppermute | solution.py:312
  48.1 10.6 %collective-permute-start.3 = (bf16[8,272,128]{2,1,0:T(8,128)(2,1)S(1)}, bf16[8,272,128]{2,1,0:T(8,128)(2,1)}, u32[]{:S(2)}, u32[]{:S(2)}) collective-permute-start(bf16[8,272,128]{2,1,0:T(8,128)(2,1)S(1)} %collective-permute-done.2.refs_2_), channel_id=1, source_target_pairs={{0,1},{1,0},{2,3},{3,2},{4,5},{5,4},{6,7},{7,6},{8,9},{9,8},{10,11... | collective-permute-start | bytes 1671176 | tf_op jit(solution)/shard_map/ppermute | solution.py:312
  53.1 3.7 %collective-permute-start.9 = (bf16[4,272,128]{2,1,0:T(8,128)(2,1)S(1)}, bf16[4,272,128]{2,1,0:T(8,128)(2,1)}, u32[]{:S(2)}, u32[]{:S(2)}) collective-permute-start(bf16[4,272,128]{2,1,0:T(8,128)(2,1)S(1)} %collective-permute-done.8.refs_8_), channel_id=1, source_target_pairs={{0,1},{1,0},{2,3},{3,2},{4,5},{5,4},{6,7},{7,6},{8,9},{9,8},{10,11... | collective-permute-start | bytes 835592 | tf_op jit(solution)/shard_map/ppermute | solution.py:312
  53.1 0.7 copy-start
  56.7 1.9 %collective-permute-start.7 = (bf16[4,272,128]{2,1,0:T(8,128)(2,1)}, bf16[4,272,128]{2,1,0:T(8,128)(2,1)}, u32[]{:S(2)}, u32[]{:S(2)}) collective-permute-start(bf16[4,272,128]{2,1,0:T(8,128)(2,1)} %collective-permute-done.6.refs_6_), channel_id=1, source_target_pairs={{0,1},{1,0},{2,3},{3,2},{4,5},{5,4},{6,7},{7,6},{8,9},{9,8},{10,11... | collective-permute-start | bytes 835592 | tf_op jit(solution)/shard_map/ppermute | solution.py:312
  58.6 1.0 copy-start.1
  87.6 2.0 %collective-permute-start.10 = (bf16[8,256,128]{2,1,0:T(8,128)(2,1)S(1)}, bf16[8,256,128]{2,1,0:T(8,128)(2,1)S(1)}, u32[]{:S(2)}, u32[]{:S(2)}) collective-permute-start(bf16[8,256,128]{2,1,0:T(8,128)(2,1)S(1)} %get-tuple-element.34), channel_id=1, source_target_pairs={{0,1},{1,0},{2,3},{3,2},{4,5},{5,4},{6,7},{7,6},{8,9},{9,8},{10,11... | collective-permute-start | bytes 1572872 | tf_op jit(solution)/shard_map/ppermute | solution.py:312
  89.7 8.8 %collective-permute-start.12 = (bf16[8,256,128]{2,1,0:T(8,128)(2,1)S(1)}, bf16[8,256,128]{2,1,0:T(8,128)(2,1)S(1)}, u32[]{:S(2)}, u32[]{:S(2)}) collective-permute-start(bf16[8,256,128]{2,1,0:T(8,128)(2,1)S(1)} %get-tuple-element.45), channel_id=1, source_target_pairs={{0,1},{1,0},{2,3},{3,2},{4,5},{5,4},{6,7},{7,6},{8,9},{9,8},{10,11... | collective-permute-start | bytes 1572872 | tf_op jit(solution)/shard_map/ppermute | solution.py:312
  90.2 8.5 %collective-permute-start.14 = (bf16[8,256,128]{2,1,0:T(8,128)(2,1)S(1)}, bf16[8,256,128]{2,1,0:T(8,128)(2,1)S(1)}, u32[]{:S(2)}, u32[]{:S(2)}) collective-permute-start(bf16[8,256,128]{2,1,0:T(8,128)(2,1)S(1)} %get-tuple-element.48), channel_id=1, source_target_pairs={{0,1},{1,0},{2,3},{3,2},{4,5},{5,4},{6,7},{7,6},{8,9},{9,8},{10,11... | collective-permute-start | bytes 1572872 | tf_op jit(solution)/shard_map/ppermute | solution.py:312
  90.6 17.5 %collective-permute-start.15 = (bf16[8,128,128]{2,1,0:T(8,128)(2,1)S(1)}, bf16[8,128,128]{2,1,0:T(8,128)(2,1)S(1)}, u32[]{:S(2)}, u32[]{:S(2)}) collective-permute-start(bf16[8,128,128]{2,1,0:T(8,128)(2,1)S(1)} %get-tuple-element.60), channel_id=1, source_target_pairs={{0,48},{16,0},{32,16},{48,32},{1,49},{17,1},{33,17},{49,33},{2,50}... | collective-permute-start | bytes 786440 | tf_op jit(solution)/shard_map/ppermute | solution.py:303
  98.5 9.5 %collective-permute-start.13 = (bf16[8,128,128]{2,1,0:T(8,128)(2,1)S(1)}, bf16[8,128,128]{2,1,0:T(8,128)(2,1)S(1)}, u32[]{:S(2)}, u32[]{:S(2)}) collective-permute-start(bf16[8,128,128]{2,1,0:T(8,128)(2,1)S(1)} %get-tuple-element.61), channel_id=1, source_target_pairs={{0,16},{16,32},{32,48},{48,0},{1,17},{17,33},{33,49},{49,1},{2,18}... | collective-permute-start | bytes 786440 | tf_op jit(solution)/shard_map/ppermute | solution.py:300
  98.5 20.4 %collective-permute-start.11 = (bf16[8,256,128]{2,1,0:T(8,128)(2,1)}, bf16[8,256,128]{2,1,0:T(8,128)(2,1)S(1)}, u32[]{:S(2)}, u32[]{:S(2)}) collective-permute-start(bf16[8,256,128]{2,1,0:T(8,128)(2,1)} %get-tuple-element.42), channel_id=1, source_target_pairs={{0,1},{1,0},{2,3},{3,2},{4,5},{5,4},{6,7},{7,6},{8,9},{9,8},{10,11... | collective-permute-start | bytes 1572872 | tf_op jit(solution)/shard_map/ppermute | solution.py:312
  108.1 22.2 %all-to-all-start.2 = ((bf16[8,256,128]{2,1,0:T(8,128)(2,1)}), bf16[8,256,128]{2,1,0:T(8,128)(2,1)S(1)}, u32[]{:S(2)}, u32[]{:S(2)}) async-start(bf16[8,256,128]{2,1,0:T(8,128)(2,1)} %get-tuple-element.51), calls=%async_computation.2 | async-start | bytes 1048576 | tf_op jit(solution)/shard_map/all_to_all | solution.py:297
  113.5 10.5 %collective-permute-start.18 = (bf16[8,128,128]{2,1,0:T(8,128)(2,1)S(1)}, bf16[8,128,128]{2,1,0:T(8,128)(2,1)S(1)}, u32[]{:S(2)}, u32[]{:S(2)}) collective-permute-start(bf16[8,128,128]{2,1,0:T(8,128)(2,1)S(1)} %slice.47), channel_id=1, source_target_pairs={{0,16},{16,32},{32,48},{48,0},{1,17},{17,33},{33,49},{49,1},{2,18}... | collective-permute-start | bytes 786440 | tf_op jit(solution)/shard_map/ppermute | solution.py:300
  113.6 14.0 %collective-permute-start.16 = (bf16[8,128,128]{2,1,0:T(8,128)(2,1)S(1)}, bf16[8,128,128]{2,1,0:T(8,128)(2,1)S(1)}, u32[]{:S(2)}, u32[]{:S(2)}) collective-permute-start(bf16[8,128,128]{2,1,0:T(8,128)(2,1)S(1)} %add_convert_fusion.7), channel_id=1, source_target_pairs={{0,16},{16,32},{32,48},{48,0},{1,17},{17,33},{33,49},{49,1},{2,18}... | collective-permute-start | bytes 786440 | tf_op jit(solution)/shard_map/ppermute | solution.py:300
  113.7 13.9 %collective-permute-start.19 = (bf16[8,128,128]{2,1,0:T(8,128)(2,1)S(1)}, bf16[8,128,128]{2,1,0:T(8,128)(2,1)S(1)}, u32[]{:S(2)}, u32[]{:S(2)}) collective-permute-start(bf16[8,128,128]{2,1,0:T(8,128)(2,1)S(1)} %add_convert_fusion.6), channel_id=1, source_target_pairs={{0,48},{16,0},{32,16},{48,32},{1,49},{17,1},{33,17},{49,33},{2,50}... | collective-permute-start | bytes 786440 | tf_op jit(solution)/shard_map/ppermute | solution.py:303
  116.9 10.7 %collective-permute-start.17 = (bf16[8,128,128]{2,1,0:T(8,128)(2,1)S(1)}, bf16[8,128,128]{2,1,0:T(8,128)(2,1)S(1)}, u32[]{:S(2)}, u32[]{:S(2)}) collective-permute-start(bf16[8,128,128]{2,1,0:T(8,128)(2,1)S(1)} %slice.45), channel_id=1, source_target_pairs={{0,48},{16,0},{32,16},{48,32},{1,49},{17,1},{33,17},{49,33},{2,50}... | collective-permute-start | bytes 786440 | tf_op jit(solution)/shard_map/ppermute | solution.py:303
  130.4 20.6 %all-to-all-start.3 = ((bf16[8,256,128]{2,1,0:T(8,128)(2,1)}), bf16[8,256,128]{2,1,0:T(8,128)(2,1)S(1)}, u32[]{:S(2)}, u32[]{:S(2)}) async-start(bf16[8,256,128]{2,1,0:T(8,128)(2,1)} %pad_maximum_fusion), calls=%async_computation.3 | async-start | bytes 1048576 | tf_op jit(solution)/shard_map/all_to_all | solution.py:297
  135.6 0.7 collective-permute-start.20
  136.3 0.8 copy-start.3
  151.0 0.8 copy-start.2

commit v4 on v3

--- a/solution.py
+++ b/solution.py
@@ -31,7 +31,9 @@
     return lax.dot_general(a, b, dims, preferred_element_type=jnp.float32)
 
 
-PIECES = ((0, 0, 8), (3, 0, 8), (1, 0, 8), (2, 0, 4), (2, 4, 4))
+PIECES = (
+    (0, 0, 8), (3, 0, 4), (3, 4, 4), (1, 0, 4), (1, 4, 4), (2, 0, 4), (2, 4, 4)
+)
 N_PIECES = 2 * len(PIECES)
 
 
@@ -39,7 +41,7 @@
     pieces, qd_in, ad_ref, grads, refs = (
         refs[:N_PIECES], refs[N_PIECES], refs[N_PIECES + 1], refs[N_PIECES + 2 : N_PIECES + 10], refs[N_PIECES + 10 :],
     )
-    kvs_ref, qd_ref, s_scr, e_scr, dk_scr, dv_scr, acc_scr, dq_scr, don_scr, q_scr, ds_scr, now_scr, dp_scr, top_scr, tops_scr, delta_scr, sum_scr, qs_scr, sems, qsem = refs
+    kvs_ref, qd_ref, s_scr, e_scr, dk_scr, dv_scr, acc_scr, dq_scr, don_scr, dont_scr, q_scr, qt_scr, ds_scr, now_scr, dp_scr, top_scr, tops_scr, delta_scr, sum_scr, qs_scr, sems, qsem = refs
     x, own_core = at_ref[0], at_ref[1]
 
     def first_chunk(distance, other):
@@ -125,6 +127,7 @@
                         s_scr[half * SLAB + r : half * SLAB + r + GROUP, cols] = tile
 
         q_scr[...] = rows(0)
+        qt_scr[...] = rows(0).astype(jnp.float32).T.astype(jnp.bfloat16)
         top_scr[...] = jnp.full_like(top_scr, NEG)
         sum_scr[...] = jnp.zeros_like(sum_scr)
         acc_scr[...] = jnp.zeros_like(acc_scr)
@@ -175,6 +178,7 @@
             ad_ref[first + i, 0:128, :] = attn[i * ROWS : (i + 1) * ROWS, :].astype(jnp.bfloat16)
         do_n = (rows(128).astype(jnp.float32) * inv_rows).astype(jnp.bfloat16)
         don_scr[...] = do_n
+        dont_scr[...] = do_n.astype(jnp.float32).T.astype(jnp.bfloat16)
         delta = jnp.sum(do_n.astype(jnp.float32) * attn, axis=1, keepdims=True)
         delta_scr[...] = jnp.broadcast_to(delta, (QB, HDIM)).T[0:8, :]
         dq_scr[...] = jnp.zeros_like(dq_scr)
@@ -193,12 +197,15 @@
                 now_scr[r : r + GROUP, :] = e.astype(jnp.bfloat16)
                 ds_scr[r : r + GROUP, :] = (e * (dp_scr[r : r + GROUP, :] - delta)).astype(jnp.bfloat16)
             for half in range(KB // SLAB):
-                dv = dot(now_scr[half * SLAB : (half + 1) * SLAB, :], don_scr[...])
-                dv_scr[pl.ds(parts(step)[half], 2)] += dv.reshape(2, ROWS, HDIM)
+                dv = dot(dont_scr[...], now_scr[half * SLAB : (half + 1) * SLAB, :], NT)
+                for i in range(SLAB // ROWS):
+                    dv_scr[parts(step)[half] + i] += dv[:, i * ROWS : (i + 1) * ROWS]
             dprobs(jnp.minimum(step + 1, STEPS - 1))
             for half in range(KB // SLAB):
                 own = slice(half * SLAB, (half + 1) * SLAB)
-                dk_scr[pl.ds(parts(step)[half], 2)] += dot(ds_scr[own, :], q_scr[...]).reshape(2, ROWS, HDIM)
+                dk = dot(qt_scr[...], ds_scr[own, :], NT)
+                for i in range(SLAB // ROWS):
+                    dk_scr[parts(step)[half] + i] += dk[:, i * ROWS : (i + 1) * ROWS]
                 dq_scr[...] += dot(slab(step, half, 0), ds_scr[own, :], TN)
             return 0
 
@@ -237,7 +244,9 @@
             pltpu.VMEM((HDIM, QB), jnp.float32),
             pltpu.VMEM((HDIM, QB), jnp.float32),
             pltpu.VMEM((QB, HDIM), jnp.bfloat16),
+            pltpu.VMEM((HDIM, QB), jnp.bfloat16),
             pltpu.VMEM((QB, HDIM), jnp.bfloat16),
+            pltpu.VMEM((HDIM, QB), jnp.bfloat16),
             pltpu.VMEM((KB, QB), jnp.bfloat16),
             pltpu.VMEM((KB, QB), jnp.bfloat16),
             pltpu.VMEM((KB, QB), jnp.float32),
@@ -272,17 +281,21 @@
     )(a, b, scale_ids)
 
 
-def unpack_kernel(in_ref, *outs):
+def unpack_kernel(in_ref, *outs, turned):
     for h in range(HEADS):
         for i, out in enumerate(outs):
-            out[0, :, h * HDIM : (h + 1) * HDIM] = in_ref[h, i * ROWS : (i + 1) * ROWS, :]
-
-
-def unpack(arr):
+            tile = in_ref[h, i * ROWS : (i + 1) * ROWS, :]
+            if turned:
+                tile = tile.astype(jnp.float32).T.astype(jnp.bfloat16)
+            out[0, :, h * HDIM : (h + 1) * HDIM] = tile
+
+
+def unpack(arr, turned=False):
     vmem = pl.BlockSpec(memory_space=pltpu.VMEM)
     rows = jax.ShapeDtypeStruct((1, ROWS, HEADS * HDIM), jnp.bfloat16)
     n = arr.shape[1] // ROWS
-    return pl.pallas_call(unpack_kernel, out_shape=(rows,) * n, in_specs=[vmem], out_specs=(vmem,) * n)(arr)
+    kernel = functools.partial(unpack_kernel, turned=turned)
+    return pl.pallas_call(kernel, out_shape=(rows,) * n, in_specs=[vmem], out_specs=(vmem,) * n)(arr)
 
 
 def add(*arrs):
@@ -317,31 +330,33 @@
     kvs = over_heads(pack(key, value, scale_ids))
     swapped = swap(pack(query, grad_attn, scale_ids))
     kvs, swapped = lax.optimization_barrier((kvs, swapped))
-    from_left, from_right = right(kvs), left(kvs)
+    kvs_twin = twin(kvs)
+    low, high = kvs[:half], kvs[half:]
+    left_low, right_high = right(low), left(high)
+    left_high, right_low = right(high), left(low)
+    swapped, kvs_twin = lax.optimization_barrier((swapped, kvs_twin))
     qd = over_heads(swapped)
-    opposite_a, opposite_b = right(from_left[:half]), left(from_right[half:])
-    pieces = []
-    for piece in (kvs, from_left, from_right, opposite_a, opposite_b):
+    opposite_low, opposite_high = right(left_low), left(right_high)
+    pieces = [kvs, kvs_twin]
+    for piece in (left_low, left_high, right_low, right_high, opposite_low, opposite_high):
         pieces += [piece, twin(piece)]
 
     ad, *grads = attention(at, pieces, qd)
 
+    k, v = slice(0, ROWS), slice(ROWS, 2 * ROWS)
     far = add(grads[4], twin(grads[5]))
     far, *grads = lax.optimization_barrier((far, *grads))
     sums = {distance: add(grads[2 * distance], twin(grads[2 * distance + 1])) for distance in (3, 1, 0)}
-    k, v = slice(0, ROWS), slice(ROWS, 2 * ROWS)
-    key_left = left(sums[3][:, k])
-    key_relay = add(sums[1][:, k], right(far[:, k]))
-    value_relay = add(sums[3][:, v], left(far[:, v]))
-    ad, key_relay, value_relay = lax.optimization_barrier((ad, key_relay, value_relay))
+    key_left, value_right = left(sums[3][:, k]), right(sums[1][:, v])
+    key_right = right(add(sums[1][:, k], right(far[:, k])))
+    value_left = left(add(sums[3][:, v], left(far[:, v])))
+    ad, key_left, value_right = lax.optimization_barrier((ad, key_left, value_right))
     ad_back = over_heads(ad)
-    key_right, value_left = right(key_relay), left(value_relay)
-    value_right = right(sums[1][:, v])
     key_sum = add(sums[0][:, k], key_right, key_left)
     value_sum = add(sums[0][:, v], value_right, value_left)
     sums = jnp.concatenate([key_sum, value_sum], axis=1)
     sums, ad_back = lax.optimization_barrier((sums, ad_back))
-    return (*unpack(swap(ad_back)), *unpack(over_heads(sums)))
+    return (*unpack(swap(ad_back)), *unpack(over_heads(sums), turned=True))
 
 
 def solution(mesh):

time: 156 us -> 167 us (1.071)
  the two profiles are of different devices: /device:TPU:16 before, /device:TPU:152 now
where the time goes in v4:
time: 167 us; the launch traced here: 166 us
  starting transfers between devices  66.6 us (40%)
  waiting for transfers between devices  51.1 us (31%)
  Pallas kernels  35.6 us (21%)
  local copies, waits for them, and re-layouts  8.89 us (5%)
  other arithmetic  3.33 us (2%)
    all_to_all x4, starting transfers between devices, over_heads(): return lax.all_to_all(arr, 'z', split_axis=0, concat_axis=0, tiled=True)  30.4 us
    pallas_call x1, Pallas kernels, attention(): pl.pallas_call(attention_kernel, out_shape=outs, in_specs=[pl.BlockSpec(m...  27.7 us
    ppermute x2, waiting for transfers between devices, swap(): return lax.ppermute(arr, ('x', 'z'), pairs)  23.3 us
    ppermute x6, starting transfers between devices, left(): return lax.ppermute(arr, 'x', [(i, (i + XS - 1) % XS) for i in range(XS)])  17.5 us
    ppermute x6, waiting for transfers between devices, left(): return lax.ppermute(arr, 'x', [(i, (i + XS - 1) % XS) for i in range(XS)])  12 us
    ppermute x6, waiting for transfers between devices, right(): return lax.ppermute(arr, 'x', [(i, (i + 1) % XS) for i in range(XS)])  9.2 us
    ppermute x6, starting transfers between devices, right(): return lax.ppermute(arr, 'x', [(i, (i + 1) % XS) for i in range(XS)])  8.71 us
    ppermute x2, starting transfers between devices, swap(): return lax.ppermute(arr, ('x', 'z'), pairs)  8.1 us
  transfers between devices with their start and end apart: 29, of which 14 were waited for; matrix products, arithmetic and copies ran while one was open for 2% of the time, Pallas kernels for 2%

profile of v4, /device:TPU:152, one launch (start us, length us, event | category | flops | bytes accessed | tf_op | source)
XLA Modules:
  0.0 166.3 jit_solution(13503831830904355097)
XLA Ops:
  0.6 1.9 %shard_map.84 = bf16[8,272,128]{2,1,0:T(8,128)(2,1)} custom-call(bf16[1,128,1024]{2,1,0:T(8,128)(2,1)} %a_ref.2, bf16[1,128,1024]{2,1,0:T(8,128)(2,1)} %b_ref.2, s32[1,128]{1,0:T(1,128)} %scale_ref.3), custom_call_target="tpu_custom_call" | custom-call | tf_op jit(solution)/shard_map/pallas_call | solution.py:276
  2.6 7.2 %all-to-all-start = ((bf16[8,272,128]{2,1,0:T(8,128)(2,1)}), bf16[8,272,128]{2,1,0:T(8,128)(2,1)S(1)}, u32[]{:S(2)}, u32[]{:S(2)}) async-start(bf16[8,272,128]{2,1,0:T(8,128)(2,1)} %shard_map.84), calls=%async_computation | async-start | bytes 1114112 | tf_op jit(solution)/shard_map/all_to_all | solution.py:310
  9.8 1.9 %shard_map.85 = bf16[8,272,128]{2,1,0:T(8,128)(2,1)} custom-call(bf16[1,128,1024]{2,1,0:T(8,128)(2,1)} %a_ref.3, bf16[1,128,1024]{2,1,0:T(8,128)(2,1)} %b_ref.3, s32[1,128]{1,0:T(1,128)} %scale_ref.3), custom_call_target="tpu_custom_call" | custom-call | tf_op jit(solution)/shard_map/pallas_call | solution.py:276
  11.7 4.7 %collective-permute-start = (bf16[8,272,128]{2,1,0:T(8,128)(2,1)}, bf16[8,272,128]{2,1,0:T(8,128)(2,1)}, u32[]{:S(2)}, u32[]{:S(2)}) collective-permute-start(bf16[8,272,128]{2,1,0:T(8,128)(2,1)} %shard_map.85), channel_id=1, source_target_pairs={{0,0},{2,2},{4,4},{6,6},{8,56},{10,58},{12,60},{14,62},{16,16},{18... | collective-permute-start | bytes 1671176 | tf_op jit(solution)/shard_map/ppermute | solution.py:322
  16.4 12.6 %collective-permute-done = bf16[8,272,128]{2,1,0:T(8,128)(2,1)} collective-permute-done((bf16[8,272,128]{2,1,0:T(8,128)(2,1)}, bf16[8,272,128]{2,1,0:T(8,128)(2,1)}, u32[]{:S(2)}, u32[]{:S(2)}) %collective-permute-start) | collective-permute-done | bytes 557088 | tf_op jit(solution)/shard_map/ppermute | solution.py:322
  28.9 2.0 %collective-permute-done.1.refs_1_ = bf16[8,272,128]{2,1,0:T(8,128)(2,1)S(1)} collective-permute-done((bf16[8,272,128]{2,1,0:T(8,128)(2,1)S(1)}, bf16[8,272,128]{2,1,0:T(8,128)(2,1)S(1)}, u32[]{:S(2)}, u32[]{:S(2)}) %collective-permute-start.1) | collective-permute-done | bytes 557088 | tf_op jit(solution)/shard_map/ppermute | solution.py:325
  30.9 7.2 %all-to-all-start.1 = ((bf16[8,272,128]{2,1,0:T(8,128)(2,1)}), bf16[8,272,128]{2,1,0:T(8,128)(2,1)S(1)}, u32[]{:S(2)}, u32[]{:S(2)}) async-start(bf16[8,272,128]{2,1,0:T(8,128)(2,1)} %collective-permute-done), calls=%async_computation.1 | async-start | bytes 1114112 | tf_op jit(solution)/shard_map/all_to_all | solution.py:310
  38.1 2.8 %collective-permute-start.8 = (bf16[4,272,128]{2,1,0:T(8,128)(2,1)S(1)}, bf16[4,272,128]{2,1,0:T(8,128)(2,1)S(1)}, u32[]{:S(2)}, u32[]{:S(2)}) collective-permute-start(bf16[4,272,128]{2,1,0:T(8,128)(2,1)S(1)} %get-tuple-element.62), channel_id=1, source_target_pairs={{0,48},{16,0},{32,16},{48,32},{1,49},{17,1},{33,17},{49,33},{2,50}... | collective-permute-start | bytes 835592 | tf_op jit(solution)/shard_map/ppermute | solution.py:316
  41.0 3.3 %collective-permute-start.6 = (bf16[4,272,128]{2,1,0:T(8,128)(2,1)S(1)}, bf16[4,272,128]{2,1,0:T(8,128)(2,1)S(1)}, u32[]{:S(2)}, u32[]{:S(2)}) collective-permute-start(bf16[4,272,128]{2,1,0:T(8,128)(2,1)S(1)} %get-tuple-element.63), channel_id=1, source_target_pairs={{0,48},{16,0},{32,16},{48,32},{1,49},{17,1},{33,17},{49,33},{2,50}... | collective-permute-start | bytes 835592 | tf_op jit(solution)/shard_map/ppermute | solution.py:316
  44.2 3.8 %collective-permute-done.8.refs_8_ = bf16[4,272,128]{2,1,0:T(8,128)(2,1)S(1)} collective-permute-done((bf16[4,272,128]{2,1,0:T(8,128)(2,1)S(1)}, bf16[4,272,128]{2,1,0:T(8,128)(2,1)S(1)}, u32[]{:S(2)}, u32[]{:S(2)}) %collective-permute-start.8) | collective-permute-done | bytes 278560 | tf_op jit(solution)/shard_map/ppermute | solution.py:316
  48.1 3.7 %collective-permute-start.12 = (bf16[4,272,128]{2,1,0:T(8,128)(2,1)S(1)}, bf16[4,272,128]{2,1,0:T(8,128)(2,1)S(1)}, u32[]{:S(2)}, u32[]{:S(2)}) collective-permute-start(bf16[4,272,128]{2,1,0:T(8,128)(2,1)S(1)} %collective-permute-done.8.refs_8_), channel_id=1, source_target_pairs={{0,48},{16,0},{32,16},{48,32},{1,49},{17,1},{33,17},{49,33},{2,50}... | collective-permute-start | bytes 835592 | tf_op jit(solution)/shard_map/ppermute | solution.py:316
  51.8 4.2 %collective-permute-done.4.refs_4_ = bf16[4,272,128]{2,1,0:T(8,128)(2,1)S(1)} collective-permute-done((bf16[4,272,128]{2,1,0:T(8,128)(2,1)S(1)}, bf16[4,272,128]{2,1,0:T(8,128)(2,1)S(1)}, u32[]{:S(2)}, u32[]{:S(2)}) %collective-permute-start.4) | collective-permute-done | bytes 278560 | tf_op jit(solution)/shard_map/ppermute | solution.py:313
  56.5 2.0 %collective-permute-done.12.refs_12_ = bf16[4,272,128]{2,1,0:T(8,128)(2,1)S(1)} collective-permute-done((bf16[4,272,128]{2,1,0:T(8,128)(2,1)S(1)}, bf16[4,272,128]{2,1,0:T(8,128)(2,1)S(1)}, u32[]{:S(2)}, u32[]{:S(2)}) %collective-permute-start.12) | collective-permute-done | bytes 278560 | tf_op jit(solution)/shard_map/ppermute | solution.py:316
  62.8 1.3 collective-permute-done.11.refs_11_
  67.6 27.7 %shard_map.86 = (bf16[8,256,128]{2,1,0:T(8,128)(2,1)}, bf16[8,256,128]{2,1,0:T(8,128)(2,1)S(1)}, bf16[8,256,128]{2,1,0:T(8,128)(2,1)S(1)}, bf16[8,256,128]{2,1,0...) custom-call(s32[2]{0:T(128)S(1)} %copy-done.6, ...), custom_call_target="tpu_custom_call" | custom-call | flops 8000000000 | bytes 10485760 | tf_op jit(solution)/shard_map/pallas_call | solution.py:232
  95.6 1.8 %collective-permute-done.14 = bf16[8,256,128]{2,1,0:T(8,128)(2,1)S(1)} collective-permute-done((bf16[8,256,128]{2,1,0:T(8,128)(2,1)S(1)}, bf16[8,256,128]{2,1,0:T(8,128)(2,1)S(1)}, u32[]{:S(2)}, u32[]{:S(2)}) %collective-permute-start.14) | collective-permute-done | bytes 524320 | tf_op jit(solution)/shard_map/ppermute | solution.py:325
  98.1 1.4 collective-permute-done.16
  99.7 2.7 %collective-permute-start.21 = (bf16[8,128,128]{2,1,0:T(8,128)(2,1)S(1)}, bf16[8,128,128]{2,1,0:T(8,128)(2,1)S(1)}, u32[]{:S(2)}, u32[]{:S(2)}) collective-permute-start(bf16[8,128,128]{2,1,0:T(8,128)(2,1)S(1)} %slice.43), channel_id=1, source_target_pairs={{0,16},{16,32},{32,48},{48,0},{1,17},{17,33},{33,49},{49,1},{2,18}... | collective-permute-start | bytes 786440 | tf_op jit(solution)/shard_map/ppermute | solution.py:313
  102.5 5.3 %collective-permute-start.20 = (bf16[8,128,128]{2,1,0:T(8,128)(2,1)S(1)}, bf16[8,128,128]{2,1,0:T(8,128)(2,1)S(1)}, u32[]{:S(2)}, u32[]{:S(2)}) collective-permute-start(bf16[8,128,128]{2,1,0:T(8,128)(2,1)S(1)} %slice.42), channel_id=1, source_target_pairs={{0,48},{16,0},{32,16},{48,32},{1,49},{17,1},{33,17},{49,33},{2,50}... | collective-permute-start | bytes 786440 | tf_op jit(solution)/shard_map/ppermute | solution.py:316
  108.7 3.9 %collective-permute-start.17 = (bf16[8,128,128]{2,1,0:T(8,128)(2,1)}, bf16[8,128,128]{2,1,0:T(8,128)(2,1)}, u32[]{:S(2)}, u32[]{:S(2)}) collective-permute-start(bf16[8,128,128]{2,1,0:T(8,128)(2,1)} %get-tuple-element.66), channel_id=1, source_target_pairs={{0,16},{16,32},{32,48},{48,0},{1,17},{17,33},{33,49},{49,1},{2,18}... | collective-permute-start | bytes 786440 | tf_op jit(solution)/shard_map/ppermute | solution.py:313
  112.6 1.1 collective-permute-start.22
  113.7 5.1 %collective-permute-done.20 = bf16[8,128,128]{2,1,0:T(8,128)(2,1)S(1)} collective-permute-done((bf16[8,128,128]{2,1,0:T(8,128)(2,1)S(1)}, bf16[8,128,128]{2,1,0:T(8,128)(2,1)S(1)}, u32[]{:S(2)}, u32[]{:S(2)}) %collective-permute-start.20) | collective-permute-done | bytes 262176 | tf_op jit(solution)/shard_map/ppermute | solution.py:316
  119.6 7.2 %all-to-all-start.2 = ((bf16[8,256,128]{2,1,0:T(8,128)(2,1)}), bf16[8,256,128]{2,1,0:T(8,128)(2,1)S(1)}, u32[]{:S(2)}, u32[]{:S(2)}) async-start(bf16[8,256,128]{2,1,0:T(8,128)(2,1)} %get-tuple-element.55), calls=%async_computation.2 | async-start | bytes 1048576 | tf_op jit(solution)/shard_map/all_to_all | solution.py:310
  127.8 2.1 %collective-permute-start.18 = (bf16[8,128,128]{2,1,0:T(8,128)(2,1)S(1)}, bf16[8,128,128]{2,1,0:T(8,128)(2,1)S(1)}, u32[]{:S(2)}, u32[]{:S(2)}) collective-permute-start(bf16[8,128,128]{2,1,0:T(8,128)(2,1)S(1)} %add_convert_fusion.7), channel_id=1, source_target_pairs={{0,16},{16,32},{32,48},{48,0},{1,17},{17,33},{33,49},{49,1},{2,18}... | collective-permute-start | bytes 786440 | tf_op jit(solution)/shard_map/ppermute | solution.py:313
  130.0 1.3 collective-permute-start.23
  131.4 4.0 %collective-permute-done.18 = bf16[8,128,128]{2,1,0:T(8,128)(2,1)S(1)} collective-permute-done((bf16[8,128,128]{2,1,0:T(8,128)(2,1)S(1)}, bf16[8,128,128]{2,1,0:T(8,128)(2,1)S(1)}, u32[]{:S(2)}, u32[]{:S(2)}) %collective-permute-start.18) | collective-permute-done | bytes 262176 | tf_op jit(solution)/shard_map/ppermute | solution.py:313
  135.4 1.0 collective-permute-done.23
  137.7 8.8 %all-to-all-start.3 = ((bf16[8,256,128]{2,1,0:T(8,128)(2,1)}), bf16[8,256,128]{2,1,0:T(8,128)(2,1)S(1)}, u32[]{:S(2)}, u32[]{:S(2)}) async-start(bf16[8,256,128]{2,1,0:T(8,128)(2,1)} %pad_maximum_fusion), calls=%async_computation.3 | async-start | bytes 1048576 | tf_op jit(solution)/shard_map/all_to_all | solution.py:310
  146.5 3.4 %collective-permute-start.24 = (bf16[8,256,128]{2,1,0:T(8,128)(2,1)S(1)}, bf16[8,256,128]{2,1,0:T(8,128)(2,1)S(1)}, u32[]{:S(2)}, u32[]{:S(2)}) collective-permute-start(bf16[8,256,128]{2,1,0:T(8,128)(2,1)S(1)} %all-to-all-done.2), channel_id=1, source_target_pairs={{0,0},{2,2},{4,4},{6,6},{8,56},{10,58},{12,60},{14,62},{16,16},{18... | collective-permute-start | bytes 1572872 | tf_op jit(solution)/shard_map/ppermute | solution.py:322
  149.9 10.8 %collective-permute-done.24.in_ref = bf16[8,256,128]{2,1,0:T(8,128)(2,1)S(1)} collective-permute-done((bf16[8,256,128]{2,1,0:T(8,128)(2,1)S(1)}, bf16[8,256,128]{2,1,0:T(8,128)(2,1)S(1)}, u32[]{:S(2)}, u32[]{:S(2)}) %collective-permute-start.24) | collective-permute-done | bytes 524320 | tf_op jit(solution)/shard_map/ppermute | solution.py:322
  161.5 2.0 %shard_map.87 = (bf16[1,128,1024]{2,1,0:T(8,128)(2,1)}, bf16[1,128,1024]{2,1,0:T(8,128)(2,1)}) custom-call(bf16[8,256,128]{2,1,0:T(8,128)(2,1)} %copy-done.8), custom_call_target="tpu_custom_call" | custom-call | tf_op jit(solution)/shard_map/pallas_call | solution.py:298
  164.3 2.0 %shard_map.88 = (bf16[1,128,1024]{2,1,0:T(8,128)(2,1)}, bf16[1,128,1024]{2,1,0:T(8,128)(2,1)}) custom-call(bf16[8,256,128]{2,1,0:T(8,128)(2,1)} %copy-done.7), custom_call_target="tpu_custom_call" | custom-call | tf_op jit(solution)/shard_map/pallas_call | solution.py:298
  (70 shorter events, 15.2 us)
Async XLA Ops:
  2.6 26.4 %all-to-all-start = ((bf16[8,272,128]{2,1,0:T(8,128)(2,1)}), bf16[8,272,128]{2,1,0:T(8,128)(2,1)S(1)}, u32[]{:S(2)}, u32[]{:S(2)}) async-start(bf16[8,272,128]{2,1,0:T(8,128)(2,1)} %shard_map.84), calls=%async_computation | async-start | bytes 1114112 | tf_op jit(solution)/shard_map/all_to_all | solution.py:310
  11.7 17.2 %collective-permute-start = (bf16[8,272,128]{2,1,0:T(8,128)(2,1)}, bf16[8,272,128]{2,1,0:T(8,128)(2,1)}, u32[]{:S(2)}, u32[]{:S(2)}) collective-permute-start(bf16[8,272,128]{2,1,0:T(8,128)(2,1)} %shard_map.85), channel_id=1, source_target_pairs={{0,0},{2,2},{4,4},{6,6},{8,56},{10,58},{12,60},{14,62},{16,16},{18... | collective-permute-start | bytes 1671176 | tf_op jit(solution)/shard_map/ppermute | solution.py:322
  28.9 2.0 %collective-permute-start.1 = (bf16[8,272,128]{2,1,0:T(8,128)(2,1)S(1)}, bf16[8,272,128]{2,1,0:T(8,128)(2,1)S(1)}, u32[]{:S(2)}, u32[]{:S(2)}) collective-permute-start(bf16[8,272,128]{2,1,0:T(8,128)(2,1)S(1)} %all-to-all-done.refs_0_), channel_id=1, source_target_pairs={{0,1},{1,0},{2,3},{3,2},{4,5},{5,4},{6,7},{7,6},{8,9},{9,8},{10,11... | collective-permute-start | bytes 1671176 | tf_op jit(solution)/shard_map/ppermute | solution.py:325
  30.9 33.2 %all-to-all-start.1 = ((bf16[8,272,128]{2,1,0:T(8,128)(2,1)}), bf16[8,272,128]{2,1,0:T(8,128)(2,1)S(1)}, u32[]{:S(2)}, u32[]{:S(2)}) async-start(bf16[8,272,128]{2,1,0:T(8,128)(2,1)} %collective-permute-done), calls=%async_computation.1 | async-start | bytes 1114112 | tf_op jit(solution)/shard_map/all_to_all | solution.py:310
  38.1 9.9 %collective-permute-start.8 = (bf16[4,272,128]{2,1,0:T(8,128)(2,1)S(1)}, bf16[4,272,128]{2,1,0:T(8,128)(2,1)S(1)}, u32[]{:S(2)}, u32[]{:S(2)}) collective-permute-start(bf16[4,272,128]{2,1,0:T(8,128)(2,1)S(1)} %get-tuple-element.62), channel_id=1, source_target_pairs={{0,48},{16,0},{32,16},{48,32},{1,49},{17,1},{33,17},{49,33},{2,50}... | collective-permute-start | bytes 835592 | tf_op jit(solution)/shard_map/ppermute | solution.py:316
  41.0 10.8 %collective-permute-start.2 = (bf16[4,272,128]{2,1,0:T(8,128)(2,1)S(1)}, bf16[4,272,128]{2,1,0:T(8,128)(2,1)S(1)}, u32[]{:S(2)}, u32[]{:S(2)}) collective-permute-start(bf16[4,272,128]{2,1,0:T(8,128)(2,1)S(1)} %get-tuple-element.63), channel_id=1, source_target_pairs={{0,16},{16,32},{32,48},{48,0},{1,17},{17,33},{33,49},{49,1},{2,18}... | collective-permute-start | bytes 835592 | tf_op jit(solution)/shard_map/ppermute | solution.py:313
  41.0 15.0 %collective-permute-start.4 = (bf16[4,272,128]{2,1,0:T(8,128)(2,1)S(1)}, bf16[4,272,128]{2,1,0:T(8,128)(2,1)S(1)}, u32[]{:S(2)}, u32[]{:S(2)}) collective-permute-start(bf16[4,272,128]{2,1,0:T(8,128)(2,1)S(1)} %get-tuple-element.62), channel_id=1, source_target_pairs={{0,16},{16,32},{32,48},{48,0},{1,17},{17,33},{33,49},{49,1},{2,18}... | collective-permute-start | bytes 835592 | tf_op jit(solution)/shard_map/ppermute | solution.py:313
  41.0 15.0 %collective-permute-start.6 = (bf16[4,272,128]{2,1,0:T(8,128)(2,1)S(1)}, bf16[4,272,128]{2,1,0:T(8,128)(2,1)S(1)}, u32[]{:S(2)}, u32[]{:S(2)}) collective-permute-start(bf16[4,272,128]{2,1,0:T(8,128)(2,1)S(1)} %get-tuple-element.63), channel_id=1, source_target_pairs={{0,48},{16,0},{32,16},{48,32},{1,49},{17,1},{33,17},{49,33},{2,50}... | collective-permute-start | bytes 835592 | tf_op jit(solution)/shard_map/ppermute | solution.py:316
  48.1 10.5 %collective-permute-start.12 = (bf16[4,272,128]{2,1,0:T(8,128)(2,1)S(1)}, bf16[4,272,128]{2,1,0:T(8,128)(2,1)S(1)}, u32[]{:S(2)}, u32[]{:S(2)}) collective-permute-start(bf16[4,272,128]{2,1,0:T(8,128)(2,1)S(1)} %collective-permute-done.8.refs_8_), channel_id=1, source_target_pairs={{0,48},{16,0},{32,16},{48,32},{1,49},{17,1},{33,17},{49,33},{2,50}... | collective-permute-start | bytes 835592 | tf_op jit(solution)/shard_map/ppermute | solution.py:316
  51.8 7.5 %collective-permute-start.9 = (bf16[4,272,128]{2,1,0:T(8,128)(2,1)S(1)}, bf16[4,272,128]{2,1,0:T(8,128)(2,1)S(1)}, u32[]{:S(2)}, u32[]{:S(2)}) collective-permute-start(bf16[4,272,128]{2,1,0:T(8,128)(2,1)S(1)} %collective-permute-done.8.refs_8_), channel_id=1, source_target_pairs={{0,1},{1,0},{2,3},{3,2},{4,5},{5,4},{6,7},{7,6},{8,9},{9,8},{10,11... | collective-permute-start | bytes 835592 | tf_op jit(solution)/shard_map/ppermute | solution.py:325
  51.8 10.4 %collective-permute-start.10 = (bf16[4,272,128]{2,1,0:T(8,128)(2,1)S(1)}, bf16[4,272,128]{2,1,0:T(8,128)(2,1)}, u32[]{:S(2)}, u32[]{:S(2)}) collective-permute-start(bf16[4,272,128]{2,1,0:T(8,128)(2,1)S(1)} %collective-permute-done.2.refs_2_), channel_id=1, source_target_pairs={{0,16},{16,32},{32,48},{48,0},{1,17},{17,33},{33,49},{49,1},{2,18}... | collective-permute-start | bytes 835592 | tf_op jit(solution)/shard_map/ppermute | solution.py:313
  56.0 6.8 %collective-permute-start.3 = (bf16[4,272,128]{2,1,0:T(8,128)(2,1)S(1)}, bf16[4,272,128]{2,1,0:T(8,128)(2,1)}, u32[]{:S(2)}, u32[]{:S(2)}) collective-permute-start(bf16[4,272,128]{2,1,0:T(8,128)(2,1)S(1)} %collective-permute-done.2.refs_2_), channel_id=1, source_target_pairs={{0,1},{1,0},{2,3},{3,2},{4,5},{5,4},{6,7},{7,6},{8,9},{9,8},{10,11... | collective-permute-start | bytes 835592 | tf_op jit(solution)/shard_map/ppermute | solution.py:325
  56.0 6.7 %collective-permute-start.5 = (bf16[4,272,128]{2,1,0:T(8,128)(2,1)S(1)}, bf16[4,272,128]{2,1,0:T(8,128)(2,1)}, u32[]{:S(2)}, u32[]{:S(2)}) collective-permute-start(bf16[4,272,128]{2,1,0:T(8,128)(2,1)S(1)} %collective-permute-done.4.refs_4_), channel_id=1, source_target_pairs={{0,1},{1,0},{2,3},{3,2},{4,5},{5,4},{6,7},{7,6},{8,9},{9,8},{10,11... | collective-permute-start | bytes 835592 | tf_op jit(solution)/shard_map/ppermute | solution.py:325
  58.6 4.2 %collective-permute-start.7 = (bf16[4,272,128]{2,1,0:T(8,128)(2,1)S(1)}, bf16[4,272,128]{2,1,0:T(8,128)(2,1)}, u32[]{:S(2)}, u32[]{:S(2)}) collective-permute-start(bf16[4,272,128]{2,1,0:T(8,128)(2,1)S(1)} %collective-permute-done.6.refs_6_), channel_id=1, source_target_pairs={{0,1},{1,0},{2,3},{3,2},{4,5},{5,4},{6,7},{7,6},{8,9},{9,8},{10,11... | collective-permute-start | bytes 835592 | tf_op jit(solution)/shard_map/ppermute | solution.py:325
  60.0 2.7 %collective-permute-start.13 = (bf16[4,272,128]{2,1,0:T(8,128)(2,1)S(1)}, bf16[4,272,128]{2,1,0:T(8,128)(2,1)}, u32[]{:S(2)}, u32[]{:S(2)}) collective-permute-start(bf16[4,272,128]{2,1,0:T(8,128)(2,1)S(1)} %collective-permute-done.12.refs_12_), channel_id=1, source_target_pairs={{0,1},{1,0},{2,3},{3,2},{4,5},{5,4},{6,7},{7,6},{8,9},{9,8},{10,11... | collective-permute-start | bytes 835592 | tf_op jit(solution)/shard_map/ppermute | solution.py:325
  62.2 1.9 %collective-permute-start.11 = (bf16[4,272,128]{2,1,0:T(8,128)(2,1)}, bf16[4,272,128]{2,1,0:T(8,128)(2,1)}, u32[]{:S(2)}, u32[]{:S(2)}) collective-permute-start(bf16[4,272,128]{2,1,0:T(8,128)(2,1)} %collective-permute-done.10.refs_10_), channel_id=1, source_target_pairs={{0,1},{1,0},{2,3},{3,2},{4,5},{5,4},{6,7},{7,6},{8,9},{9,8},{10,11... | collective-permute-start | bytes 835592 | tf_op jit(solution)/shard_map/ppermute | solution.py:325
  95.4 2.0 %collective-permute-start.14 = (bf16[8,256,128]{2,1,0:T(8,128)(2,1)S(1)}, bf16[8,256,128]{2,1,0:T(8,128)(2,1)S(1)}, u32[]{:S(2)}, u32[]{:S(2)}) collective-permute-start(bf16[8,256,128]{2,1,0:T(8,128)(2,1)S(1)} %get-tuple-element.38), channel_id=1, source_target_pairs={{0,1},{1,0},{2,3},{3,2},{4,5},{5,4},{6,7},{7,6},{8,9},{9,8},{10,11... | collective-permute-start | bytes 1572872 | tf_op jit(solution)/shard_map/ppermute | solution.py:325
  97.5 2.0 %collective-permute-start.16 = (bf16[8,256,128]{2,1,0:T(8,128)(2,1)S(1)}, bf16[8,256,128]{2,1,0:T(8,128)(2,1)S(1)}, u32[]{:S(2)}, u32[]{:S(2)}) collective-permute-start(bf16[8,256,128]{2,1,0:T(8,128)(2,1)S(1)} %get-tuple-element.48), channel_id=1, source_target_pairs={{0,1},{1,0},{2,3},{3,2},{4,5},{5,4},{6,7},{7,6},{8,9},{9,8},{10,11... | collective-permute-start | bytes 1572872 | tf_op jit(solution)/shard_map/ppermute | solution.py:325
  97.7 4.6 %collective-permute-start.19 = (bf16[8,256,128]{2,1,0:T(8,128)(2,1)S(1)}, bf16[8,256,128]{2,1,0:T(8,128)(2,1)S(1)}, u32[]{:S(2)}, u32[]{:S(2)}) collective-permute-start(bf16[8,256,128]{2,1,0:T(8,128)(2,1)S(1)} %get-tuple-element.52), channel_id=1, source_target_pairs={{0,1},{1,0},{2,3},{3,2},{4,5},{5,4},{6,7},{7,6},{8,9},{9,8},{10,11... | collective-permute-start | bytes 1572872 | tf_op jit(solution)/shard_map/ppermute | solution.py:325
  99.7 14.0 %collective-permute-start.21 = (bf16[8,128,128]{2,1,0:T(8,128)(2,1)S(1)}, bf16[8,128,128]{2,1,0:T(8,128)(2,1)S(1)}, u32[]{:S(2)}, u32[]{:S(2)}) collective-permute-start(bf16[8,128,128]{2,1,0:T(8,128)(2,1)S(1)} %slice.43), channel_id=1, source_target_pairs={{0,16},{16,32},{32,48},{48,0},{1,17},{17,33},{33,49},{49,1},{2,18}... | collective-permute-start | bytes 786440 | tf_op jit(solution)/shard_map/ppermute | solution.py:313
  102.5 16.3 %collective-permute-start.20 = (bf16[8,128,128]{2,1,0:T(8,128)(2,1)S(1)}, bf16[8,128,128]{2,1,0:T(8,128)(2,1)S(1)}, u32[]{:S(2)}, u32[]{:S(2)}) collective-permute-start(bf16[8,128,128]{2,1,0:T(8,128)(2,1)S(1)} %slice.42), channel_id=1, source_target_pairs={{0,48},{16,0},{32,16},{48,32},{1,49},{17,1},{33,17},{49,33},{2,50}... | collective-permute-start | bytes 786440 | tf_op jit(solution)/shard_map/ppermute | solution.py:316
  108.7 18.1 %collective-permute-start.17 = (bf16[8,128,128]{2,1,0:T(8,128)(2,1)}, bf16[8,128,128]{2,1,0:T(8,128)(2,1)}, u32[]{:S(2)}, u32[]{:S(2)}) collective-permute-start(bf16[8,128,128]{2,1,0:T(8,128)(2,1)} %get-tuple-element.66), channel_id=1, source_target_pairs={{0,16},{16,32},{32,48},{48,0},{1,17},{17,33},{33,49},{49,1},{2,18}... | collective-permute-start | bytes 786440 | tf_op jit(solution)/shard_map/ppermute | solution.py:313
  112.6 18.7 %collective-permute-start.15 = (bf16[8,256,128]{2,1,0:T(8,128)(2,1)S(1)}, bf16[8,256,128]{2,1,0:T(8,128)(2,1)S(1)}, u32[]{:S(2)}, u32[]{:S(2)}) collective-permute-start(bf16[8,256,128]{2,1,0:T(8,128)(2,1)S(1)} %get-tuple-element.46), channel_id=1, source_target_pairs={{0,1},{1,0},{2,3},{3,2},{4,5},{5,4},{6,7},{7,6},{8,9},{9,8},{10,11... | collective-permute-start | bytes 1572872 | tf_op jit(solution)/shard_map/ppermute | solution.py:325
  112.6 17.4 %collective-permute-start.22 = (bf16[8,128,128]{2,1,0:T(8,128)(2,1)}, bf16[8,128,128]{2,1,0:T(8,128)(2,1)S(1)}, u32[]{:S(2)}, u32[]{:S(2)}) collective-permute-start(bf16[8,128,128]{2,1,0:T(8,128)(2,1)} %get-tuple-element.67), channel_id=1, source_target_pairs={{0,48},{16,0},{32,16},{48,32},{1,49},{17,1},{33,17},{49,33},{2,50}... | collective-permute-start | bytes 786440 | tf_op jit(solution)/shard_map/ppermute | solution.py:316
  113.7 5.1 %copy-start.9 = (bf16[8,128,128]{2,1,0:T(8,128)(2,1)}, bf16[8,128,128]{2,1,0:T(8,128)(2,1)S(1)}, u32[]{:S(2)}) copy-start(bf16[8,128,128]{2,1,0:T(8,128)(2,1)S(1)} %collective-permute-done.21) | copy-start | bytes 786436
  119.6 18.1 %all-to-all-start.2 = ((bf16[8,256,128]{2,1,0:T(8,128)(2,1)}), bf16[8,256,128]{2,1,0:T(8,128)(2,1)S(1)}, u32[]{:S(2)}, u32[]{:S(2)}) async-start(bf16[8,256,128]{2,1,0:T(8,128)(2,1)} %get-tuple-element.55), calls=%async_computation.2 | async-start | bytes 1048576 | tf_op jit(solution)/shard_map/all_to_all | solution.py:310
  127.8 7.7 %collective-permute-start.18 = (bf16[8,128,128]{2,1,0:T(8,128)(2,1)S(1)}, bf16[8,128,128]{2,1,0:T(8,128)(2,1)S(1)}, u32[]{:S(2)}, u32[]{:S(2)}) collective-permute-start(bf16[8,128,128]{2,1,0:T(8,128)(2,1)S(1)} %add_convert_fusion.7), channel_id=1, source_target_pairs={{0,16},{16,32},{32,48},{48,0},{1,17},{17,33},{33,49},{49,1},{2,18}... | collective-permute-start | bytes 786440 | tf_op jit(solution)/shard_map/ppermute | solution.py:313
  130.0 6.5 %copy-start.10 = (bf16[8,128,128]{2,1,0:T(8,128)(2,1)S(1)}, bf16[8,128,128]{2,1,0:T(8,128)(2,1)}, u32[]{:S(2)}) copy-start(bf16[8,128,128]{2,1,0:T(8,128)(2,1)} %copy-done.9) | copy-start | bytes 786436
  130.0 6.5 %copy-start.12 = (bf16[8,128,128]{2,1,0:T(8,128)(2,1)S(1)}, bf16[8,128,128]{2,1,0:T(8,128)(2,1)}, u32[]{:S(2)}) copy-start(bf16[8,128,128]{2,1,0:T(8,128)(2,1)} %copy-done.11) | copy-start | bytes 786436
  130.0 6.4 %collective-permute-start.23 = (bf16[8,128,128]{2,1,0:T(8,128)(2,1)S(1)}, bf16[8,128,128]{2,1,0:T(8,128)(2,1)S(1)}, u32[]{:S(2)}, u32[]{:S(2)}) collective-permute-start(bf16[8,128,128]{2,1,0:T(8,128)(2,1)S(1)} %add_convert_fusion.5), channel_id=1, source_target_pairs={{0,48},{16,0},{32,16},{48,32},{1,49},{17,1},{33,17},{49,33},{2,50}... | collective-permute-start | bytes 786440 | tf_op jit(solution)/shard_map/ppermute | solution.py:316
  137.7 25.8 %all-to-all-start.3 = ((bf16[8,256,128]{2,1,0:T(8,128)(2,1)}), bf16[8,256,128]{2,1,0:T(8,128)(2,1)S(1)}, u32[]{:S(2)}, u32[]{:S(2)}) async-start(bf16[8,256,128]{2,1,0:T(8,128)(2,1)} %pad_maximum_fusion), calls=%async_computation.3 | async-start | bytes 1048576 | tf_op jit(solution)/shard_map/all_to_all | solution.py:310
  146.5 14.2 %collective-permute-start.24 = (bf16[8,256,128]{2,1,0:T(8,128)(2,1)S(1)}, bf16[8,256,128]{2,1,0:T(8,128)(2,1)S(1)}, u32[]{:S(2)}, u32[]{:S(2)}) collective-permute-start(bf16[8,256,128]{2,1,0:T(8,128)(2,1)S(1)} %all-to-all-done.2), channel_id=1, source_target_pairs={{0,0},{2,2},{4,4},{6,6},{8,56},{10,58},{12,60},{14,62},{16,16},{18... | collective-permute-start | bytes 1572872 | tf_op jit(solution)/shard_map/ppermute | solution.py:322
  (10 other events, 8.0 us)

commit v5 on v4

--- a/solution.py
+++ b/solution.py
@@ -31,9 +31,7 @@
     return lax.dot_general(a, b, dims, preferred_element_type=jnp.float32)
 
 
-PIECES = (
-    (0, 0, 8), (3, 0, 4), (3, 4, 4), (1, 0, 4), (1, 4, 4), (2, 0, 4), (2, 4, 4)
-)
+PIECES = ((0, 0, 8), (3, 0, 8), (1, 0, 8), (2, 0, 4), (2, 4, 4))
 N_PIECES = 2 * len(PIECES)
 
 
@@ -330,28 +328,25 @@
     kvs = over_heads(pack(key, value, scale_ids))
     swapped = swap(pack(query, grad_attn, scale_ids))
     kvs, swapped = lax.optimization_barrier((kvs, swapped))
-    kvs_twin = twin(kvs)
-    low, high = kvs[:half], kvs[half:]
-    left_low, right_high = right(low), left(high)
-    left_high, right_low = right(high), left(low)
-    swapped, kvs_twin = lax.optimization_barrier((swapped, kvs_twin))
+    from_left, from_right = right(kvs), left(kvs)
     qd = over_heads(swapped)
-    opposite_low, opposite_high = right(left_low), left(right_high)
-    pieces = [kvs, kvs_twin]
-    for piece in (left_low, left_high, right_low, right_high, opposite_low, opposite_high):
+    opposite_a, opposite_b = right(from_left[:half]), left(from_right[half:])
+    pieces = []
+    for piece in (kvs, from_left, from_right, opposite_a, opposite_b):
         pieces += [piece, twin(piece)]
 
     ad, *grads = attention(at, pieces, qd)
 
-    k, v = slice(0, ROWS), slice(ROWS, 2 * ROWS)
+    ad_back = over_heads(ad)
     far = add(grads[4], twin(grads[5]))
     far, *grads = lax.optimization_barrier((far, *grads))
     sums = {distance: add(grads[2 * distance], twin(grads[2 * distance + 1])) for distance in (3, 1, 0)}
-    key_left, value_right = left(sums[3][:, k]), right(sums[1][:, v])
-    key_right = right(add(sums[1][:, k], right(far[:, k])))
-    value_left = left(add(sums[3][:, v], left(far[:, v])))
-    ad, key_left, value_right = lax.optimization_barrier((ad, key_left, value_right))
-    ad_back = over_heads(ad)
+    k, v = slice(0, ROWS), slice(ROWS, 2 * ROWS)
+    key_left = left(sums[3][:, k])
+    key_relay = add(sums[1][:, k], right(far[:, k]))
+    value_relay = add(sums[3][:, v], left(far[:, v]))
+    key_right, value_left = right(key_relay), left(value_relay)
+    value_right = right(sums[1][:, v])
     key_sum = add(sums[0][:, k], key_right, key_left)
     value_sum = add(sums[0][:, v], value_right, value_left)
     sums = jnp.concatenate([key_sum, value_sum], axis=1)

time: 167 us -> 157 us (0.940)
  the two profiles are of different devices: /device:TPU:152 before, /device:TPU:16 now
where the time goes in v5:
time: 157 us; the launch traced here: 155 us
  starting transfers between devices  63.2 us (40%)
  waiting for transfers between devices  46.9 us (30%)
  Pallas kernels  35.8 us (23%)
  local copies, waits for them, and re-layouts  6.26 us (4%)
  other arithmetic  1.86 us (1%)
    all_to_all x4, starting transfers between devices, over_heads(): return lax.all_to_all(arr, 'z', split_axis=0, concat_axis=0, tiled=True)  29.7 us
    pallas_call x1, Pallas kernels, attention(): pl.pallas_call(attention_kernel, out_shape=outs, in_specs=[pl.BlockSpec(m...  27.9 us
    all_to_all x4, waiting for transfers between devices, over_heads(): return lax.all_to_all(arr, 'z', split_axis=0, concat_axis=0, tiled=True)  22.1 us
    ppermute x5, waiting for transfers between devices, left(): return lax.ppermute(arr, 'x', [(i, (i + XS - 1) % XS) for i in range(XS)])  14.9 us
    ppermute x5, starting transfers between devices, left(): return lax.ppermute(arr, 'x', [(i, (i + XS - 1) % XS) for i in range(XS)])  12.2 us
    ppermute x5, starting transfers between devices, right(): return lax.ppermute(arr, 'x', [(i, (i + 1) % XS) for i in range(XS)])  11.7 us
    ppermute x5, waiting for transfers between devices, right(): return lax.ppermute(arr, 'x', [(i, (i + 1) % XS) for i in range(XS)])  8.22 us
    ppermute x2, starting transfers between devices, swap(): return lax.ppermute(arr, ('x', 'z'), pairs)  7.52 us
  transfers between devices with their start and end apart: 25, of which 11 were waited for; matrix products, arithmetic and copies ran while one was open for 1% of the time, Pallas kernels for 3%

profile of v5, /device:TPU:16, one launch (start us, length us, event | category | flops | bytes accessed | tf_op | source)
XLA Modules:
  0.0 154.9 jit_solution(3183418780663135479)
XLA Ops:
  0.6 1.9 %shard_map.84 = bf16[8,272,128]{2,1,0:T(8,128)(2,1)} custom-call(bf16[1,128,1024]{2,1,0:T(8,128)(2,1)} %a_ref.2, bf16[1,128,1024]{2,1,0:T(8,128)(2,1)} %b_ref.2, s32[1,128]{1,0:T(1,128)} %scale_ref.3), custom_call_target="tpu_custom_call" | custom-call | tf_op jit(solution)/shard_map/pallas_call | solution.py:274
  2.6 8.5 %all-to-all-start = ((bf16[8,272,128]{2,1,0:T(8,128)(2,1)}), bf16[8,272,128]{2,1,0:T(8,128)(2,1)S(1)}, u32[]{:S(2)}, u32[]{:S(2)}) async-start(bf16[8,272,128]{2,1,0:T(8,128)(2,1)} %shard_map.84), calls=%async_computation | async-start | bytes 1114112 | tf_op jit(solution)/shard_map/all_to_all | solution.py:308
  11.0 2.0 %shard_map.85 = bf16[8,272,128]{2,1,0:T(8,128)(2,1)} custom-call(bf16[1,128,1024]{2,1,0:T(8,128)(2,1)} %a_ref.3, bf16[1,128,1024]{2,1,0:T(8,128)(2,1)} %b_ref.3, s32[1,128]{1,0:T(1,128)} %scale_ref.3), custom_call_target="tpu_custom_call" | custom-call | tf_op jit(solution)/shard_map/pallas_call | solution.py:274
  13.0 5.8 %collective-permute-start = (bf16[8,272,128]{2,1,0:T(8,128)(2,1)}, bf16[8,272,128]{2,1,0:T(8,128)(2,1)}, u32[]{:S(2)}, u32[]{:S(2)}) collective-permute-start(bf16[8,272,128]{2,1,0:T(8,128)(2,1)} %shard_map.85), channel_id=1, source_target_pairs={{0,0},{2,2},{4,4},{6,6},{8,56},{10,58},{12,60},{14,62},{16,16},{18... | collective-permute-start | bytes 1671176 | tf_op jit(solution)/shard_map/ppermute | solution.py:320
  18.8 10.4 %all-to-all-done.refs_0_ = bf16[8,272,128]{2,1,0:T(8,128)(2,1)S(1)} async-done(((bf16[8,272,128]{2,1,0:T(8,128)(2,1)}), bf16[8,272,128]{2,1,0:T(8,128)(2,1)S(1)}, u32[]{:S(2)}, u32[]{:S(2)}) %all-to-all-start) | async-done | bytes 557088 | tf_op jit(solution)/shard_map/all_to_all | solution.py:308
  29.2 2.8 %collective-permute-start.4 = (bf16[8,272,128]{2,1,0:T(8,128)(2,1)S(1)}, bf16[8,272,128]{2,1,0:T(8,128)(2,1)S(1)}, u32[]{:S(2)}, u32[]{:S(2)}) collective-permute-start(bf16[8,272,128]{2,1,0:T(8,128)(2,1)S(1)} %all-to-all-done.refs_0_), channel_id=1, source_target_pairs={{0,48},{16,0},{32,16},{48,32},{1,49},{17,1},{33,17},{49,33},{2,50}... | collective-permute-start | bytes 1671176 | tf_op jit(solution)/shard_map/ppermute | solution.py:314
  32.0 8.2 %all-to-all-start.1 = ((bf16[8,272,128]{2,1,0:T(8,128)(2,1)}), bf16[8,272,128]{2,1,0:T(8,128)(2,1)S(1)}, u32[]{:S(2)}, u32[]{:S(2)}) async-start(bf16[8,272,128]{2,1,0:T(8,128)(2,1)} %collective-permute-done), calls=%async_computation.1 | async-start | bytes 1114112 | tf_op jit(solution)/shard_map/all_to_all | solution.py:308
  40.2 3.9 %collective-permute-done.4.refs_4_ = bf16[8,272,128]{2,1,0:T(8,128)(2,1)S(1)} collective-permute-done((bf16[8,272,128]{2,1,0:T(8,128)(2,1)S(1)}, bf16[8,272,128]{2,1,0:T(8,128)(2,1)S(1)}, u32[]{:S(2)}, u32[]{:S(2)}) %collective-permute-start.4) | collective-permute-done | bytes 557088 | tf_op jit(solution)/shard_map/ppermute | solution.py:314
  44.1 3.8 %collective-permute-start.8 = (bf16[4,272,128]{2,1,0:T(8,128)(2,1)S(1)}, bf16[4,272,128]{2,1,0:T(8,128)(2,1)S(1)}, u32[]{:S(2)}, u32[]{:S(2)}) collective-permute-start(bf16[4,272,128]{2,1,0:T(8,128)(2,1)S(1)} %slice.41), channel_id=1, source_target_pairs={{0,48},{16,0},{32,16},{48,32},{1,49},{17,1},{33,17},{49,33},{2,50}... | collective-permute-start | bytes 835592 | tf_op jit(solution)/shard_map/ppermute | solution.py:314
  48.6 4.5 %collective-permute-done.8.refs_8_ = bf16[4,272,128]{2,1,0:T(8,128)(2,1)S(1)} collective-permute-done((bf16[4,272,128]{2,1,0:T(8,128)(2,1)S(1)}, bf16[4,272,128]{2,1,0:T(8,128)(2,1)S(1)}, u32[]{:S(2)}, u32[]{:S(2)}) %collective-permute-start.8) | collective-permute-done | bytes 278560 | tf_op jit(solution)/shard_map/ppermute | solution.py:314
  53.1 3.5 %collective-permute-done.6.refs_6_ = bf16[4,272,128]{2,1,0:T(8,128)(2,1)S(1)} collective-permute-done((bf16[4,272,128]{2,1,0:T(8,128)(2,1)S(1)}, bf16[4,272,128]{2,1,0:T(8,128)(2,1)S(1)}, u32[]{:S(2)}, u32[]{:S(2)}) %collective-permute-start.6) | collective-permute-done | bytes 278560 | tf_op jit(solution)/shard_map/ppermute | solution.py:311
  58.3 1.0 copy-done.1
  59.4 1.1 copy-done.3
  60.4 1.0 copy-done.9
  61.4 27.9 %shard_map.86 = (bf16[8,256,128]{2,1,0:T(8,128)(2,1)}, bf16[8,256,128]{2,1,0:T(8,128)(2,1)S(1)}, bf16[8,256,128]{2,1,0:T(8,128)(2,1)S(1)}, bf16[8,256,128]{2,1,0...) custom-call(s32[2]{0:T(128)S(1)} %pad_add_fusion.at_ref, ...), custom_call_target="tpu_custom_call" | custom-call | flops 8000000000 | bytes 10485760 | tf_op jit(solution)/shard_map/pallas_call | solution.py:230
  89.8 1.5 collective-permute-done.10
  92.2 5.8 %all-to-all-start.2 = ((bf16[8,256,128]{2,1,0:T(8,128)(2,1)}), bf16[8,256,128]{2,1,0:T(8,128)(2,1)}, u32[]{:S(2)}, u32[]{:S(2)}) async-start(bf16[8,256,128]{2,1,0:T(8,128)(2,1)} %get-tuple-element.45), calls=%async_computation.2 | async-start | bytes 1048576 | tf_op jit(solution)/shard_map/all_to_all | solution.py:308
  98.1 1.2 collective-permute-start.13
  99.3 2.4 %collective-permute-start.18 = (bf16[8,128,128]{2,1,0:T(8,128)(2,1)S(1)}, bf16[8,128,128]{2,1,0:T(8,128)(2,1)S(1)}, u32[]{:S(2)}, u32[]{:S(2)}) collective-permute-start(bf16[8,128,128]{2,1,0:T(8,128)(2,1)S(1)} %get-tuple-element.55), channel_id=1, source_target_pairs={{0,48},{16,0},{32,16},{48,32},{1,49},{17,1},{33,17},{49,33},{2,50}... | collective-permute-start | bytes 786440 | tf_op jit(solution)/shard_map/ppermute | solution.py:314
  102.1 5.3 %collective-permute-start.17 = (bf16[8,128,128]{2,1,0:T(8,128)(2,1)S(1)}, bf16[8,128,128]{2,1,0:T(8,128)(2,1)S(1)}, u32[]{:S(2)}, u32[]{:S(2)}) collective-permute-start(bf16[8,128,128]{2,1,0:T(8,128)(2,1)S(1)} %slice.46), channel_id=1, source_target_pairs={{0,16},{16,32},{32,48},{48,0},{1,17},{17,33},{33,49},{49,1},{2,18}... | collective-permute-start | bytes 786440 | tf_op jit(solution)/shard_map/ppermute | solution.py:311
  107.3 1.2 collective-permute-done.13
  108.6 5.2 %collective-permute-start.14 = (bf16[8,128,128]{2,1,0:T(8,128)(2,1)S(1)}, bf16[8,128,128]{2,1,0:T(8,128)(2,1)S(1)}, u32[]{:S(2)}, u32[]{:S(2)}) collective-permute-start(bf16[8,128,128]{2,1,0:T(8,128)(2,1)S(1)} %add_convert_fusion.7), channel_id=1, source_target_pairs={{0,16},{16,32},{32,48},{48,0},{1,17},{17,33},{33,49},{49,1},{2,18}... | collective-permute-start | bytes 786440 | tf_op jit(solution)/shard_map/ppermute | solution.py:311
  114.0 1.2 collective-permute-start.16
  115.2 2.1 %collective-permute-start.19 = (bf16[8,128,128]{2,1,0:T(8,128)(2,1)S(1)}, bf16[8,128,128]{2,1,0:T(8,128)(2,1)S(1)}, u32[]{:S(2)}, u32[]{:S(2)}) collective-permute-start(bf16[8,128,128]{2,1,0:T(8,128)(2,1)S(1)} %add_convert_fusion.5), channel_id=1, source_target_pairs={{0,48},{16,0},{32,16},{48,32},{1,49},{17,1},{33,17},{49,33},{2,50}... | collective-permute-start | bytes 786440 | tf_op jit(solution)/shard_map/ppermute | solution.py:314
  117.5 3.5 %collective-permute-done.14 = bf16[8,128,128]{2,1,0:T(8,128)(2,1)S(1)} collective-permute-done((bf16[8,128,128]{2,1,0:T(8,128)(2,1)S(1)}, bf16[8,128,128]{2,1,0:T(8,128)(2,1)S(1)}, u32[]{:S(2)}, u32[]{:S(2)}) %collective-permute-start.14) | collective-permute-done | bytes 262176 | tf_op jit(solution)/shard_map/ppermute | solution.py:311
  121.0 2.8 %collective-permute-done.16 = bf16[8,128,128]{2,1,0:T(8,128)(2,1)S(1)} collective-permute-done((bf16[8,128,128]{2,1,0:T(8,128)(2,1)S(1)}, bf16[8,128,128]{2,1,0:T(8,128)(2,1)S(1)}, u32[]{:S(2)}, u32[]{:S(2)}) %collective-permute-start.16) | collective-permute-done | bytes 262176 | tf_op jit(solution)/shard_map/ppermute | solution.py:314
  123.7 3.7 %collective-permute-done.19 = bf16[8,128,128]{2,1,0:T(8,128)(2,1)S(1)} collective-permute-done((bf16[8,128,128]{2,1,0:T(8,128)(2,1)S(1)}, bf16[8,128,128]{2,1,0:T(8,128)(2,1)S(1)}, u32[]{:S(2)}, u32[]{:S(2)}) %collective-permute-start.19) | collective-permute-done | bytes 262176 | tf_op jit(solution)/shard_map/ppermute | solution.py:314
  128.5 7.3 %all-to-all-start.3 = ((bf16[8,256,128]{2,1,0:T(8,128)(2,1)}), bf16[8,256,128]{2,1,0:T(8,128)(2,1)S(1)}, u32[]{:S(2)}, u32[]{:S(2)}) async-start(bf16[8,256,128]{2,1,0:T(8,128)(2,1)} %pad_maximum_fusion), calls=%async_computation.3 | async-start | bytes 1048576 | tf_op jit(solution)/shard_map/all_to_all | solution.py:308
  135.9 1.7 %collective-permute-start.20 = (bf16[8,256,128]{2,1,0:T(8,128)(2,1)}, bf16[8,256,128]{2,1,0:T(8,128)(2,1)S(1)}, u32[]{:S(2)}, u32[]{:S(2)}) collective-permute-start(bf16[8,256,128]{2,1,0:T(8,128)(2,1)} %all-to-all-done.2), channel_id=1, source_target_pairs={{0,0},{2,2},{4,4},{6,6},{8,56},{10,58},{12,60},{14,62},{16,16},{18... | collective-permute-start | bytes 1572872 | tf_op jit(solution)/shard_map/ppermute | solution.py:320
  138.4 2.0 %shard_map.87 = (bf16[1,128,1024]{2,1,0:T(8,128)(2,1)}, bf16[1,128,1024]{2,1,0:T(8,128)(2,1)}) custom-call(bf16[8,256,128]{2,1,0:T(8,128)(2,1)} %copy-done.11), custom_call_target="tpu_custom_call" | custom-call | tf_op jit(solution)/shard_map/pallas_call | solution.py:296
  140.3 11.7 %all-to-all-done.3.in_ref = bf16[8,256,128]{2,1,0:T(8,128)(2,1)S(1)} async-done(((bf16[8,256,128]{2,1,0:T(8,128)(2,1)}), bf16[8,256,128]{2,1,0:T(8,128)(2,1)S(1)}, u32[]{:S(2)}, u32[]{:S(2)}) %all-to-all-start.3) | async-done | bytes 524320 | tf_op jit(solution)/shard_map/all_to_all | solution.py:308
  152.8 2.0 %shard_map.88 = (bf16[1,128,1024]{2,1,0:T(8,128)(2,1)}, bf16[1,128,1024]{2,1,0:T(8,128)(2,1)}) custom-call(bf16[8,256,128]{2,1,0:T(8,128)(2,1)} %copy-done.10), custom_call_target="tpu_custom_call" | custom-call | tf_op jit(solution)/shard_map/pallas_call | solution.py:296
  (61 shorter events, 7.3 us)
Async XLA Ops:
  2.6 26.7 %all-to-all-start = ((bf16[8,272,128]{2,1,0:T(8,128)(2,1)}), bf16[8,272,128]{2,1,0:T(8,128)(2,1)S(1)}, u32[]{:S(2)}, u32[]{:S(2)}) async-start(bf16[8,272,128]{2,1,0:T(8,128)(2,1)} %shard_map.84), calls=%async_computation | async-start | bytes 1114112 | tf_op jit(solution)/shard_map/all_to_all | solution.py:308
  13.0 5.8 %collective-permute-start = (bf16[8,272,128]{2,1,0:T(8,128)(2,1)}, bf16[8,272,128]{2,1,0:T(8,128)(2,1)}, u32[]{:S(2)}, u32[]{:S(2)}) collective-permute-start(bf16[8,272,128]{2,1,0:T(8,128)(2,1)} %shard_map.85), channel_id=1, source_target_pairs={{0,0},{2,2},{4,4},{6,6},{8,56},{10,58},{12,60},{14,62},{16,16},{18... | collective-permute-start | bytes 1671176 | tf_op jit(solution)/shard_map/ppermute | solution.py:320
  29.2 14.8 %collective-permute-start.4 = (bf16[8,272,128]{2,1,0:T(8,128)(2,1)S(1)}, bf16[8,272,128]{2,1,0:T(8,128)(2,1)S(1)}, u32[]{:S(2)}, u32[]{:S(2)}) collective-permute-start(bf16[8,272,128]{2,1,0:T(8,128)(2,1)S(1)} %all-to-all-done.refs_0_), channel_id=1, source_target_pairs={{0,48},{16,0},{32,16},{48,32},{1,49},{17,1},{33,17},{49,33},{2,50}... | collective-permute-start | bytes 1671176 | tf_op jit(solution)/shard_map/ppermute | solution.py:314
  32.0 15.9 %collective-permute-start.2 = (bf16[8,272,128]{2,1,0:T(8,128)(2,1)S(1)}, bf16[8,272,128]{2,1,0:T(8,128)(2,1)S(1)}, u32[]{:S(2)}, u32[]{:S(2)}) collective-permute-start(bf16[8,272,128]{2,1,0:T(8,128)(2,1)S(1)} %all-to-all-done.refs_0_), channel_id=1, source_target_pairs={{0,16},{16,32},{32,48},{48,0},{1,17},{17,33},{33,49},{49,1},{2,18}... | collective-permute-start | bytes 1671176 | tf_op jit(solution)/shard_map/ppermute | solution.py:311
  32.0 26.2 %all-to-all-start.1 = ((bf16[8,272,128]{2,1,0:T(8,128)(2,1)}), bf16[8,272,128]{2,1,0:T(8,128)(2,1)S(1)}, u32[]{:S(2)}, u32[]{:S(2)}) async-start(bf16[8,272,128]{2,1,0:T(8,128)(2,1)} %collective-permute-done), calls=%async_computation.1 | async-start | bytes 1114112 | tf_op jit(solution)/shard_map/all_to_all | solution.py:308
  40.2 17.2 %collective-permute-start.1 = (bf16[8,272,128]{2,1,0:T(8,128)(2,1)S(1)}, bf16[8,272,128]{2,1,0:T(8,128)(2,1)S(1)}, u32[]{:S(2)}, u32[]{:S(2)}) collective-permute-start(bf16[8,272,128]{2,1,0:T(8,128)(2,1)S(1)} %all-to-all-done.refs_0_), channel_id=1, source_target_pairs={{0,1},{1,0},{2,3},{3,2},{4,5},{5,4},{6,7},{7,6},{8,9},{9,8},{10,11... | collective-permute-start | bytes 1671176 | tf_op jit(solution)/shard_map/ppermute | solution.py:323
  44.1 9.0 %collective-permute-start.8 = (bf16[4,272,128]{2,1,0:T(8,128)(2,1)S(1)}, bf16[4,272,128]{2,1,0:T(8,128)(2,1)S(1)}, u32[]{:S(2)}, u32[]{:S(2)}) collective-permute-start(bf16[4,272,128]{2,1,0:T(8,128)(2,1)S(1)} %slice.41), channel_id=1, source_target_pairs={{0,48},{16,0},{32,16},{48,32},{1,49},{17,1},{33,17},{49,33},{2,50}... | collective-permute-start | bytes 835592 | tf_op jit(solution)/shard_map/ppermute | solution.py:314
  47.9 10.5 %copy-start = (bf16[8,272,128]{2,1,0:T(8,128)(2,1)}, bf16[8,272,128]{2,1,0:T(8,128)(2,1)S(1)}, u32[]{:S(2)}) copy-start(bf16[8,272,128]{2,1,0:T(8,128)(2,1)S(1)} %collective-permute-done.2.refs_2_) | copy-start | bytes 1671172
  47.9 8.7 %collective-permute-start.6 = (bf16[4,272,128]{2,1,0:T(8,128)(2,1)S(1)}, bf16[4,272,128]{2,1,0:T(8,128)(2,1)S(1)}, u32[]{:S(2)}, u32[]{:S(2)}) collective-permute-start(bf16[4,272,128]{2,1,0:T(8,128)(2,1)S(1)} %slice.40), channel_id=1, source_target_pairs={{0,16},{16,32},{32,48},{48,0},{1,17},{17,33},{33,49},{49,1},{2,18}... | collective-permute-start | bytes 835592 | tf_op jit(solution)/shard_map/ppermute | solution.py:311
  48.0 10.3 %collective-permute-start.5 = (bf16[8,272,128]{2,1,0:T(8,128)(2,1)S(1)}, bf16[8,272,128]{2,1,0:T(8,128)(2,1)}, u32[]{:S(2)}, u32[]{:S(2)}) collective-permute-start(bf16[8,272,128]{2,1,0:T(8,128)(2,1)S(1)} %collective-permute-done.4.refs_4_), channel_id=1, source_target_pairs={{0,1},{1,0},{2,3},{3,2},{4,5},{5,4},{6,7},{7,6},{8,9},{9,8},{10,11... | collective-permute-start | bytes 1671176 | tf_op jit(solution)/shard_map/ppermute | solution.py:323
  48.1 10.2 %collective-permute-start.3 = (bf16[8,272,128]{2,1,0:T(8,128)(2,1)S(1)}, bf16[8,272,128]{2,1,0:T(8,128)(2,1)}, u32[]{:S(2)}, u32[]{:S(2)}) collective-permute-start(bf16[8,272,128]{2,1,0:T(8,128)(2,1)S(1)} %collective-permute-done.2.refs_2_), channel_id=1, source_target_pairs={{0,1},{1,0},{2,3},{3,2},{4,5},{5,4},{6,7},{7,6},{8,9},{9,8},{10,11... | collective-permute-start | bytes 1671176 | tf_op jit(solution)/shard_map/ppermute | solution.py:323
  53.1 5.1 %collective-permute-start.9 = (bf16[4,272,128]{2,1,0:T(8,128)(2,1)S(1)}, bf16[4,272,128]{2,1,0:T(8,128)(2,1)}, u32[]{:S(2)}, u32[]{:S(2)}) collective-permute-start(bf16[4,272,128]{2,1,0:T(8,128)(2,1)S(1)} %collective-permute-done.8.refs_8_), channel_id=1, source_target_pairs={{0,1},{1,0},{2,3},{3,2},{4,5},{5,4},{6,7},{7,6},{8,9},{9,8},{10,11... | collective-permute-start | bytes 835592 | tf_op jit(solution)/shard_map/ppermute | solution.py:323
  56.6 1.7 %collective-permute-start.7 = (bf16[4,272,128]{2,1,0:T(8,128)(2,1)S(1)}, bf16[4,272,128]{2,1,0:T(8,128)(2,1)}, u32[]{:S(2)}, u32[]{:S(2)}) collective-permute-start(bf16[4,272,128]{2,1,0:T(8,128)(2,1)S(1)} %collective-permute-done.6.refs_6_), channel_id=1, source_target_pairs={{0,1},{1,0},{2,3},{3,2},{4,5},{5,4},{6,7},{7,6},{8,9},{9,8},{10,11... | collective-permute-start | bytes 835592 | tf_op jit(solution)/shard_map/ppermute | solution.py:323
  58.3 1.1 copy-start.1
  59.4 1.1 copy-start.3
  89.3 2.2 %copy-start.4 = (bf16[8,256,128]{2,1,0:T(8,128)(2,1)}, bf16[8,256,128]{2,1,0:T(8,128)(2,1)S(1)}, u32[]{:S(2)}) copy-start(bf16[8,256,128]{2,1,0:T(8,128)(2,1)S(1)} %get-tuple-element.39) | copy-start | bytes 1572868
  89.3 2.2 %copy-start.6 = (bf16[8,256,128]{2,1,0:T(8,128)(2,1)}, bf16[8,256,128]{2,1,0:T(8,128)(2,1)S(1)}, u32[]{:S(2)}) copy-start(bf16[8,256,128]{2,1,0:T(8,128)(2,1)S(1)} %get-tuple-element.44) | copy-start | bytes 1572868
  89.3 2.0 %collective-permute-start.10 = (bf16[8,256,128]{2,1,0:T(8,128)(2,1)S(1)}, bf16[8,256,128]{2,1,0:T(8,128)(2,1)S(1)}, u32[]{:S(2)}, u32[]{:S(2)}) collective-permute-start(bf16[8,256,128]{2,1,0:T(8,128)(2,1)S(1)} %get-tuple-element.31), channel_id=1, source_target_pairs={{0,1},{1,0},{2,3},{3,2},{4,5},{5,4},{6,7},{7,6},{8,9},{9,8},{10,11... | collective-permute-start | bytes 1572872 | tf_op jit(solution)/shard_map/ppermute | solution.py:323
  91.5 10.4 %collective-permute-start.12 = (bf16[8,256,128]{2,1,0:T(8,128)(2,1)}, bf16[8,256,128]{2,1,0:T(8,128)(2,1)S(1)}, u32[]{:S(2)}, u32[]{:S(2)}) collective-permute-start(bf16[8,256,128]{2,1,0:T(8,128)(2,1)} %get-tuple-element.41), channel_id=1, source_target_pairs={{0,1},{1,0},{2,3},{3,2},{4,5},{5,4},{6,7},{7,6},{8,9},{9,8},{10,11... | collective-permute-start | bytes 1572872 | tf_op jit(solution)/shard_map/ppermute | solution.py:323
  92.2 5.8 %copy-start.7 = (bf16[8,256,128]{2,1,0:T(8,128)(2,1)S(1)}, bf16[8,256,128]{2,1,0:T(8,128)(2,1)}, u32[]{:S(2)}) copy-start(bf16[8,256,128]{2,1,0:T(8,128)(2,1)} %copy-done.6) | copy-start | bytes 1572868
  92.2 36.4 %all-to-all-start.2 = ((bf16[8,256,128]{2,1,0:T(8,128)(2,1)}), bf16[8,256,128]{2,1,0:T(8,128)(2,1)}, u32[]{:S(2)}, u32[]{:S(2)}) async-start(bf16[8,256,128]{2,1,0:T(8,128)(2,1)} %get-tuple-element.45), calls=%async_computation.2 | async-start | bytes 1048576 | tf_op jit(solution)/shard_map/all_to_all | solution.py:308
  97.9 3.8 %copy-start.5 = (bf16[8,256,128]{2,1,0:T(8,128)(2,1)S(1)}, bf16[8,256,128]{2,1,0:T(8,128)(2,1)}, u32[]{:S(2)}) copy-start(bf16[8,256,128]{2,1,0:T(8,128)(2,1)} %copy-done.4) | copy-start | bytes 1572868
  97.9 15.8 %collective-permute-start.15 = (bf16[8,256,128]{2,1,0:T(8,128)(2,1)S(1)}, bf16[8,256,128]{2,1,0:T(8,128)(2,1)S(1)}, u32[]{:S(2)}, u32[]{:S(2)}) collective-permute-start(bf16[8,256,128]{2,1,0:T(8,128)(2,1)S(1)} %copy-done.7), channel_id=1, source_target_pairs={{0,1},{1,0},{2,3},{3,2},{4,5},{5,4},{6,7},{7,6},{8,9},{9,8},{10,11... | collective-permute-start | bytes 1572872 | tf_op jit(solution)/shard_map/ppermute | solution.py:323
  98.1 10.5 %collective-permute-start.13 = (bf16[8,128,128]{2,1,0:T(8,128)(2,1)S(1)}, bf16[8,128,128]{2,1,0:T(8,128)(2,1)S(1)}, u32[]{:S(2)}, u32[]{:S(2)}) collective-permute-start(bf16[8,128,128]{2,1,0:T(8,128)(2,1)S(1)} %get-tuple-element.54), channel_id=1, source_target_pairs={{0,16},{16,32},{32,48},{48,0},{1,17},{17,33},{33,49},{49,1},{2,18}... | collective-permute-start | bytes 786440 | tf_op jit(solution)/shard_map/ppermute | solution.py:311
  99.3 15.8 %collective-permute-start.18 = (bf16[8,128,128]{2,1,0:T(8,128)(2,1)S(1)}, bf16[8,128,128]{2,1,0:T(8,128)(2,1)S(1)}, u32[]{:S(2)}, u32[]{:S(2)}) collective-permute-start(bf16[8,128,128]{2,1,0:T(8,128)(2,1)S(1)} %get-tuple-element.55), channel_id=1, source_target_pairs={{0,48},{16,0},{32,16},{48,32},{1,49},{17,1},{33,17},{49,33},{2,50}... | collective-permute-start | bytes 786440 | tf_op jit(solution)/shard_map/ppermute | solution.py:314
  101.7 15.6 %collective-permute-start.11 = (bf16[8,256,128]{2,1,0:T(8,128)(2,1)S(1)}, bf16[8,256,128]{2,1,0:T(8,128)(2,1)S(1)}, u32[]{:S(2)}, u32[]{:S(2)}) collective-permute-start(bf16[8,256,128]{2,1,0:T(8,128)(2,1)S(1)} %copy-done.5), channel_id=1, source_target_pairs={{0,1},{1,0},{2,3},{3,2},{4,5},{5,4},{6,7},{7,6},{8,9},{9,8},{10,11... | collective-permute-start | bytes 1572872 | tf_op jit(solution)/shard_map/ppermute | solution.py:323
  102.1 15.4 %collective-permute-start.17 = (bf16[8,128,128]{2,1,0:T(8,128)(2,1)S(1)}, bf16[8,128,128]{2,1,0:T(8,128)(2,1)S(1)}, u32[]{:S(2)}, u32[]{:S(2)}) collective-permute-start(bf16[8,128,128]{2,1,0:T(8,128)(2,1)S(1)} %slice.46), channel_id=1, source_target_pairs={{0,16},{16,32},{32,48},{48,0},{1,17},{17,33},{33,49},{49,1},{2,18}... | collective-permute-start | bytes 786440 | tf_op jit(solution)/shard_map/ppermute | solution.py:311
  108.6 12.3 %collective-permute-start.14 = (bf16[8,128,128]{2,1,0:T(8,128)(2,1)S(1)}, bf16[8,128,128]{2,1,0:T(8,128)(2,1)S(1)}, u32[]{:S(2)}, u32[]{:S(2)}) collective-permute-start(bf16[8,128,128]{2,1,0:T(8,128)(2,1)S(1)} %add_convert_fusion.7), channel_id=1, source_target_pairs={{0,16},{16,32},{32,48},{48,0},{1,17},{17,33},{33,49},{49,1},{2,18}... | collective-permute-start | bytes 786440 | tf_op jit(solution)/shard_map/ppermute | solution.py:311
  114.0 9.8 %collective-permute-start.16 = (bf16[8,128,128]{2,1,0:T(8,128)(2,1)S(1)}, bf16[8,128,128]{2,1,0:T(8,128)(2,1)S(1)}, u32[]{:S(2)}, u32[]{:S(2)}) collective-permute-start(bf16[8,128,128]{2,1,0:T(8,128)(2,1)S(1)} %slice.44), channel_id=1, source_target_pairs={{0,48},{16,0},{32,16},{48,32},{1,49},{17,1},{33,17},{49,33},{2,50}... | collective-permute-start | bytes 786440 | tf_op jit(solution)/shard_map/ppermute | solution.py:314
  115.2 12.2 %collective-permute-start.19 = (bf16[8,128,128]{2,1,0:T(8,128)(2,1)S(1)}, bf16[8,128,128]{2,1,0:T(8,128)(2,1)S(1)}, u32[]{:S(2)}, u32[]{:S(2)}) collective-permute-start(bf16[8,128,128]{2,1,0:T(8,128)(2,1)S(1)} %add_convert_fusion.5), channel_id=1, source_target_pairs={{0,48},{16,0},{32,16},{48,32},{1,49},{17,1},{33,17},{49,33},{2,50}... | collective-permute-start | bytes 786440 | tf_op jit(solution)/shard_map/ppermute | solution.py:314
  128.5 23.5 %all-to-all-start.3 = ((bf16[8,256,128]{2,1,0:T(8,128)(2,1)}), bf16[8,256,128]{2,1,0:T(8,128)(2,1)S(1)}, u32[]{:S(2)}, u32[]{:S(2)}) async-start(bf16[8,256,128]{2,1,0:T(8,128)(2,1)} %pad_maximum_fusion), calls=%async_computation.3 | async-start | bytes 1048576 | tf_op jit(solution)/shard_map/all_to_all | solution.py:308
  135.9 1.7 %collective-permute-start.20 = (bf16[8,256,128]{2,1,0:T(8,128)(2,1)}, bf16[8,256,128]{2,1,0:T(8,128)(2,1)S(1)}, u32[]{:S(2)}, u32[]{:S(2)}) collective-permute-start(bf16[8,256,128]{2,1,0:T(8,128)(2,1)} %all-to-all-done.2), channel_id=1, source_target_pairs={{0,0},{2,2},{4,4},{6,6},{8,56},{10,58},{12,60},{14,62},{16,16},{18... | collective-permute-start | bytes 1572872 | tf_op jit(solution)/shard_map/ppermute | solution.py:320
  (5 other events, 4.0 us)

commit v6 on v5

--- a/solution.py
+++ b/solution.py
@@ -256,7 +256,7 @@
             pltpu.SemaphoreType.DMA((N_PIECES,)),
             pltpu.SemaphoreType.DMA((1,)),
         ],
-        compiler_params=pltpu.CompilerParams(vmem_limit_bytes=38 * 1024 * 1024),
+        compiler_params=pltpu.CompilerParams(vmem_limit_bytes=34 * 1024 * 1024),
         cost_estimate=pl.CostEstimate(flops=8 * 10**9, bytes_accessed=10 * 2**20, transcendentals=5 * 10**6),
     )(at, *pieces, qd)
 
@@ -337,20 +337,21 @@
 
     ad, *grads = attention(at, pieces, qd)
 
-    ad_back = over_heads(ad)
     far = add(grads[4], twin(grads[5]))
     far, *grads = lax.optimization_barrier((far, *grads))
     sums = {distance: add(grads[2 * distance], twin(grads[2 * distance + 1])) for distance in (3, 1, 0)}
+    ad, sums[1], sums[3] = lax.optimization_barrier((ad, sums[1], sums[3]))
+    ad_back = over_heads(ad)
     k, v = slice(0, ROWS), slice(ROWS, 2 * ROWS)
     key_left = left(sums[3][:, k])
     key_relay = add(sums[1][:, k], right(far[:, k]))
     value_relay = add(sums[3][:, v], left(far[:, v]))
     key_right, value_left = right(key_relay), left(value_relay)
     value_right = right(sums[1][:, v])
+    key_right, ad_back = lax.optimization_barrier((key_right, ad_back))
     key_sum = add(sums[0][:, k], key_right, key_left)
     value_sum = add(sums[0][:, v], value_right, value_left)
     sums = jnp.concatenate([key_sum, value_sum], axis=1)
-    sums, ad_back = lax.optimization_barrier((sums, ad_back))
     return (*unpack(swap(ad_back)), *unpack(over_heads(sums), turned=True))
 
 

time: 157 us -> 158 us (level)
  the two profiles are of different devices: /device:TPU:16 before, /device:TPU:136 now
where the time goes in v6:
time: 158 us; the launch traced here: 156 us
  starting transfers between devices  56.8 us (36%)
  waiting for transfers between devices  54.9 us (35%)
  Pallas kernels  35.7 us (23%)
  local copies, waits for them, and re-layouts  4.81 us (3%)
  other arithmetic  2.86 us (2%)
    all_to_all x4, starting transfers between devices, over_heads(): return lax.all_to_all(arr, 'z', split_axis=0, concat_axis=0, tiled=True)  29 us
    pallas_call x1, Pallas kernels, attention(): pl.pallas_call(attention_kernel, out_shape=outs, in_specs=[pl.BlockSpec(m...  27.8 us
    ppermute x2, waiting for transfers between devices, swap(): return lax.ppermute(arr, ('x', 'z'), pairs)  26.6 us
    ppermute x5, waiting for transfers between devices, right(): return lax.ppermute(arr, 'x', [(i, (i + 1) % XS) for i in range(XS)])  18.1 us
    ppermute x5, starting transfers between devices, left(): return lax.ppermute(arr, 'x', [(i, (i + XS - 1) % XS) for i in range(XS)])  17.4 us
    ppermute x2, starting transfers between devices, swap(): return lax.ppermute(arr, ('x', 'z'), pairs)  6.58 us
    ppermute x5, waiting for transfers between devices, left(): return lax.ppermute(arr, 'x', [(i, (i + XS - 1) % XS) for i in range(XS)])  6.54 us
    pallas_call x2, Pallas kernels, unpack(): pl.pallas_call(kernel, out_shape=(rows,) * n, in_specs=[vmem], out_specs=...  4.01 us
  transfers between devices with their start and end apart: 25, of which 9 were waited for; matrix products, arithmetic and copies ran while one was open for 1% of the time, Pallas kernels for 3%

profile of v6, /device:TPU:136, one launch (start us, length us, event | category | flops | bytes accessed | tf_op | source)
XLA Modules:
  0.0 155.9 jit_solution(12988241425174886883)
XLA Ops:
  0.6 1.9 %shard_map.84 = bf16[8,272,128]{2,1,0:T(8,128)(2,1)} custom-call(bf16[1,128,1024]{2,1,0:T(8,128)(2,1)} %a_ref.2, bf16[1,128,1024]{2,1,0:T(8,128)(2,1)} %b_ref.2, s32[1,128]{1,0:T(1,128)} %scale_ref.3), custom_call_target="tpu_custom_call" | custom-call | tf_op jit(solution)/shard_map/pallas_call | solution.py:274
  2.6 7.2 %all-to-all-start = ((bf16[8,272,128]{2,1,0:T(8,128)(2,1)}), bf16[8,272,128]{2,1,0:T(8,128)(2,1)S(1)}, u32[]{:S(2)}, u32[]{:S(2)}) async-start(bf16[8,272,128]{2,1,0:T(8,128)(2,1)} %shard_map.84), calls=%async_computation | async-start | bytes 1114112 | tf_op jit(solution)/shard_map/all_to_all | solution.py:308
  9.8 2.0 %shard_map.85 = bf16[8,272,128]{2,1,0:T(8,128)(2,1)} custom-call(bf16[1,128,1024]{2,1,0:T(8,128)(2,1)} %a_ref.3, bf16[1,128,1024]{2,1,0:T(8,128)(2,1)} %b_ref.3, s32[1,128]{1,0:T(1,128)} %scale_ref.3), custom_call_target="tpu_custom_call" | custom-call | tf_op jit(solution)/shard_map/pallas_call | solution.py:274
  11.7 4.7 %collective-permute-start = (bf16[8,272,128]{2,1,0:T(8,128)(2,1)}, bf16[8,272,128]{2,1,0:T(8,128)(2,1)}, u32[]{:S(2)}, u32[]{:S(2)}) collective-permute-start(bf16[8,272,128]{2,1,0:T(8,128)(2,1)} %shard_map.85), channel_id=1, source_target_pairs={{0,0},{2,2},{4,4},{6,6},{8,56},{10,58},{12,60},{14,62},{16,16},{18... | collective-permute-start | bytes 1671176 | tf_op jit(solution)/shard_map/ppermute | solution.py:320
  16.4 12.6 %collective-permute-done = bf16[8,272,128]{2,1,0:T(8,128)(2,1)} collective-permute-done((bf16[8,272,128]{2,1,0:T(8,128)(2,1)}, bf16[8,272,128]{2,1,0:T(8,128)(2,1)}, u32[]{:S(2)}, u32[]{:S(2)}) %collective-permute-start) | collective-permute-done | bytes 557088 | tf_op jit(solution)/shard_map/ppermute | solution.py:320
  28.9 2.8 %collective-permute-start.4 = (bf16[8,272,128]{2,1,0:T(8,128)(2,1)S(1)}, bf16[8,272,128]{2,1,0:T(8,128)(2,1)S(1)}, u32[]{:S(2)}, u32[]{:S(2)}) collective-permute-start(bf16[8,272,128]{2,1,0:T(8,128)(2,1)S(1)} %all-to-all-done.refs_0_), channel_id=1, source_target_pairs={{0,48},{16,0},{32,16},{48,32},{1,49},{17,1},{33,17},{49,33},{2,50}... | collective-permute-start | bytes 1671176 | tf_op jit(solution)/shard_map/ppermute | solution.py:314
  31.7 7.2 %all-to-all-start.1 = ((bf16[8,272,128]{2,1,0:T(8,128)(2,1)}), bf16[8,272,128]{2,1,0:T(8,128)(2,1)S(1)}, u32[]{:S(2)}, u32[]{:S(2)}) async-start(bf16[8,272,128]{2,1,0:T(8,128)(2,1)} %collective-permute-done), calls=%async_computation.1 | async-start | bytes 1114112 | tf_op jit(solution)/shard_map/all_to_all | solution.py:308
  38.9 3.2 %collective-permute-done.4.refs_4_ = bf16[8,272,128]{2,1,0:T(8,128)(2,1)S(1)} collective-permute-done((bf16[8,272,128]{2,1,0:T(8,128)(2,1)S(1)}, bf16[8,272,128]{2,1,0:T(8,128)(2,1)S(1)}, u32[]{:S(2)}, u32[]{:S(2)}) %collective-permute-start.4) | collective-permute-done | bytes 557088 | tf_op jit(solution)/shard_map/ppermute | solution.py:314
  42.1 3.8 %collective-permute-start.8 = (bf16[4,272,128]{2,1,0:T(8,128)(2,1)S(1)}, bf16[4,272,128]{2,1,0:T(8,128)(2,1)S(1)}, u32[]{:S(2)}, u32[]{:S(2)}) collective-permute-start(bf16[4,272,128]{2,1,0:T(8,128)(2,1)S(1)} %slice.41), channel_id=1, source_target_pairs={{0,48},{16,0},{32,16},{48,32},{1,49},{17,1},{33,17},{49,33},{2,50}... | collective-permute-start | bytes 835592 | tf_op jit(solution)/shard_map/ppermute | solution.py:314
  46.6 3.3 %collective-permute-done.8.refs_8_ = bf16[4,272,128]{2,1,0:T(8,128)(2,1)S(1)} collective-permute-done((bf16[4,272,128]{2,1,0:T(8,128)(2,1)S(1)}, bf16[4,272,128]{2,1,0:T(8,128)(2,1)S(1)}, u32[]{:S(2)}, u32[]{:S(2)}) %collective-permute-start.8) | collective-permute-done | bytes 278560 | tf_op jit(solution)/shard_map/ppermute | solution.py:314
  50.7 3.2 %collective-permute-done.6.refs_6_ = bf16[4,272,128]{2,1,0:T(8,128)(2,1)} collective-permute-done((bf16[4,272,128]{2,1,0:T(8,128)(2,1)S(1)}, bf16[4,272,128]{2,1,0:T(8,128)(2,1)}, u32[]{:S(2)}, u32[]{:S(2)}) %collective-permute-start.6) | collective-permute-done | bytes 278560 | tf_op jit(solution)/shard_map/ppermute | solution.py:311
  54.0 1.8 %collective-permute-done.7.refs_7_ = bf16[4,272,128]{2,1,0:T(8,128)(2,1)} collective-permute-done((bf16[4,272,128]{2,1,0:T(8,128)(2,1)}, bf16[4,272,128]{2,1,0:T(8,128)(2,1)}, u32[]{:S(2)}, u32[]{:S(2)}) %collective-permute-start.7) | collective-permute-done | bytes 278560 | tf_op jit(solution)/shard_map/ppermute | solution.py:323
  55.8 1.0 copy-done.3
  56.7 27.8 %shard_map.86 = (bf16[8,256,128]{2,1,0:T(8,128)(2,1)}, bf16[8,256,128]{2,1,0:T(8,128)(2,1)S(1)}, bf16[8,256,128]{2,1,0:T(8,128)(2,1)S(1)}, bf16[8,256,128]{2,1,0...) custom-call(s32[2]{0:T(128)S(1)} %pad_add_fusion.at_ref, ...), custom_call_target="tpu_custom_call" | custom-call | flops 8000000000 | bytes 10485760 | tf_op jit(solution)/shard_map/pallas_call | solution.py:230
  84.8 1.8 %collective-permute-done.10 = bf16[8,256,128]{2,1,0:T(8,128)(2,1)S(1)} collective-permute-done((bf16[8,256,128]{2,1,0:T(8,128)(2,1)S(1)}, bf16[8,256,128]{2,1,0:T(8,128)(2,1)S(1)}, u32[]{:S(2)}, u32[]{:S(2)}) %collective-permute-start.10) | collective-permute-done | bytes 524320 | tf_op jit(solution)/shard_map/ppermute | solution.py:323
  87.5 0.7 fusion
  88.2 7.5 %collective-permute-start.19 = (bf16[8,128,128]{2,1,0:T(8,128)(2,1)S(1)}, bf16[8,128,128]{2,1,0:T(8,128)(2,1)S(1)}, u32[]{:S(2)}, u32[]{:S(2)}) collective-permute-start(bf16[8,128,128]{2,1,0:T(8,128)(2,1)S(1)} %get-tuple-element.60), channel_id=1, source_target_pairs={{0,48},{16,0},{32,16},{48,32},{1,49},{17,1},{33,17},{49,33},{2,50}... | collective-permute-start | bytes 786440 | tf_op jit(solution)/shard_map/ppermute | solution.py:314
  96.1 7.3 %all-to-all-start.2 = ((bf16[8,256,128]{2,1,0:T(8,128)(2,1)}), bf16[8,256,128]{2,1,0:T(8,128)(2,1)S(1)}, u32[]{:S(2)}, u32[]{:S(2)}) async-start(bf16[8,256,128]{2,1,0:T(8,128)(2,1)} %get-tuple-element.48), calls=%async_computation.2 | async-start | bytes 1048576 | tf_op jit(solution)/shard_map/all_to_all | solution.py:308
  103.6 0.7 slice.35
  104.3 3.2 %collective-permute-start.17 = (bf16[8,128,128]{2,1,0:T(8,128)(2,1)}, bf16[8,128,128]{2,1,0:T(8,128)(2,1)}, u32[]{:S(2)}, u32[]{:S(2)}) collective-permute-start(bf16[8,128,128]{2,1,0:T(8,128)(2,1)} %slice.35), channel_id=1, source_target_pairs={{0,48},{16,0},{32,16},{48,32},{1,49},{17,1},{33,17},{49,33},{2,50}... | collective-permute-start | bytes 786440 | tf_op jit(solution)/shard_map/ppermute | solution.py:314
  107.7 2.0 %collective-permute-start.18 = (bf16[8,128,128]{2,1,0:T(8,128)(2,1)S(1)}, bf16[8,128,128]{2,1,0:T(8,128)(2,1)S(1)}, u32[]{:S(2)}, u32[]{:S(2)}) collective-permute-start(bf16[8,128,128]{2,1,0:T(8,128)(2,1)S(1)} %slice.37), channel_id=1, source_target_pairs={{0,16},{16,32},{32,48},{48,0},{1,17},{17,33},{33,49},{49,1},{2,18}... | collective-permute-start | bytes 786440 | tf_op jit(solution)/shard_map/ppermute | solution.py:311
  109.7 4.4 %collective-permute-done.13 = bf16[8,128,128]{2,1,0:T(8,128)(2,1)S(1)} collective-permute-done((bf16[8,128,128]{2,1,0:T(8,128)(2,1)}, bf16[8,128,128]{2,1,0:T(8,128)(2,1)S(1)}, u32[]{:S(2)}, u32[]{:S(2)}) %collective-permute-start.13) | collective-permute-done | bytes 262176 | tf_op jit(solution)/shard_map/ppermute | solution.py:311
  114.4 10.5 %collective-permute-done.14 = bf16[8,128,128]{2,1,0:T(8,128)(2,1)} collective-permute-done((bf16[8,128,128]{2,1,0:T(8,128)(2,1)S(1)}, bf16[8,128,128]{2,1,0:T(8,128)(2,1)}, u32[]{:S(2)}, u32[]{:S(2)}) %collective-permute-start.14) | collective-permute-done | bytes 262176 | tf_op jit(solution)/shard_map/ppermute | solution.py:311
  125.0 1.2 add_convert_fusion.6
  126.2 0.8 pad_maximum_fusion
  127.0 7.2 %all-to-all-start.3 = ((bf16[8,256,128]{2,1,0:T(8,128)(2,1)}), bf16[8,256,128]{2,1,0:T(8,128)(2,1)S(1)}, u32[]{:S(2)}, u32[]{:S(2)}) async-start(bf16[8,256,128]{2,1,0:T(8,128)(2,1)} %pad_maximum_fusion), calls=%async_computation.3 | async-start | bytes 1048576 | tf_op jit(solution)/shard_map/all_to_all | solution.py:308
  134.2 1.9 %collective-permute-start.15 = (bf16[8,256,128]{2,1,0:T(8,128)(2,1)S(1)}, bf16[8,256,128]{2,1,0:T(8,128)(2,1)S(1)}, u32[]{:S(2)}, u32[]{:S(2)}) collective-permute-start(bf16[8,256,128]{2,1,0:T(8,128)(2,1)S(1)} %all-to-all-done.2), channel_id=1, source_target_pairs={{0,0},{2,2},{4,4},{6,6},{8,56},{10,58},{12,60},{14,62},{16,16},{18... | collective-permute-start | bytes 1572872 | tf_op jit(solution)/shard_map/ppermute | solution.py:320
  136.2 14.1 %collective-permute-done.15.in_ref = bf16[8,256,128]{2,1,0:T(8,128)(2,1)S(1)} collective-permute-done((bf16[8,256,128]{2,1,0:T(8,128)(2,1)S(1)}, bf16[8,256,128]{2,1,0:T(8,128)(2,1)S(1)}, u32[]{:S(2)}, u32[]{:S(2)}) %collective-permute-start.15) | collective-permute-done | bytes 524320 | tf_op jit(solution)/shard_map/ppermute | solution.py:320
  150.3 0.8 copy-done.5
  151.1 2.0 %shard_map.87 = (bf16[1,128,1024]{2,1,0:T(8,128)(2,1)}, bf16[1,128,1024]{2,1,0:T(8,128)(2,1)}) custom-call(bf16[8,256,128]{2,1,0:T(8,128)(2,1)} %copy-done.5), custom_call_target="tpu_custom_call" | custom-call | tf_op jit(solution)/shard_map/pallas_call | solution.py:296
  153.1 0.8 copy-done.4
  153.8 2.0 %shard_map.88 = (bf16[1,128,1024]{2,1,0:T(8,128)(2,1)}, bf16[1,128,1024]{2,1,0:T(8,128)(2,1)}) custom-call(bf16[8,256,128]{2,1,0:T(8,128)(2,1)} %copy-done.4), custom_call_target="tpu_custom_call" | custom-call | tf_op jit(solution)/shard_map/pallas_call | solution.py:296
  (49 shorter events, 3.6 us)
Async XLA Ops:
  2.6 26.4 %all-to-all-start = ((bf16[8,272,128]{2,1,0:T(8,128)(2,1)}), bf16[8,272,128]{2,1,0:T(8,128)(2,1)S(1)}, u32[]{:S(2)}, u32[]{:S(2)}) async-start(bf16[8,272,128]{2,1,0:T(8,128)(2,1)} %shard_map.84), calls=%async_computation | async-start | bytes 1114112 | tf_op jit(solution)/shard_map/all_to_all | solution.py:308
  11.7 17.2 %collective-permute-start = (bf16[8,272,128]{2,1,0:T(8,128)(2,1)}, bf16[8,272,128]{2,1,0:T(8,128)(2,1)}, u32[]{:S(2)}, u32[]{:S(2)}) collective-permute-start(bf16[8,272,128]{2,1,0:T(8,128)(2,1)} %shard_map.85), channel_id=1, source_target_pairs={{0,0},{2,2},{4,4},{6,6},{8,56},{10,58},{12,60},{14,62},{16,16},{18... | collective-permute-start | bytes 1671176 | tf_op jit(solution)/shard_map/ppermute | solution.py:320
  28.9 13.2 %collective-permute-start.4 = (bf16[8,272,128]{2,1,0:T(8,128)(2,1)S(1)}, bf16[8,272,128]{2,1,0:T(8,128)(2,1)S(1)}, u32[]{:S(2)}, u32[]{:S(2)}) collective-permute-start(bf16[8,272,128]{2,1,0:T(8,128)(2,1)S(1)} %all-to-all-done.refs_0_), channel_id=1, source_target_pairs={{0,48},{16,0},{32,16},{48,32},{1,49},{17,1},{33,17},{49,33},{2,50}... | collective-permute-start | bytes 1671176 | tf_op jit(solution)/shard_map/ppermute | solution.py:314
  31.7 14.2 %collective-permute-start.2 = (bf16[8,272,128]{2,1,0:T(8,128)(2,1)S(1)}, bf16[8,272,128]{2,1,0:T(8,128)(2,1)S(1)}, u32[]{:S(2)}, u32[]{:S(2)}) collective-permute-start(bf16[8,272,128]{2,1,0:T(8,128)(2,1)S(1)} %all-to-all-done.refs_0_), channel_id=1, source_target_pairs={{0,16},{16,32},{32,48},{48,0},{1,17},{17,33},{33,49},{49,1},{2,18}... | collective-permute-start | bytes 1671176 | tf_op jit(solution)/shard_map/ppermute | solution.py:311
  31.7 22.2 %all-to-all-start.1 = ((bf16[8,272,128]{2,1,0:T(8,128)(2,1)}), bf16[8,272,128]{2,1,0:T(8,128)(2,1)S(1)}, u32[]{:S(2)}, u32[]{:S(2)}) async-start(bf16[8,272,128]{2,1,0:T(8,128)(2,1)} %collective-permute-done), calls=%async_computation.1 | async-start | bytes 1114112 | tf_op jit(solution)/shard_map/all_to_all | solution.py:308
  38.9 15.0 %collective-permute-start.1 = (bf16[8,272,128]{2,1,0:T(8,128)(2,1)S(1)}, bf16[8,272,128]{2,1,0:T(8,128)(2,1)S(1)}, u32[]{:S(2)}, u32[]{:S(2)}) collective-permute-start(bf16[8,272,128]{2,1,0:T(8,128)(2,1)S(1)} %all-to-all-done.refs_0_), channel_id=1, source_target_pairs={{0,1},{1,0},{2,3},{3,2},{4,5},{5,4},{6,7},{7,6},{8,9},{9,8},{10,11... | collective-permute-start | bytes 1671176 | tf_op jit(solution)/shard_map/ppermute | solution.py:323
  42.1 7.8 %collective-permute-start.8 = (bf16[4,272,128]{2,1,0:T(8,128)(2,1)S(1)}, bf16[4,272,128]{2,1,0:T(8,128)(2,1)S(1)}, u32[]{:S(2)}, u32[]{:S(2)}) collective-permute-start(bf16[4,272,128]{2,1,0:T(8,128)(2,1)S(1)} %slice.41), channel_id=1, source_target_pairs={{0,48},{16,0},{32,16},{48,32},{1,49},{17,1},{33,17},{49,33},{2,50}... | collective-permute-start | bytes 835592 | tf_op jit(solution)/shard_map/ppermute | solution.py:314
  45.9 7.9 %collective-permute-start.6 = (bf16[4,272,128]{2,1,0:T(8,128)(2,1)S(1)}, bf16[4,272,128]{2,1,0:T(8,128)(2,1)}, u32[]{:S(2)}, u32[]{:S(2)}) collective-permute-start(bf16[4,272,128]{2,1,0:T(8,128)(2,1)S(1)} %slice.40), channel_id=1, source_target_pairs={{0,16},{16,32},{32,48},{48,0},{1,17},{17,33},{33,49},{49,1},{2,18}... | collective-permute-start | bytes 835592 | tf_op jit(solution)/shard_map/ppermute | solution.py:311
  46.0 9.8 %collective-permute-start.5 = (bf16[8,272,128]{2,1,0:T(8,128)(2,1)S(1)}, bf16[8,272,128]{2,1,0:T(8,128)(2,1)}, u32[]{:S(2)}, u32[]{:S(2)}) collective-permute-start(bf16[8,272,128]{2,1,0:T(8,128)(2,1)S(1)} %collective-permute-done.4.refs_4_), channel_id=1, source_target_pairs={{0,1},{1,0},{2,3},{3,2},{4,5},{5,4},{6,7},{7,6},{8,9},{9,8},{10,11... | collective-permute-start | bytes 1671176 | tf_op jit(solution)/shard_map/ppermute | solution.py:323
  46.1 9.7 %collective-permute-start.3 = (bf16[8,272,128]{2,1,0:T(8,128)(2,1)S(1)}, bf16[8,272,128]{2,1,0:T(8,128)(2,1)}, u32[]{:S(2)}, u32[]{:S(2)}) collective-permute-start(bf16[8,272,128]{2,1,0:T(8,128)(2,1)S(1)} %collective-permute-done.2.refs_2_), channel_id=1, source_target_pairs={{0,1},{1,0},{2,3},{3,2},{4,5},{5,4},{6,7},{7,6},{8,9},{9,8},{10,11... | collective-permute-start | bytes 1671176 | tf_op jit(solution)/shard_map/ppermute | solution.py:323
  50.0 4.0 %collective-permute-start.9 = (bf16[4,272,128]{2,1,0:T(8,128)(2,1)S(1)}, bf16[4,272,128]{2,1,0:T(8,128)(2,1)}, u32[]{:S(2)}, u32[]{:S(2)}) collective-permute-start(bf16[4,272,128]{2,1,0:T(8,128)(2,1)S(1)} %collective-permute-done.8.refs_8_), channel_id=1, source_target_pairs={{0,1},{1,0},{2,3},{3,2},{4,5},{5,4},{6,7},{7,6},{8,9},{9,8},{10,11... | collective-permute-start | bytes 835592 | tf_op jit(solution)/shard_map/ppermute | solution.py:323
  50.0 0.7 copy-start.2
  53.9 1.9 %collective-permute-start.7 = (bf16[4,272,128]{2,1,0:T(8,128)(2,1)}, bf16[4,272,128]{2,1,0:T(8,128)(2,1)}, u32[]{:S(2)}, u32[]{:S(2)}) collective-permute-start(bf16[4,272,128]{2,1,0:T(8,128)(2,1)} %collective-permute-done.6.refs_6_), channel_id=1, source_target_pairs={{0,1},{1,0},{2,3},{3,2},{4,5},{5,4},{6,7},{7,6},{8,9},{9,8},{10,11... | collective-permute-start | bytes 835592 | tf_op jit(solution)/shard_map/ppermute | solution.py:323
  55.8 1.0 copy-start.3
  84.6 2.2 %copy-start = (bf16[8,256,128]{2,1,0:T(8,128)(2,1)}, bf16[8,256,128]{2,1,0:T(8,128)(2,1)S(1)}, u32[]{:S(2)}) copy-start(bf16[8,256,128]{2,1,0:T(8,128)(2,1)S(1)} %get-tuple-element.53) | copy-start | bytes 1572868
  84.6 2.0 %collective-permute-start.10 = (bf16[8,256,128]{2,1,0:T(8,128)(2,1)S(1)}, bf16[8,256,128]{2,1,0:T(8,128)(2,1)S(1)}, u32[]{:S(2)}, u32[]{:S(2)}) collective-permute-start(bf16[8,256,128]{2,1,0:T(8,128)(2,1)S(1)} %get-tuple-element.35), channel_id=1, source_target_pairs={{0,1},{1,0},{2,3},{3,2},{4,5},{5,4},{6,7},{7,6},{8,9},{9,8},{10,11... | collective-permute-start | bytes 1572872 | tf_op jit(solution)/shard_map/ppermute | solution.py:323
  86.7 9.0 %collective-permute-start.11 = (bf16[8,256,128]{2,1,0:T(8,128)(2,1)S(1)}, bf16[8,256,128]{2,1,0:T(8,128)(2,1)S(1)}, u32[]{:S(2)}, u32[]{:S(2)}) collective-permute-start(bf16[8,256,128]{2,1,0:T(8,128)(2,1)S(1)} %get-tuple-element.43), channel_id=1, source_target_pairs={{0,1},{1,0},{2,3},{3,2},{4,5},{5,4},{6,7},{7,6},{8,9},{9,8},{10,11... | collective-permute-start | bytes 1572872 | tf_op jit(solution)/shard_map/ppermute | solution.py:323
  87.1 8.8 %collective-permute-start.12 = (bf16[8,256,128]{2,1,0:T(8,128)(2,1)S(1)}, bf16[8,256,128]{2,1,0:T(8,128)(2,1)S(1)}, u32[]{:S(2)}, u32[]{:S(2)}) collective-permute-start(bf16[8,256,128]{2,1,0:T(8,128)(2,1)S(1)} %get-tuple-element.45), channel_id=1, source_target_pairs={{0,1},{1,0},{2,3},{3,2},{4,5},{5,4},{6,7},{7,6},{8,9},{9,8},{10,11... | collective-permute-start | bytes 1572872 | tf_op jit(solution)/shard_map/ppermute | solution.py:323
  88.2 19.3 %collective-permute-start.19 = (bf16[8,128,128]{2,1,0:T(8,128)(2,1)S(1)}, bf16[8,128,128]{2,1,0:T(8,128)(2,1)S(1)}, u32[]{:S(2)}, u32[]{:S(2)}) collective-permute-start(bf16[8,128,128]{2,1,0:T(8,128)(2,1)S(1)} %get-tuple-element.60), channel_id=1, source_target_pairs={{0,48},{16,0},{32,16},{48,32},{1,49},{17,1},{33,17},{49,33},{2,50}... | collective-permute-start | bytes 786440 | tf_op jit(solution)/shard_map/ppermute | solution.py:314
  96.1 7.4 %copy-start.1 = (bf16[8,256,128]{2,1,0:T(8,128)(2,1)S(1)}, bf16[8,256,128]{2,1,0:T(8,128)(2,1)}, u32[]{:S(2)}) copy-start(bf16[8,256,128]{2,1,0:T(8,128)(2,1)} %copy-done) | copy-start | bytes 1572868
  96.1 28.9 %all-to-all-start.2 = ((bf16[8,256,128]{2,1,0:T(8,128)(2,1)}), bf16[8,256,128]{2,1,0:T(8,128)(2,1)S(1)}, u32[]{:S(2)}, u32[]{:S(2)}) async-start(bf16[8,256,128]{2,1,0:T(8,128)(2,1)} %get-tuple-element.48), calls=%async_computation.2 | async-start | bytes 1048576 | tf_op jit(solution)/shard_map/all_to_all | solution.py:308
  103.4 10.8 %collective-permute-start.16 = (bf16[8,256,128]{2,1,0:T(8,128)(2,1)S(1)}, bf16[8,256,128]{2,1,0:T(8,128)(2,1)S(1)}, u32[]{:S(2)}, u32[]{:S(2)}) collective-permute-start(bf16[8,256,128]{2,1,0:T(8,128)(2,1)S(1)} %copy-done.1), channel_id=1, source_target_pairs={{0,1},{1,0},{2,3},{3,2},{4,5},{5,4},{6,7},{7,6},{8,9},{9,8},{10,11... | collective-permute-start | bytes 1572872 | tf_op jit(solution)/shard_map/ppermute | solution.py:323
  103.4 10.6 %collective-permute-start.13 = (bf16[8,128,128]{2,1,0:T(8,128)(2,1)}, bf16[8,128,128]{2,1,0:T(8,128)(2,1)S(1)}, u32[]{:S(2)}, u32[]{:S(2)}) collective-permute-start(bf16[8,128,128]{2,1,0:T(8,128)(2,1)} %get-tuple-element.61), channel_id=1, source_target_pairs={{0,16},{16,32},{32,48},{48,0},{1,17},{17,33},{33,49},{49,1},{2,18}... | collective-permute-start | bytes 786440 | tf_op jit(solution)/shard_map/ppermute | solution.py:311
  104.3 20.7 %collective-permute-start.17 = (bf16[8,128,128]{2,1,0:T(8,128)(2,1)}, bf16[8,128,128]{2,1,0:T(8,128)(2,1)}, u32[]{:S(2)}, u32[]{:S(2)}) collective-permute-start(bf16[8,128,128]{2,1,0:T(8,128)(2,1)} %slice.35), channel_id=1, source_target_pairs={{0,48},{16,0},{32,16},{48,32},{1,49},{17,1},{33,17},{49,33},{2,50}... | collective-permute-start | bytes 786440 | tf_op jit(solution)/shard_map/ppermute | solution.py:314
  107.6 17.4 %collective-permute-start.20 = (bf16[8,128,128]{2,1,0:T(8,128)(2,1)S(1)}, bf16[8,128,128]{2,1,0:T(8,128)(2,1)S(1)}, u32[]{:S(2)}, u32[]{:S(2)}) collective-permute-start(bf16[8,128,128]{2,1,0:T(8,128)(2,1)S(1)} %add_convert_fusion.5), channel_id=1, source_target_pairs={{0,48},{16,0},{32,16},{48,32},{1,49},{17,1},{33,17},{49,33},{2,50}... | collective-permute-start | bytes 786440 | tf_op jit(solution)/shard_map/ppermute | solution.py:314
  107.7 17.3 %collective-permute-start.18 = (bf16[8,128,128]{2,1,0:T(8,128)(2,1)S(1)}, bf16[8,128,128]{2,1,0:T(8,128)(2,1)S(1)}, u32[]{:S(2)}, u32[]{:S(2)}) collective-permute-start(bf16[8,128,128]{2,1,0:T(8,128)(2,1)S(1)} %slice.37), channel_id=1, source_target_pairs={{0,16},{16,32},{32,48},{48,0},{1,17},{17,33},{33,49},{49,1},{2,18}... | collective-permute-start | bytes 786440 | tf_op jit(solution)/shard_map/ppermute | solution.py:311
  114.1 10.8 %collective-permute-start.14 = (bf16[8,128,128]{2,1,0:T(8,128)(2,1)S(1)}, bf16[8,128,128]{2,1,0:T(8,128)(2,1)}, u32[]{:S(2)}, u32[]{:S(2)}) collective-permute-start(bf16[8,128,128]{2,1,0:T(8,128)(2,1)S(1)} %add_convert_fusion.7), channel_id=1, source_target_pairs={{0,16},{16,32},{32,48},{48,0},{1,17},{17,33},{33,49},{49,1},{2,18}... | collective-permute-start | bytes 786440 | tf_op jit(solution)/shard_map/ppermute | solution.py:311
  127.0 26.0 %all-to-all-start.3 = ((bf16[8,256,128]{2,1,0:T(8,128)(2,1)}), bf16[8,256,128]{2,1,0:T(8,128)(2,1)S(1)}, u32[]{:S(2)}, u32[]{:S(2)}) async-start(bf16[8,256,128]{2,1,0:T(8,128)(2,1)} %pad_maximum_fusion), calls=%async_computation.3 | async-start | bytes 1048576 | tf_op jit(solution)/shard_map/all_to_all | solution.py:308
  134.2 16.0 %collective-permute-start.15 = (bf16[8,256,128]{2,1,0:T(8,128)(2,1)S(1)}, bf16[8,256,128]{2,1,0:T(8,128)(2,1)S(1)}, u32[]{:S(2)}, u32[]{:S(2)}) collective-permute-start(bf16[8,256,128]{2,1,0:T(8,128)(2,1)S(1)} %all-to-all-done.2), channel_id=1, source_target_pairs={{0,0},{2,2},{4,4},{6,6},{8,56},{10,58},{12,60},{14,62},{16,16},{18... | collective-permute-start | bytes 1572872 | tf_op jit(solution)/shard_map/ppermute | solution.py:320
  150.3 0.8 copy-start.5
  153.0 0.8 copy-start.4

commit v7 on v6

--- a/solution.py
+++ b/solution.py
@@ -17,7 +17,7 @@
 KB = 512
 SLAB = 256
 GROUP = 32
-COLS = tuple(slice(i, i + SLAB) for i in range(0, QB, SLAB))
+ALL, LATE = slice(0, QB), slice(QB // 2, QB)
 STEPS = CHUNKS * ROWS // KB
 INV_ROOT = HDIM ** -0.5
 LOG2E = 1.4426950408889634
@@ -33,6 +33,10 @@
 
 PIECES = ((0, 0, 8), (3, 0, 8), (1, 0, 8), (2, 0, 4), (2, 4, 4))
 N_PIECES = 2 * len(PIECES)
+
+
+def columns(wide):
+    return [slice(i, i + SLAB) for i in range(wide.start, wide.stop, SLAB)]
 
 
 def attention_kernel(at_ref, *refs):
@@ -92,12 +96,19 @@
         own = qd_ref[pl.ds(first, QB // ROWS), 256:272, :].astype(jnp.float32)[:, 0, :]
         for i in range(QB // ROWS):
             qs_scr[:, i * ROWS : (i + 1) * ROWS] = jnp.broadcast_to(own[i : i + 1, :], (8, ROWS))
-        low, high = jnp.min(own), jnp.max(own)
-        n_steps = jnp.sum(jnp.where(is_first & (key_scales <= high), 1.0, 0.0)).astype(jnp.int32)
-        n_steps = jnp.maximum(n_steps, 2)
-        n_full = jnp.sum(jnp.where(is_last & (key_scales <= low), 1.0, 0.0)).astype(jnp.int32)
-
-        def scores(masked, step):
+        late = own[QB // ROWS // 2 :, :]
+
+        def needed(rows):
+            return jnp.sum(jnp.where(is_first & (key_scales <= jnp.max(rows)), 1.0, 0.0)).astype(jnp.int32)
+
+        def open_to(rows):
+            return jnp.sum(jnp.where(is_last & (key_scales <= jnp.min(rows)), 1.0, 0.0)).astype(jnp.int32)
+
+        n_wide = jnp.maximum(needed(own[: QB // ROWS // 2, :]), 2)
+        n_steps = jnp.maximum(needed(late), n_wide)
+        n_wide = jnp.where(n_steps - n_wide == 1, n_steps, n_wide)
+
+        def scores(wide, masked, step):
             for half in range(KB // SLAB):
                 k = slab(step, half, 0)
                 if masked:
@@ -105,7 +116,7 @@
                         down(kvs_ref[parts(step)[half] + i, 256:272, :].astype(jnp.float32)[0:1, :])
                         for i in range(SLAB // ROWS)
                     ]
-                for cols in COLS:
+                for cols in columns(wide):
                     s = dot(k, q_scr[cols, :], NT)
                     for r in range(0, SLAB, GROUP):
                         tile = s[r : r + GROUP, :]
@@ -130,45 +141,53 @@
         sum_scr[...] = jnp.zeros_like(sum_scr)
         acc_scr[...] = jnp.zeros_like(acc_scr)
 
-        def weigh(step):
+        def weigh(wide, step):
             for half in range(KB // SLAB):
                 own = slice(half * SLAB, (half + 1) * SLAB)
-                acc_scr[...] += dot(slab(step, half, 128), now_scr[own, :], TN)
-
-        def exponentials(step):
-            top = fold(s_scr[0:GROUP, :], jnp.max)
+                acc_scr[:, wide] += dot(slab(step, half, 128), now_scr[own, wide], TN)
+
+        def exponentials(wide, step):
+            top = fold(s_scr[0:GROUP, wide], jnp.max)
             for r in range(GROUP, KB, GROUP):
-                top = jnp.maximum(top, fold(s_scr[r : r + GROUP, :], jnp.max))
+                top = jnp.maximum(top, fold(s_scr[r : r + GROUP, wide], jnp.max))
             top = jnp.ceil(jnp.max(top, axis=0, keepdims=True) * (INV_ROOT * LOG2E))
-            top = jnp.maximum(top_scr[0:1, :], top)
-            drop = jnp.exp2(top_scr[0:1, :] - top)
-            top_scr[...] = jnp.broadcast_to(top, top_scr.shape)
-            tops_scr[step] = jnp.broadcast_to(top, top_scr.shape)
-            acc_scr[...] = acc_scr[...] * drop
-            total = sum_scr[...] * drop
+            top = jnp.maximum(top_scr[0:1, wide], top)
+            drop = jnp.exp2(top_scr[0:1, wide] - top)
+            top_scr[:, wide] = jnp.broadcast_to(top, (8, top.shape[1]))
+            tops_scr[step, :, wide] = jnp.broadcast_to(top, (8, top.shape[1]))
+            acc_scr[:, wide] = acc_scr[:, wide] * drop
+            total = sum_scr[:, wide] * drop
             for r in range(0, KB, GROUP):
-                e = jnp.exp2(s_scr[r : r + GROUP, :] * (INV_ROOT * LOG2E) - top)
+                e = jnp.exp2(s_scr[r : r + GROUP, wide] * (INV_ROOT * LOG2E) - top)
                 total = total + fold(e, jnp.sum)
                 e = e.astype(jnp.bfloat16)
-                now_scr[r : r + GROUP, :] = e
-                e_scr[step, r : r + GROUP, :] = e
-            sum_scr[...] = total
-
-        def forward(masked, step, _):
-            weigh(step - 1)
-            exponentials(step)
-            scores(masked, step + 1)
+                now_scr[r : r + GROUP, wide] = e
+                e_scr[step, r : r + GROUP, wide] = e
+            sum_scr[:, wide] = total
+
+        def forward(wide, masked, step, _):
+            weigh(wide, step - 1)
+            exponentials(wide, step)
+            scores(wide, masked, step + 1)
             return 0
 
-        scores(True, 0)
-        exponentials(0)
-        scores(True, 1)
-        n_open = jnp.maximum(n_full - 1, 1)
-        lax.fori_loop(1, n_open, functools.partial(forward, False), 0)
-        lax.fori_loop(n_open, n_steps - 1, functools.partial(forward, True), 0)
-        weigh(n_steps - 2)
-        exponentials(n_steps - 1)
-        weigh(n_steps - 1)
+        def forward_pass(wide, start, n_open, end):
+            scores(wide, True, start)
+            exponentials(wide, start)
+            scores(wide, True, start + 1)
+            n_open = jnp.minimum(jnp.maximum(n_open - 1, start + 1), end - 1)
+            lax.fori_loop(start + 1, n_open, functools.partial(forward, wide, False), 0)
+            lax.fori_loop(n_open, end - 1, functools.partial(forward, wide, True), 0)
+            weigh(wide, end - 2)
+            exponentials(wide, end - 1)
+            weigh(wide, end - 1)
+
+        forward_pass(ALL, 0, open_to(own), n_wide)
+
+        @pl.when(n_steps > n_wide)
+        def _():
+            forward_pass(LATE, n_wide, open_to(late), n_steps)
+
         inv = 1.0 / jnp.sum(sum_scr[...], axis=0, keepdims=True)
         attn = (acc_scr[...] * inv).T
         inv_rows = jnp.broadcast_to(inv, (HDIM, QB)).T
@@ -181,34 +200,42 @@
         delta_scr[...] = jnp.broadcast_to(delta, (QB, HDIM)).T[0:8, :]
         dq_scr[...] = jnp.zeros_like(dq_scr)
 
-        def dprobs(step):
+        def dprobs(wide, step):
             for half in range(KB // SLAB):
                 v = slab(step, half, 128)
-                for cols in COLS:
+                for cols in columns(wide):
                     dp_scr[half * SLAB : (half + 1) * SLAB, cols] = dot(v, don_scr[cols, :], NT)
 
-        def backward(step, _):
-            drop = jnp.exp2(tops_scr[step, 0:1, :] - top_scr[0:1, :])
-            delta = delta_scr[0:1, :]
+        def backward(wide, step, _):
+            drop = jnp.exp2(tops_scr[step, 0:1, wide] - top_scr[0:1, wide])
+            delta = delta_scr[0:1, wide]
             for r in range(0, KB, GROUP):
-                e = e_scr[step, r : r + GROUP, :].astype(jnp.float32) * drop
-                now_scr[r : r + GROUP, :] = e.astype(jnp.bfloat16)
-                ds_scr[r : r + GROUP, :] = (e * (dp_scr[r : r + GROUP, :] - delta)).astype(jnp.bfloat16)
+                e = e_scr[step, r : r + GROUP, wide].astype(jnp.float32) * drop
+                now_scr[r : r + GROUP, wide] = e.astype(jnp.bfloat16)
+                ds_scr[r : r + GROUP, wide] = (e * (dp_scr[r : r + GROUP, wide] - delta)).astype(jnp.bfloat16)
             for half in range(KB // SLAB):
-                dv = dot(dont_scr[...], now_scr[half * SLAB : (half + 1) * SLAB, :], NT)
+                dv = dot(dont_scr[:, wide], now_scr[half * SLAB : (half + 1) * SLAB, wide], NT)
                 for i in range(SLAB // ROWS):
                     dv_scr[parts(step)[half] + i] += dv[:, i * ROWS : (i + 1) * ROWS]
-            dprobs(jnp.minimum(step + 1, STEPS - 1))
+            dprobs(wide, jnp.minimum(step + 1, STEPS - 1))
             for half in range(KB // SLAB):
                 own = slice(half * SLAB, (half + 1) * SLAB)
-                dk = dot(qt_scr[...], ds_scr[own, :], NT)
+                dk = dot(qt_scr[:, wide], ds_scr[own, wide], NT)
                 for i in range(SLAB // ROWS):
                     dk_scr[parts(step)[half] + i] += dk[:, i * ROWS : (i + 1) * ROWS]
-                dq_scr[...] += dot(slab(step, half, 0), ds_scr[own, :], TN)
+                dq_scr[:, wide] += dot(slab(step, half, 0), ds_scr[own, wide], TN)
             return 0
 
-        dprobs(0)
-        lax.fori_loop(0, n_steps, backward, 0)
+        def backward_pass(wide, start, end):
+            dprobs(wide, start)
+            lax.fori_loop(start, end, functools.partial(backward, wide), 0)
+
+        backward_pass(ALL, 0, n_wide)
+
+        @pl.when(n_steps > n_wide)
+        def _():
+            backward_pass(LATE, n_wide, n_steps)
+
         dq = (dq_scr[...] * INV_ROOT).T.astype(jnp.bfloat16)
         for i in range(QB // ROWS):
             ad_ref[first + i, 128:256, :] = dq[i * ROWS : (i + 1) * ROWS, :]
@@ -279,21 +306,33 @@
     )(a, b, scale_ids)
 
 
-def unpack_kernel(in_ref, *outs, turned):
-    for h in range(HEADS):
-        for i, out in enumerate(outs):
-            tile = in_ref[h, i * ROWS : (i + 1) * ROWS, :]
-            if turned:
-                tile = tile.astype(jnp.float32).T.astype(jnp.bfloat16)
-            out[0, :, h * HDIM : (h + 1) * HDIM] = tile
-
-
-def unpack(arr, turned=False):
+def unpack_kernel(ad_ref, dkv_ref, attn_ref, dq_ref, dk_ref, dv_ref, buf, sems):
+    copies = [pltpu.make_async_copy(ref, buf.at[i], sems.at[i]) for i, ref in enumerate((ad_ref, dkv_ref))]
+    for copy in copies:
+        copy.start()
+    for which, outs in enumerate(((attn_ref, dq_ref), (dk_ref, dv_ref))):
+        copies[which].wait()
+        for h in range(HEADS):
+            for i, out in enumerate(outs):
+                tile = buf[which, h, i * ROWS : (i + 1) * ROWS, :]
+                if which:
+                    tile = tile.astype(jnp.float32).T.astype(jnp.bfloat16)
+                out[0, :, h * HDIM : (h + 1) * HDIM] = tile
+
+
+def unpack(ad, dkv):
     vmem = pl.BlockSpec(memory_space=pltpu.VMEM)
     rows = jax.ShapeDtypeStruct((1, ROWS, HEADS * HDIM), jnp.bfloat16)
-    n = arr.shape[1] // ROWS
-    kernel = functools.partial(unpack_kernel, turned=turned)
-    return pl.pallas_call(kernel, out_shape=(rows,) * n, in_specs=[vmem], out_specs=(vmem,) * n)(arr)
+    return pl.pallas_call(
+        unpack_kernel,
+        out_shape=(rows,) * 4,
+        in_specs=[pl.BlockSpec(memory_space=pl.ANY)] * 2,
+        out_specs=(vmem,) * 4,
+        scratch_shapes=[
+            pltpu.VMEM((2, HEADS, 2 * ROWS, HDIM), jnp.bfloat16),
+            pltpu.SemaphoreType.DMA((2,)),
+        ],
+    )(ad, dkv)
 
 
 def add(*arrs):
@@ -352,7 +391,7 @@
     key_sum = add(sums[0][:, k], key_right, key_left)
     value_sum = add(sums[0][:, v], value_right, value_left)
     sums = jnp.concatenate([key_sum, value_sum], axis=1)
-    return (*unpack(swap(ad_back)), *unpack(over_heads(sums), turned=True))
+    return unpack(swap(ad_back), over_heads(sums))
 
 
 def solution(mesh):

time: 158 us -> 157 us (level)
  the two profiles are of different devices: /device:TPU:136 before, /device:TPU:24 now
where the time goes in v7:
time: 157 us; the launch traced here: 154 us
  starting transfers between devices  56.3 us (36%)
  waiting for transfers between devices  56 us (36%)
  Pallas kernels  34.1 us (22%)
  local copies, waits for them, and re-layouts  4.03 us (3%)
  other arithmetic  2.87 us (2%)
    all_to_all x4, starting transfers between devices, over_heads(): return lax.all_to_all(arr, 'z', split_axis=0, concat_axis=0, tiled=True)  29.2 us
    pallas_call x1, Pallas kernels, attention(): pl.pallas_call(attention_kernel, out_shape=outs, in_specs=[pl.BlockSpec(m...  28 us
    all_to_all x4, waiting for transfers between devices, over_heads(): return lax.all_to_all(arr, 'z', split_axis=0, concat_axis=0, tiled=True)  26.6 us
    ppermute x5, waiting for transfers between devices, right(): return lax.ppermute(arr, 'x', [(i, (i + 1) % XS) for i in range(XS)])  17.6 us
    ppermute x5, starting transfers between devices, left(): return lax.ppermute(arr, 'x', [(i, (i + XS - 1) % XS) for i in range(XS)])  16.7 us
    ppermute x5, waiting for transfers between devices, left(): return lax.ppermute(arr, 'x', [(i, (i + XS - 1) % XS) for i in range(XS)])  8.41 us
    ppermute x2, starting transfers between devices, swap(): return lax.ppermute(arr, ('x', 'z'), pairs)  6.52 us
    pallas_call x2, Pallas kernels, pack(): pl.pallas_call(pack_kernel, out_shape=jax.ShapeDtypeStruct((HEADS, 2 * RO...  3.88 us
  transfers between devices with their start and end apart: 25, of which 9 were waited for; matrix products, arithmetic and copies ran while one was open for 1% of the time, Pallas kernels for 1%

profile of v7, /device:TPU:24, one launch (start us, length us, event | category | flops | bytes accessed | tf_op | source)
XLA Modules:
  0.0 154.3 jit_solution(1915490370439925353)
XLA Ops:
  0.6 1.9 %shard_map.84 = bf16[8,272,128]{2,1,0:T(8,128)(2,1)} custom-call(bf16[1,128,1024]{2,1,0:T(8,128)(2,1)} %a_ref.2, bf16[1,128,1024]{2,1,0:T(8,128)(2,1)} %b_ref.2, s32[1,128]{1,0:T(1,128)} %scale_ref.3), custom_call_target="tpu_custom_call" | custom-call | tf_op jit(solution)/shard_map/pallas_call | solution.py:301
  2.6 8.5 %all-to-all-start = ((bf16[8,272,128]{2,1,0:T(8,128)(2,1)}), bf16[8,272,128]{2,1,0:T(8,128)(2,1)S(1)}, u32[]{:S(2)}, u32[]{:S(2)}) async-start(bf16[8,272,128]{2,1,0:T(8,128)(2,1)} %shard_map.84), calls=%async_computation | async-start | bytes 1114112 | tf_op jit(solution)/shard_map/all_to_all | solution.py:347
  11.0 2.0 %shard_map.85 = bf16[8,272,128]{2,1,0:T(8,128)(2,1)} custom-call(bf16[1,128,1024]{2,1,0:T(8,128)(2,1)} %a_ref.3, bf16[1,128,1024]{2,1,0:T(8,128)(2,1)} %b_ref.3, s32[1,128]{1,0:T(1,128)} %scale_ref.3), custom_call_target="tpu_custom_call" | custom-call | tf_op jit(solution)/shard_map/pallas_call | solution.py:301
  13.0 5.8 %collective-permute-start = (bf16[8,272,128]{2,1,0:T(8,128)(2,1)}, bf16[8,272,128]{2,1,0:T(8,128)(2,1)}, u32[]{:S(2)}, u32[]{:S(2)}) collective-permute-start(bf16[8,272,128]{2,1,0:T(8,128)(2,1)} %shard_map.85), channel_id=1, source_target_pairs={{0,0},{2,2},{4,4},{6,6},{8,56},{10,58},{12,60},{14,62},{16,16},{18... | collective-permute-start | bytes 1671176 | tf_op jit(solution)/shard_map/ppermute | solution.py:359
  18.8 10.4 %all-to-all-done.refs_0_ = bf16[8,272,128]{2,1,0:T(8,128)(2,1)S(1)} async-done(((bf16[8,272,128]{2,1,0:T(8,128)(2,1)}), bf16[8,272,128]{2,1,0:T(8,128)(2,1)S(1)}, u32[]{:S(2)}, u32[]{:S(2)}) %all-to-all-start) | async-done | bytes 557088 | tf_op jit(solution)/shard_map/all_to_all | solution.py:347
  29.2 2.8 %collective-permute-start.4 = (bf16[8,272,128]{2,1,0:T(8,128)(2,1)S(1)}, bf16[8,272,128]{2,1,0:T(8,128)(2,1)S(1)}, u32[]{:S(2)}, u32[]{:S(2)}) collective-permute-start(bf16[8,272,128]{2,1,0:T(8,128)(2,1)S(1)} %all-to-all-done.refs_0_), channel_id=1, source_target_pairs={{0,48},{16,0},{32,16},{48,32},{1,49},{17,1},{33,17},{49,33},{2,50}... | collective-permute-start | bytes 1671176 | tf_op jit(solution)/shard_map/ppermute | solution.py:353
  32.0 8.2 %all-to-all-start.1 = ((bf16[8,272,128]{2,1,0:T(8,128)(2,1)}), bf16[8,272,128]{2,1,0:T(8,128)(2,1)S(1)}, u32[]{:S(2)}, u32[]{:S(2)}) async-start(bf16[8,272,128]{2,1,0:T(8,128)(2,1)} %collective-permute-done), calls=%async_computation.1 | async-start | bytes 1114112 | tf_op jit(solution)/shard_map/all_to_all | solution.py:347
  40.2 3.9 %collective-permute-done.4.refs_4_ = bf16[8,272,128]{2,1,0:T(8,128)(2,1)S(1)} collective-permute-done((bf16[8,272,128]{2,1,0:T(8,128)(2,1)S(1)}, bf16[8,272,128]{2,1,0:T(8,128)(2,1)S(1)}, u32[]{:S(2)}, u32[]{:S(2)}) %collective-permute-start.4) | collective-permute-done | bytes 557088 | tf_op jit(solution)/shard_map/ppermute | solution.py:353
  44.1 3.8 %collective-permute-start.8 = (bf16[4,272,128]{2,1,0:T(8,128)(2,1)S(1)}, bf16[4,272,128]{2,1,0:T(8,128)(2,1)S(1)}, u32[]{:S(2)}, u32[]{:S(2)}) collective-permute-start(bf16[4,272,128]{2,1,0:T(8,128)(2,1)S(1)} %slice.41), channel_id=1, source_target_pairs={{0,48},{16,0},{32,16},{48,32},{1,49},{17,1},{33,17},{49,33},{2,50}... | collective-permute-start | bytes 835592 | tf_op jit(solution)/shard_map/ppermute | solution.py:353
  48.6 4.5 %collective-permute-done.8.refs_8_ = bf16[4,272,128]{2,1,0:T(8,128)(2,1)S(1)} collective-permute-done((bf16[4,272,128]{2,1,0:T(8,128)(2,1)S(1)}, bf16[4,272,128]{2,1,0:T(8,128)(2,1)S(1)}, u32[]{:S(2)}, u32[]{:S(2)}) %collective-permute-start.8) | collective-permute-done | bytes 278560 | tf_op jit(solution)/shard_map/ppermute | solution.py:353
  53.1 0.7 copy-done.2
  53.8 2.9 %collective-permute-done.6.refs_6_ = bf16[4,272,128]{2,1,0:T(8,128)(2,1)} collective-permute-done((bf16[4,272,128]{2,1,0:T(8,128)(2,1)S(1)}, bf16[4,272,128]{2,1,0:T(8,128)(2,1)}, u32[]{:S(2)}, u32[]{:S(2)}) %collective-permute-start.6) | collective-permute-done | bytes 278560 | tf_op jit(solution)/shard_map/ppermute | solution.py:350
  56.8 1.8 %collective-permute-done.7.refs_7_ = bf16[4,272,128]{2,1,0:T(8,128)(2,1)} collective-permute-done((bf16[4,272,128]{2,1,0:T(8,128)(2,1)}, bf16[4,272,128]{2,1,0:T(8,128)(2,1)}, u32[]{:S(2)}, u32[]{:S(2)}) %collective-permute-start.7) | collective-permute-done | bytes 278560 | tf_op jit(solution)/shard_map/ppermute | solution.py:362
  58.6 1.0 copy-done.3
  59.6 28.0 %shard_map.86 = (bf16[8,256,128]{2,1,0:T(8,128)(2,1)}, bf16[8,256,128]{2,1,0:T(8,128)(2,1)S(1)}, bf16[8,256,128]{2,1,0:T(8,128)(2,1)S(1)}, bf16[8,256,128]{2,1,0...) custom-call(s32[2]{0:T(128)S(1)} %pad_add_fusion.at_ref, ...), custom_call_target="tpu_custom_call" | custom-call | flops 8000000000 | bytes 10485760 | tf_op jit(solution)/shard_map/pallas_call | solution.py:257
  87.6 2.0 %collective-permute-start.10 = (bf16[8,256,128]{2,1,0:T(8,128)(2,1)S(1)}, bf16[8,256,128]{2,1,0:T(8,128)(2,1)S(1)}, u32[]{:S(2)}, u32[]{:S(2)}) collective-permute-start(bf16[8,256,128]{2,1,0:T(8,128)(2,1)S(1)} %get-tuple-element.31), channel_id=1, source_target_pairs={{0,1},{1,0},{2,3},{3,2},{4,5},{5,4},{6,7},{7,6},{8,9},{9,8},{10,11... | collective-permute-start | bytes 1572872 | tf_op jit(solution)/shard_map/ppermute | solution.py:362
  89.6 1.5 collective-permute-done.10
  91.9 0.7 fusion
  92.6 3.0 %collective-permute-start.19 = (bf16[8,128,128]{2,1,0:T(8,128)(2,1)S(1)}, bf16[8,128,128]{2,1,0:T(8,128)(2,1)S(1)}, u32[]{:S(2)}, u32[]{:S(2)}) collective-permute-start(bf16[8,128,128]{2,1,0:T(8,128)(2,1)S(1)} %get-tuple-element.52), channel_id=1, source_target_pairs={{0,48},{16,0},{32,16},{48,32},{1,49},{17,1},{33,17},{49,33},{2,50}... | collective-permute-start | bytes 786440 | tf_op jit(solution)/shard_map/ppermute | solution.py:353
  95.9 5.5 %all-to-all-start.2 = ((bf16[8,256,128]{2,1,0:T(8,128)(2,1)}), bf16[8,256,128]{2,1,0:T(8,128)(2,1)S(1)}, u32[]{:S(2)}, u32[]{:S(2)}) async-start(bf16[8,256,128]{2,1,0:T(8,128)(2,1)} %get-tuple-element.44), calls=%async_computation.2 | async-start | bytes 1048576 | tf_op jit(solution)/shard_map/all_to_all | solution.py:347
  101.6 0.7 slice.35
  102.3 4.9 %collective-permute-start.17 = (bf16[8,128,128]{2,1,0:T(8,128)(2,1)}, bf16[8,128,128]{2,1,0:T(8,128)(2,1)}, u32[]{:S(2)}, u32[]{:S(2)}) collective-permute-start(bf16[8,128,128]{2,1,0:T(8,128)(2,1)} %slice.35), channel_id=1, source_target_pairs={{0,48},{16,0},{32,16},{48,32},{1,49},{17,1},{33,17},{49,33},{2,50}... | collective-permute-start | bytes 786440 | tf_op jit(solution)/shard_map/ppermute | solution.py:353
  107.3 2.3 %collective-permute-start.20 = (bf16[8,128,128]{2,1,0:T(8,128)(2,1)S(1)}, bf16[8,128,128]{2,1,0:T(8,128)(2,1)S(1)}, u32[]{:S(2)}, u32[]{:S(2)}) collective-permute-start(bf16[8,128,128]{2,1,0:T(8,128)(2,1)S(1)} %add_convert_fusion.5), channel_id=1, source_target_pairs={{0,48},{16,0},{32,16},{48,32},{1,49},{17,1},{33,17},{49,33},{2,50}... | collective-permute-start | bytes 786440 | tf_op jit(solution)/shard_map/ppermute | solution.py:353
  109.7 4.2 %collective-permute-done.13 = bf16[8,128,128]{2,1,0:T(8,128)(2,1)S(1)} collective-permute-done((bf16[8,128,128]{2,1,0:T(8,128)(2,1)}, bf16[8,128,128]{2,1,0:T(8,128)(2,1)S(1)}, u32[]{:S(2)}, u32[]{:S(2)}) %collective-permute-start.13) | collective-permute-done | bytes 262176 | tf_op jit(solution)/shard_map/ppermute | solution.py:350
  114.4 10.6 %collective-permute-done.14 = bf16[8,128,128]{2,1,0:T(8,128)(2,1)} collective-permute-done((bf16[8,128,128]{2,1,0:T(8,128)(2,1)S(1)}, bf16[8,128,128]{2,1,0:T(8,128)(2,1)}, u32[]{:S(2)}, u32[]{:S(2)}) %collective-permute-start.14) | collective-permute-done | bytes 262176 | tf_op jit(solution)/shard_map/ppermute | solution.py:350
  125.0 1.2 add_convert_fusion.6
  126.2 0.8 pad_maximum_fusion
  127.1 7.1 %all-to-all-start.3 = ((bf16[8,256,128]{2,1,0:T(8,128)(2,1)}), bf16[8,256,128]{2,1,0:T(8,128)(2,1)S(1)}, u32[]{:S(2)}, u32[]{:S(2)}) async-start(bf16[8,256,128]{2,1,0:T(8,128)(2,1)} %pad_maximum_fusion), calls=%async_computation.3 | async-start | bytes 1048576 | tf_op jit(solution)/shard_map/all_to_all | solution.py:347
  134.2 0.7 collective-permute-start.15
  134.9 16.2 %all-to-all-done.3.dkv_ref = bf16[8,256,128]{2,1,0:T(8,128)(2,1)S(1)} async-done(((bf16[8,256,128]{2,1,0:T(8,128)(2,1)}), bf16[8,256,128]{2,1,0:T(8,128)(2,1)S(1)}, u32[]{:S(2)}, u32[]{:S(2)}) %all-to-all-start.3) | async-done | bytes 524320 | tf_op jit(solution)/shard_map/all_to_all | solution.py:347
  151.1 0.8 copy-done.4
  151.9 2.2 %shard_map.87 = (bf16[1,128,1024]{2,1,0:T(8,128)(2,1)}, bf16[1,128,1024]{2,1,0:T(8,128)(2,1)}, bf16[1,128,1024]{2,1,0:T(8,128)(2,1)}, bf16[1,128,1024]{2,1,0:T(8,128)(2,1)}) custom-call(bf16[8,256,128]{2,1,0:T(8,128)(2,1)} %copy-done.5, bf16[8,256,128]{2,1,0:T(8,128)(2,1)} %copy-done.4), custom_call_target="tpu_custom_call" | custom-call | tf_op jit(solution)/shard_map/pallas_call | solution.py:326
  (48 shorter events, 2.7 us)
Async XLA Ops:
  2.6 26.7 %all-to-all-start = ((bf16[8,272,128]{2,1,0:T(8,128)(2,1)}), bf16[8,272,128]{2,1,0:T(8,128)(2,1)S(1)}, u32[]{:S(2)}, u32[]{:S(2)}) async-start(bf16[8,272,128]{2,1,0:T(8,128)(2,1)} %shard_map.84), calls=%async_computation | async-start | bytes 1114112 | tf_op jit(solution)/shard_map/all_to_all | solution.py:347
  13.0 5.8 %collective-permute-start = (bf16[8,272,128]{2,1,0:T(8,128)(2,1)}, bf16[8,272,128]{2,1,0:T(8,128)(2,1)}, u32[]{:S(2)}, u32[]{:S(2)}) collective-permute-start(bf16[8,272,128]{2,1,0:T(8,128)(2,1)} %shard_map.85), channel_id=1, source_target_pairs={{0,0},{2,2},{4,4},{6,6},{8,56},{10,58},{12,60},{14,62},{16,16},{18... | collective-permute-start | bytes 1671176 | tf_op jit(solution)/shard_map/ppermute | solution.py:359
  29.2 14.8 %collective-permute-start.4 = (bf16[8,272,128]{2,1,0:T(8,128)(2,1)S(1)}, bf16[8,272,128]{2,1,0:T(8,128)(2,1)S(1)}, u32[]{:S(2)}, u32[]{:S(2)}) collective-permute-start(bf16[8,272,128]{2,1,0:T(8,128)(2,1)S(1)} %all-to-all-done.refs_0_), channel_id=1, source_target_pairs={{0,48},{16,0},{32,16},{48,32},{1,49},{17,1},{33,17},{49,33},{2,50}... | collective-permute-start | bytes 1671176 | tf_op jit(solution)/shard_map/ppermute | solution.py:353
  32.0 15.9 %collective-permute-start.2 = (bf16[8,272,128]{2,1,0:T(8,128)(2,1)S(1)}, bf16[8,272,128]{2,1,0:T(8,128)(2,1)S(1)}, u32[]{:S(2)}, u32[]{:S(2)}) collective-permute-start(bf16[8,272,128]{2,1,0:T(8,128)(2,1)S(1)} %all-to-all-done.refs_0_), channel_id=1, source_target_pairs={{0,16},{16,32},{32,48},{48,0},{1,17},{17,33},{33,49},{49,1},{2,18}... | collective-permute-start | bytes 1671176 | tf_op jit(solution)/shard_map/ppermute | solution.py:350
  32.0 24.8 %all-to-all-start.1 = ((bf16[8,272,128]{2,1,0:T(8,128)(2,1)}), bf16[8,272,128]{2,1,0:T(8,128)(2,1)S(1)}, u32[]{:S(2)}, u32[]{:S(2)}) async-start(bf16[8,272,128]{2,1,0:T(8,128)(2,1)} %collective-permute-done), calls=%async_computation.1 | async-start | bytes 1114112 | tf_op jit(solution)/shard_map/all_to_all | solution.py:347
  40.2 16.6 %collective-permute-start.1 = (bf16[8,272,128]{2,1,0:T(8,128)(2,1)S(1)}, bf16[8,272,128]{2,1,0:T(8,128)(2,1)S(1)}, u32[]{:S(2)}, u32[]{:S(2)}) collective-permute-start(bf16[8,272,128]{2,1,0:T(8,128)(2,1)S(1)} %all-to-all-done.refs_0_), channel_id=1, source_target_pairs={{0,1},{1,0},{2,3},{3,2},{4,5},{5,4},{6,7},{7,6},{8,9},{9,8},{10,11... | collective-permute-start | bytes 1671176 | tf_op jit(solution)/shard_map/ppermute | solution.py:362
  44.1 9.0 %collective-permute-start.8 = (bf16[4,272,128]{2,1,0:T(8,128)(2,1)S(1)}, bf16[4,272,128]{2,1,0:T(8,128)(2,1)S(1)}, u32[]{:S(2)}, u32[]{:S(2)}) collective-permute-start(bf16[4,272,128]{2,1,0:T(8,128)(2,1)S(1)} %slice.41), channel_id=1, source_target_pairs={{0,48},{16,0},{32,16},{48,32},{1,49},{17,1},{33,17},{49,33},{2,50}... | collective-permute-start | bytes 835592 | tf_op jit(solution)/shard_map/ppermute | solution.py:353
  47.9 8.8 %collective-permute-start.6 = (bf16[4,272,128]{2,1,0:T(8,128)(2,1)S(1)}, bf16[4,272,128]{2,1,0:T(8,128)(2,1)}, u32[]{:S(2)}, u32[]{:S(2)}) collective-permute-start(bf16[4,272,128]{2,1,0:T(8,128)(2,1)S(1)} %slice.40), channel_id=1, source_target_pairs={{0,16},{16,32},{32,48},{48,0},{1,17},{17,33},{33,49},{49,1},{2,18}... | collective-permute-start | bytes 835592 | tf_op jit(solution)/shard_map/ppermute | solution.py:350
  48.0 10.7 %collective-permute-start.5 = (bf16[8,272,128]{2,1,0:T(8,128)(2,1)S(1)}, bf16[8,272,128]{2,1,0:T(8,128)(2,1)}, u32[]{:S(2)}, u32[]{:S(2)}) collective-permute-start(bf16[8,272,128]{2,1,0:T(8,128)(2,1)S(1)} %collective-permute-done.4.refs_4_), channel_id=1, source_target_pairs={{0,1},{1,0},{2,3},{3,2},{4,5},{5,4},{6,7},{7,6},{8,9},{9,8},{10,11... | collective-permute-start | bytes 1671176 | tf_op jit(solution)/shard_map/ppermute | solution.py:362
  48.1 10.6 %collective-permute-start.3 = (bf16[8,272,128]{2,1,0:T(8,128)(2,1)S(1)}, bf16[8,272,128]{2,1,0:T(8,128)(2,1)}, u32[]{:S(2)}, u32[]{:S(2)}) collective-permute-start(bf16[8,272,128]{2,1,0:T(8,128)(2,1)S(1)} %collective-permute-done.2.refs_2_), channel_id=1, source_target_pairs={{0,1},{1,0},{2,3},{3,2},{4,5},{5,4},{6,7},{7,6},{8,9},{9,8},{10,11... | collective-permute-start | bytes 1671176 | tf_op jit(solution)/shard_map/ppermute | solution.py:362
  53.1 3.7 %collective-permute-start.9 = (bf16[4,272,128]{2,1,0:T(8,128)(2,1)S(1)}, bf16[4,272,128]{2,1,0:T(8,128)(2,1)}, u32[]{:S(2)}, u32[]{:S(2)}) collective-permute-start(bf16[4,272,128]{2,1,0:T(8,128)(2,1)S(1)} %collective-permute-done.8.refs_8_), channel_id=1, source_target_pairs={{0,1},{1,0},{2,3},{3,2},{4,5},{5,4},{6,7},{7,6},{8,9},{9,8},{10,11... | collective-permute-start | bytes 835592 | tf_op jit(solution)/shard_map/ppermute | solution.py:362
  53.1 0.7 copy-start.2
  56.7 1.9 %collective-permute-start.7 = (bf16[4,272,128]{2,1,0:T(8,128)(2,1)}, bf16[4,272,128]{2,1,0:T(8,128)(2,1)}, u32[]{:S(2)}, u32[]{:S(2)}) collective-permute-start(bf16[4,272,128]{2,1,0:T(8,128)(2,1)} %collective-permute-done.6.refs_6_), channel_id=1, source_target_pairs={{0,1},{1,0},{2,3},{3,2},{4,5},{5,4},{6,7},{7,6},{8,9},{9,8},{10,11... | collective-permute-start | bytes 835592 | tf_op jit(solution)/shard_map/ppermute | solution.py:362
  58.6 1.0 copy-start.3
  87.6 3.7 %copy-start = (bf16[8,256,128]{2,1,0:T(8,128)(2,1)}, bf16[8,256,128]{2,1,0:T(8,128)(2,1)S(1)}, u32[]{:S(2)}) copy-start(bf16[8,256,128]{2,1,0:T(8,128)(2,1)S(1)} %get-tuple-element.47) | copy-start | bytes 1572868
  87.6 3.6 %collective-permute-start.10 = (bf16[8,256,128]{2,1,0:T(8,128)(2,1)S(1)}, bf16[8,256,128]{2,1,0:T(8,128)(2,1)S(1)}, u32[]{:S(2)}, u32[]{:S(2)}) collective-permute-start(bf16[8,256,128]{2,1,0:T(8,128)(2,1)S(1)} %get-tuple-element.31), channel_id=1, source_target_pairs={{0,1},{1,0},{2,3},{3,2},{4,5},{5,4},{6,7},{7,6},{8,9},{9,8},{10,11... | collective-permute-start | bytes 1572872 | tf_op jit(solution)/shard_map/ppermute | solution.py:362
  91.3 4.3 %collective-permute-start.11 = (bf16[8,256,128]{2,1,0:T(8,128)(2,1)S(1)}, bf16[8,256,128]{2,1,0:T(8,128)(2,1)S(1)}, u32[]{:S(2)}, u32[]{:S(2)}) collective-permute-start(bf16[8,256,128]{2,1,0:T(8,128)(2,1)S(1)} %get-tuple-element.39), channel_id=1, source_target_pairs={{0,1},{1,0},{2,3},{3,2},{4,5},{5,4},{6,7},{7,6},{8,9},{9,8},{10,11... | collective-permute-start | bytes 1572872 | tf_op jit(solution)/shard_map/ppermute | solution.py:362
  91.8 4.0 %collective-permute-start.12 = (bf16[8,256,128]{2,1,0:T(8,128)(2,1)S(1)}, bf16[8,256,128]{2,1,0:T(8,128)(2,1)S(1)}, u32[]{:S(2)}, u32[]{:S(2)}) collective-permute-start(bf16[8,256,128]{2,1,0:T(8,128)(2,1)S(1)} %get-tuple-element.41), channel_id=1, source_target_pairs={{0,1},{1,0},{2,3},{3,2},{4,5},{5,4},{6,7},{7,6},{8,9},{9,8},{10,11... | collective-permute-start | bytes 1572872 | tf_op jit(solution)/shard_map/ppermute | solution.py:362
  92.6 14.6 %collective-permute-start.19 = (bf16[8,128,128]{2,1,0:T(8,128)(2,1)S(1)}, bf16[8,128,128]{2,1,0:T(8,128)(2,1)S(1)}, u32[]{:S(2)}, u32[]{:S(2)}) collective-permute-start(bf16[8,128,128]{2,1,0:T(8,128)(2,1)S(1)} %get-tuple-element.52), channel_id=1, source_target_pairs={{0,48},{16,0},{32,16},{48,32},{1,49},{17,1},{33,17},{49,33},{2,50}... | collective-permute-start | bytes 786440 | tf_op jit(solution)/shard_map/ppermute | solution.py:353
  95.9 5.5 %copy-start.1 = (bf16[8,256,128]{2,1,0:T(8,128)(2,1)S(1)}, bf16[8,256,128]{2,1,0:T(8,128)(2,1)}, u32[]{:S(2)}) copy-start(bf16[8,256,128]{2,1,0:T(8,128)(2,1)} %copy-done) | copy-start | bytes 1572868
  95.9 29.0 %all-to-all-start.2 = ((bf16[8,256,128]{2,1,0:T(8,128)(2,1)}), bf16[8,256,128]{2,1,0:T(8,128)(2,1)S(1)}, u32[]{:S(2)}, u32[]{:S(2)}) async-start(bf16[8,256,128]{2,1,0:T(8,128)(2,1)} %get-tuple-element.44), calls=%async_computation.2 | async-start | bytes 1048576 | tf_op jit(solution)/shard_map/all_to_all | solution.py:347
  101.4 12.8 %collective-permute-start.16 = (bf16[8,256,128]{2,1,0:T(8,128)(2,1)S(1)}, bf16[8,256,128]{2,1,0:T(8,128)(2,1)S(1)}, u32[]{:S(2)}, u32[]{:S(2)}) collective-permute-start(bf16[8,256,128]{2,1,0:T(8,128)(2,1)S(1)} %copy-done.1), channel_id=1, source_target_pairs={{0,1},{1,0},{2,3},{3,2},{4,5},{5,4},{6,7},{7,6},{8,9},{9,8},{10,11... | collective-permute-start | bytes 1572872 | tf_op jit(solution)/shard_map/ppermute | solution.py:362
  101.5 12.4 %collective-permute-start.13 = (bf16[8,128,128]{2,1,0:T(8,128)(2,1)}, bf16[8,128,128]{2,1,0:T(8,128)(2,1)S(1)}, u32[]{:S(2)}, u32[]{:S(2)}) collective-permute-start(bf16[8,128,128]{2,1,0:T(8,128)(2,1)} %get-tuple-element.53), channel_id=1, source_target_pairs={{0,16},{16,32},{32,48},{48,0},{1,17},{17,33},{33,49},{49,1},{2,18}... | collective-permute-start | bytes 786440 | tf_op jit(solution)/shard_map/ppermute | solution.py:350
  102.3 22.6 %collective-permute-start.17 = (bf16[8,128,128]{2,1,0:T(8,128)(2,1)}, bf16[8,128,128]{2,1,0:T(8,128)(2,1)}, u32[]{:S(2)}, u32[]{:S(2)}) collective-permute-start(bf16[8,128,128]{2,1,0:T(8,128)(2,1)} %slice.35), channel_id=1, source_target_pairs={{0,48},{16,0},{32,16},{48,32},{1,49},{17,1},{33,17},{49,33},{2,50}... | collective-permute-start | bytes 786440 | tf_op jit(solution)/shard_map/ppermute | solution.py:353
  107.3 17.6 %collective-permute-start.20 = (bf16[8,128,128]{2,1,0:T(8,128)(2,1)S(1)}, bf16[8,128,128]{2,1,0:T(8,128)(2,1)S(1)}, u32[]{:S(2)}, u32[]{:S(2)}) collective-permute-start(bf16[8,128,128]{2,1,0:T(8,128)(2,1)S(1)} %add_convert_fusion.5), channel_id=1, source_target_pairs={{0,48},{16,0},{32,16},{48,32},{1,49},{17,1},{33,17},{49,33},{2,50}... | collective-permute-start | bytes 786440 | tf_op jit(solution)/shard_map/ppermute | solution.py:353
  109.6 15.3 %collective-permute-start.18 = (bf16[8,128,128]{2,1,0:T(8,128)(2,1)S(1)}, bf16[8,128,128]{2,1,0:T(8,128)(2,1)S(1)}, u32[]{:S(2)}, u32[]{:S(2)}) collective-permute-start(bf16[8,128,128]{2,1,0:T(8,128)(2,1)S(1)} %slice.37), channel_id=1, source_target_pairs={{0,16},{16,32},{32,48},{48,0},{1,17},{17,33},{33,49},{49,1},{2,18}... | collective-permute-start | bytes 786440 | tf_op jit(solution)/shard_map/ppermute | solution.py:350
  113.9 11.0 %collective-permute-start.14 = (bf16[8,128,128]{2,1,0:T(8,128)(2,1)S(1)}, bf16[8,128,128]{2,1,0:T(8,128)(2,1)}, u32[]{:S(2)}, u32[]{:S(2)}) collective-permute-start(bf16[8,128,128]{2,1,0:T(8,128)(2,1)S(1)} %add_convert_fusion.7), channel_id=1, source_target_pairs={{0,16},{16,32},{32,48},{48,0},{1,17},{17,33},{33,49},{49,1},{2,18}... | collective-permute-start | bytes 786440 | tf_op jit(solution)/shard_map/ppermute | solution.py:350
  127.1 24.0 %all-to-all-start.3 = ((bf16[8,256,128]{2,1,0:T(8,128)(2,1)}), bf16[8,256,128]{2,1,0:T(8,128)(2,1)S(1)}, u32[]{:S(2)}, u32[]{:S(2)}) async-start(bf16[8,256,128]{2,1,0:T(8,128)(2,1)} %pad_maximum_fusion), calls=%async_computation.3 | async-start | bytes 1048576 | tf_op jit(solution)/shard_map/all_to_all | solution.py:347
  134.2 0.7 collective-permute-start.15
  134.9 16.2 %copy-start.5 = (bf16[8,256,128]{2,1,0:T(8,128)(2,1)}, bf16[8,256,128]{2,1,0:T(8,128)(2,1)S(1)}, u32[]{:S(2)}) copy-start(bf16[8,256,128]{2,1,0:T(8,128)(2,1)S(1)} %collective-permute-done.15.ad_ref) | copy-start | bytes 1572868
  151.1 0.8 copy-start.4

commit v8 on v7

--- a/solution.py
+++ b/solution.py
@@ -283,7 +283,7 @@
             pltpu.SemaphoreType.DMA((N_PIECES,)),
             pltpu.SemaphoreType.DMA((1,)),
         ],
-        compiler_params=pltpu.CompilerParams(vmem_limit_bytes=34 * 1024 * 1024),
+        compiler_params=pltpu.CompilerParams(vmem_limit_bytes=31 * 1024 * 1024),
         cost_estimate=pl.CostEstimate(flops=8 * 10**9, bytes_accessed=10 * 2**20, transcendentals=5 * 10**6),
     )(at, *pieces, qd)
 
@@ -376,22 +376,14 @@
 
     ad, *grads = attention(at, pieces, qd)
 
-    far = add(grads[4], twin(grads[5]))
-    far, *grads = lax.optimization_barrier((far, *grads))
-    sums = {distance: add(grads[2 * distance], twin(grads[2 * distance + 1])) for distance in (3, 1, 0)}
-    ad, sums[1], sums[3] = lax.optimization_barrier((ad, sums[1], sums[3]))
+    sums = {distance: add(grads[2 * distance], twin(grads[2 * distance + 1])) for distance in (2, 1, 3, 0)}
+    right_b, left_a = right(sums[1][half:]), left(sums[3][:half])
+    right_a = right(add(sums[1][:half], right(sums[2][:half])))
+    left_b = left(add(sums[3][half:], left(sums[2][half:])))
+    dkv = jnp.concatenate([add(sums[0][:half], right_a, left_a), add(sums[0][half:], right_b, left_b)], axis=0)
     ad_back = over_heads(ad)
-    k, v = slice(0, ROWS), slice(ROWS, 2 * ROWS)
-    key_left = left(sums[3][:, k])
-    key_relay = add(sums[1][:, k], right(far[:, k]))
-    value_relay = add(sums[3][:, v], left(far[:, v]))
-    key_right, value_left = right(key_relay), left(value_relay)
-    value_right = right(sums[1][:, v])
-    key_right, ad_back = lax.optimization_barrier((key_right, ad_back))
-    key_sum = add(sums[0][:, k], key_right, key_left)
-    value_sum = add(sums[0][:, v], value_right, value_left)
-    sums = jnp.concatenate([key_sum, value_sum], axis=1)
-    return unpack(swap(ad_back), over_heads(sums))
+    dkv, ad_back = lax.optimization_barrier((dkv, ad_back))
+    return unpack(swap(ad_back), over_heads(dkv))
 
 
 def solution(mesh):

time: 157 us -> 160 us (1.019)
  the two profiles are of different devices: /device:TPU:24 before, /device:TPU:16 now
where the time goes in v8:
time: 160 us; the launch traced here: 158 us
  starting transfers between devices  58.8 us (37%)
  waiting for transfers between devices  50.1 us (31%)
  Pallas kernels  35.4 us (22%)
  local copies, waits for them, and re-layouts  9 us (6%)
  other arithmetic  3.91 us (2%)
    all_to_all x4, starting transfers between devices, over_heads(): return lax.all_to_all(arr, 'z', split_axis=0, concat_axis=0, tiled=True)  29.4 us
    pallas_call x1, Pallas kernels, attention(): pl.pallas_call(attention_kernel, out_shape=outs, in_specs=[pl.BlockSpec(m...  29.3 us
    all_to_all x4, waiting for transfers between devices, over_heads(): return lax.all_to_all(arr, 'z', split_axis=0, concat_axis=0, tiled=True)  25.3 us
    ppermute x5, waiting for transfers between devices, right(): return lax.ppermute(arr, 'x', [(i, (i + 1) % XS) for i in range(XS)])  12.5 us
    ppermute x5, waiting for transfers between devices, left(): return lax.ppermute(arr, 'x', [(i, (i + XS - 1) % XS) for i in range(XS)])  11.3 us
    ppermute x5, starting transfers between devices, right(): return lax.ppermute(arr, 'x', [(i, (i + 1) % XS) for i in range(XS)])  11.1 us
    ppermute x5, starting transfers between devices, left(): return lax.ppermute(arr, 'x', [(i, (i + XS - 1) % XS) for i in range(XS)])  8.99 us
    unnamed x30, local copies, waits for them, and re-layouts  8.89 us
  transfers between devices with their start and end apart: 25, of which 10 were waited for; matrix products, arithmetic and copies ran while one was open for 3% of the time, Pallas kernels for 1%

profile of v8, /device:TPU:16, one launch (start us, length us, event | category | flops | bytes accessed | tf_op | source)
XLA Modules:
  0.0 158.2 jit_solution(2614240734810051235)
XLA Ops:
  0.6 1.9 %shard_map.84 = bf16[8,272,128]{2,1,0:T(8,128)(2,1)} custom-call(bf16[1,128,1024]{2,1,0:T(8,128)(2,1)} %a_ref.2, bf16[1,128,1024]{2,1,0:T(8,128)(2,1)} %b_ref.2, s32[1,128]{1,0:T(1,128)} %scale_ref.3), custom_call_target="tpu_custom_call" | custom-call | tf_op jit(solution)/shard_map/pallas_call | solution.py:301
  2.6 8.5 %all-to-all-start = ((bf16[8,272,128]{2,1,0:T(8,128)(2,1)}), bf16[8,272,128]{2,1,0:T(8,128)(2,1)S(1)}, u32[]{:S(2)}, u32[]{:S(2)}) async-start(bf16[8,272,128]{2,1,0:T(8,128)(2,1)} %shard_map.84), calls=%async_computation | async-start | bytes 1114112 | tf_op jit(solution)/shard_map/all_to_all | solution.py:347
  11.0 2.0 %shard_map.85 = bf16[8,272,128]{2,1,0:T(8,128)(2,1)} custom-call(bf16[1,128,1024]{2,1,0:T(8,128)(2,1)} %a_ref.3, bf16[1,128,1024]{2,1,0:T(8,128)(2,1)} %b_ref.3, s32[1,128]{1,0:T(1,128)} %scale_ref.3), custom_call_target="tpu_custom_call" | custom-call | tf_op jit(solution)/shard_map/pallas_call | solution.py:301
  13.0 5.9 %collective-permute-start = (bf16[8,272,128]{2,1,0:T(8,128)(2,1)}, bf16[8,272,128]{2,1,0:T(8,128)(2,1)}, u32[]{:S(2)}, u32[]{:S(2)}) collective-permute-start(bf16[8,272,128]{2,1,0:T(8,128)(2,1)} %shard_map.85), channel_id=1, source_target_pairs={{0,0},{2,2},{4,4},{6,6},{8,56},{10,58},{12,60},{14,62},{16,16},{18... | collective-permute-start | bytes 1671176 | tf_op jit(solution)/shard_map/ppermute | solution.py:359
  18.9 10.4 %all-to-all-done.refs_0_ = bf16[8,272,128]{2,1,0:T(8,128)(2,1)S(1)} async-done(((bf16[8,272,128]{2,1,0:T(8,128)(2,1)}), bf16[8,272,128]{2,1,0:T(8,128)(2,1)S(1)}, u32[]{:S(2)}, u32[]{:S(2)}) %all-to-all-start) | async-done | bytes 557088 | tf_op jit(solution)/shard_map/all_to_all | solution.py:347
  29.2 2.8 %collective-permute-start.4 = (bf16[8,272,128]{2,1,0:T(8,128)(2,1)S(1)}, bf16[8,272,128]{2,1,0:T(8,128)(2,1)S(1)}, u32[]{:S(2)}, u32[]{:S(2)}) collective-permute-start(bf16[8,272,128]{2,1,0:T(8,128)(2,1)S(1)} %all-to-all-done.refs_0_), channel_id=1, source_target_pairs={{0,48},{16,0},{32,16},{48,32},{1,49},{17,1},{33,17},{49,33},{2,50}... | collective-permute-start | bytes 1671176 | tf_op jit(solution)/shard_map/ppermute | solution.py:353
  32.0 8.2 %all-to-all-start.1 = ((bf16[8,272,128]{2,1,0:T(8,128)(2,1)}), bf16[8,272,128]{2,1,0:T(8,128)(2,1)S(1)}, u32[]{:S(2)}, u32[]{:S(2)}) async-start(bf16[8,272,128]{2,1,0:T(8,128)(2,1)} %collective-permute-done), calls=%async_computation.1 | async-start | bytes 1114112 | tf_op jit(solution)/shard_map/all_to_all | solution.py:347
  40.2 3.9 %collective-permute-done.4.refs_4_ = bf16[8,272,128]{2,1,0:T(8,128)(2,1)S(1)} collective-permute-done((bf16[8,272,128]{2,1,0:T(8,128)(2,1)S(1)}, bf16[8,272,128]{2,1,0:T(8,128)(2,1)S(1)}, u32[]{:S(2)}, u32[]{:S(2)}) %collective-permute-start.4) | collective-permute-done | bytes 557088 | tf_op jit(solution)/shard_map/ppermute | solution.py:353
  44.1 3.8 %collective-permute-start.8 = (bf16[4,272,128]{2,1,0:T(8,128)(2,1)S(1)}, bf16[4,272,128]{2,1,0:T(8,128)(2,1)S(1)}, u32[]{:S(2)}, u32[]{:S(2)}) collective-permute-start(bf16[4,272,128]{2,1,0:T(8,128)(2,1)S(1)} %slice.41), channel_id=1, source_target_pairs={{0,48},{16,0},{32,16},{48,32},{1,49},{17,1},{33,17},{49,33},{2,50}... | collective-permute-start | bytes 835592 | tf_op jit(solution)/shard_map/ppermute | solution.py:353
  48.6 4.5 %collective-permute-done.8.refs_8_ = bf16[4,272,128]{2,1,0:T(8,128)(2,1)S(1)} collective-permute-done((bf16[4,272,128]{2,1,0:T(8,128)(2,1)S(1)}, bf16[4,272,128]{2,1,0:T(8,128)(2,1)S(1)}, u32[]{:S(2)}, u32[]{:S(2)}) %collective-permute-start.8) | collective-permute-done | bytes 278560 | tf_op jit(solution)/shard_map/ppermute | solution.py:353
  53.8 2.9 %collective-permute-done.6.refs_6_ = bf16[4,272,128]{2,1,0:T(8,128)(2,1)} collective-permute-done((bf16[4,272,128]{2,1,0:T(8,128)(2,1)S(1)}, bf16[4,272,128]{2,1,0:T(8,128)(2,1)}, u32[]{:S(2)}, u32[]{:S(2)}) %collective-permute-start.6) | collective-permute-done | bytes 278560 | tf_op jit(solution)/shard_map/ppermute | solution.py:350
  57.6 1.0 collective-permute-done.7.refs_7_
  58.7 1.0 copy-done.2
  59.7 1.1 copy-done.4
  60.8 1.1 copy-done.6
  61.8 1.0 copy-done.12
  62.8 29.3 %shard_map.86 = (bf16[8,256,128]{2,1,0:T(8,128)(2,1)S(1)}, bf16[8,256,128]{2,1,0:T(8,128)(2,1)S(1)}, bf16[8,256,128]{2,1,0:T(8,128)(2,1)S(1)}, bf16[8,256,128]{2...) custom-call(s32[2]{0:T(128)S(1)} %pad_add_fusion.at_ref, ...), custom_call_target="tpu_custom_call" | custom-call | flops 8000000000 | bytes 10485760 | tf_op jit(solution)/shard_map/pallas_call | solution.py:257
  95.0 5.8 %all-to-all-start.2 = ((bf16[8,256,128]{2,1,0:T(8,128)(2,1)}), bf16[8,256,128]{2,1,0:T(8,128)(2,1)}, u32[]{:S(2)}, u32[]{:S(2)}) async-start(bf16[8,256,128]{2,1,0:T(8,128)(2,1)} %copy-done), calls=%async_computation.2 | async-start | bytes 1048576 | tf_op jit(solution)/shard_map/all_to_all | solution.py:347
  101.4 1.2 add_convert_fusion.2
  103.5 1.2 add_convert_fusion.1
  104.8 6.4 %collective-permute-start.13 = (bf16[4,256,128]{2,1,0:T(8,128)(2,1)S(1)}, bf16[4,256,128]{2,1,0:T(8,128)(2,1)S(1)}, u32[]{:S(2)}, u32[]{:S(2)}) collective-permute-start(bf16[4,256,128]{2,1,0:T(8,128)(2,1)S(1)} %get-tuple-element.32), channel_id=1, source_target_pairs={{0,16},{16,32},{32,48},{48,0},{1,17},{17,33},{33,49},{49,1},{2,18}... | collective-permute-start | bytes 786440 | tf_op jit(solution)/shard_map/ppermute | solution.py:350
  111.4 1.0 collective-permute-start.16
  112.4 5.5 %collective-permute-done.13 = bf16[4,256,128]{2,1,0:T(8,128)(2,1)S(1)} collective-permute-done((bf16[4,256,128]{2,1,0:T(8,128)(2,1)S(1)}, bf16[4,256,128]{2,1,0:T(8,128)(2,1)S(1)}, u32[]{:S(2)}, u32[]{:S(2)}) %collective-permute-start.13) | collective-permute-done | bytes 262176 | tf_op jit(solution)/shard_map/ppermute | solution.py:350
  117.9 3.7 %collective-permute-start.14 = (bf16[4,256,128]{2,1,0:T(8,128)(2,1)S(1)}, bf16[4,256,128]{2,1,0:T(8,128)(2,1)S(1)}, u32[]{:S(2)}, u32[]{:S(2)}) collective-permute-start(bf16[4,256,128]{2,1,0:T(8,128)(2,1)S(1)} %add_convert_fusion.7), channel_id=1, source_target_pairs={{0,16},{16,32},{32,48},{48,0},{1,17},{17,33},{33,49},{49,1},{2,18}... | collective-permute-start | bytes 786440 | tf_op jit(solution)/shard_map/ppermute | solution.py:350
  121.7 1.4 collective-permute-start.19
  123.3 1.8 %collective-permute-done.16 = bf16[4,256,128]{2,1,0:T(8,128)(2,1)S(1)} collective-permute-done((bf16[4,256,128]{2,1,0:T(8,128)(2,1)S(1)}, bf16[4,256,128]{2,1,0:T(8,128)(2,1)S(1)}, u32[]{:S(2)}, u32[]{:S(2)}) %collective-permute-start.16) | collective-permute-done | bytes 262176 | tf_op jit(solution)/shard_map/ppermute | solution.py:353
  125.1 4.1 %collective-permute-done.14 = bf16[4,256,128]{2,1,0:T(8,128)(2,1)S(1)} collective-permute-done((bf16[4,256,128]{2,1,0:T(8,128)(2,1)S(1)}, bf16[4,256,128]{2,1,0:T(8,128)(2,1)S(1)}, u32[]{:S(2)}, u32[]{:S(2)}) %collective-permute-start.14) | collective-permute-done | bytes 262176 | tf_op jit(solution)/shard_map/ppermute | solution.py:350
  129.2 1.2 collective-permute-done.19
  131.4 7.0 %all-to-all-start.3 = ((bf16[8,256,128]{2,1,0:T(8,128)(2,1)}), bf16[8,256,128]{2,1,0:T(8,128)(2,1)S(1)}, u32[]{:S(2)}, u32[]{:S(2)}) async-start(bf16[8,256,128]{2,1,0:T(8,128)(2,1)} %pad_maximum_fusion), calls=%async_computation.3 | async-start | bytes 1048576 | tf_op jit(solution)/shard_map/all_to_all | solution.py:347
  138.4 1.7 %collective-permute-start.20 = (bf16[8,256,128]{2,1,0:T(8,128)(2,1)}, bf16[8,256,128]{2,1,0:T(8,128)(2,1)S(1)}, u32[]{:S(2)}, u32[]{:S(2)}) collective-permute-start(bf16[8,256,128]{2,1,0:T(8,128)(2,1)} %all-to-all-done.2), channel_id=1, source_target_pairs={{0,0},{2,2},{4,4},{6,6},{8,56},{10,58},{12,60},{14,62},{16,16},{18... | collective-permute-start | bytes 1572872 | tf_op jit(solution)/shard_map/ppermute | solution.py:359
  140.1 14.9 %all-to-all-done.3.dkv_ref = bf16[8,256,128]{2,1,0:T(8,128)(2,1)S(1)} async-done(((bf16[8,256,128]{2,1,0:T(8,128)(2,1)}), bf16[8,256,128]{2,1,0:T(8,128)(2,1)S(1)}, u32[]{:S(2)}, u32[]{:S(2)}) %all-to-all-start.3) | async-done | bytes 524320 | tf_op jit(solution)/shard_map/all_to_all | solution.py:347
  155.8 2.2 %shard_map.87 = (bf16[1,128,1024]{2,1,0:T(8,128)(2,1)}, bf16[1,128,1024]{2,1,0:T(8,128)(2,1)}, bf16[1,128,1024]{2,1,0:T(8,128)(2,1)}, bf16[1,128,1024]{2,1,0:T(8,128)(2,1)}) custom-call(bf16[8,256,128]{2,1,0:T(8,128)(2,1)} %copy-done.14, bf16[8,256,128]{2,1,0:T(8,128)(2,1)} %copy-done.13), custom_call_target="tpu_custom_call" | custom-call | tf_op jit(solution)/shard_map/pallas_call | solution.py:326
  (66 shorter events, 9.2 us)
Async XLA Ops:
  2.6 26.7 %all-to-all-start = ((bf16[8,272,128]{2,1,0:T(8,128)(2,1)}), bf16[8,272,128]{2,1,0:T(8,128)(2,1)S(1)}, u32[]{:S(2)}, u32[]{:S(2)}) async-start(bf16[8,272,128]{2,1,0:T(8,128)(2,1)} %shard_map.84), calls=%async_computation | async-start | bytes 1114112 | tf_op jit(solution)/shard_map/all_to_all | solution.py:347
  13.0 5.9 %collective-permute-start = (bf16[8,272,128]{2,1,0:T(8,128)(2,1)}, bf16[8,272,128]{2,1,0:T(8,128)(2,1)}, u32[]{:S(2)}, u32[]{:S(2)}) collective-permute-start(bf16[8,272,128]{2,1,0:T(8,128)(2,1)} %shard_map.85), channel_id=1, source_target_pairs={{0,0},{2,2},{4,4},{6,6},{8,56},{10,58},{12,60},{14,62},{16,16},{18... | collective-permute-start | bytes 1671176 | tf_op jit(solution)/shard_map/ppermute | solution.py:359
  29.2 14.8 %collective-permute-start.4 = (bf16[8,272,128]{2,1,0:T(8,128)(2,1)S(1)}, bf16[8,272,128]{2,1,0:T(8,128)(2,1)S(1)}, u32[]{:S(2)}, u32[]{:S(2)}) collective-permute-start(bf16[8,272,128]{2,1,0:T(8,128)(2,1)S(1)} %all-to-all-done.refs_0_), channel_id=1, source_target_pairs={{0,48},{16,0},{32,16},{48,32},{1,49},{17,1},{33,17},{49,33},{2,50}... | collective-permute-start | bytes 1671176 | tf_op jit(solution)/shard_map/ppermute | solution.py:353
  32.0 15.9 %collective-permute-start.2 = (bf16[8,272,128]{2,1,0:T(8,128)(2,1)S(1)}, bf16[8,272,128]{2,1,0:T(8,128)(2,1)S(1)}, u32[]{:S(2)}, u32[]{:S(2)}) collective-permute-start(bf16[8,272,128]{2,1,0:T(8,128)(2,1)S(1)} %all-to-all-done.refs_0_), channel_id=1, source_target_pairs={{0,16},{16,32},{32,48},{48,0},{1,17},{17,33},{33,49},{49,1},{2,18}... | collective-permute-start | bytes 1671176 | tf_op jit(solution)/shard_map/ppermute | solution.py:350
  32.0 25.6 %all-to-all-start.1 = ((bf16[8,272,128]{2,1,0:T(8,128)(2,1)}), bf16[8,272,128]{2,1,0:T(8,128)(2,1)S(1)}, u32[]{:S(2)}, u32[]{:S(2)}) async-start(bf16[8,272,128]{2,1,0:T(8,128)(2,1)} %collective-permute-done), calls=%async_computation.1 | async-start | bytes 1114112 | tf_op jit(solution)/shard_map/all_to_all | solution.py:347
  40.2 16.6 %collective-permute-start.1 = (bf16[8,272,128]{2,1,0:T(8,128)(2,1)S(1)}, bf16[8,272,128]{2,1,0:T(8,128)(2,1)S(1)}, u32[]{:S(2)}, u32[]{:S(2)}) collective-permute-start(bf16[8,272,128]{2,1,0:T(8,128)(2,1)S(1)} %all-to-all-done.refs_0_), channel_id=1, source_target_pairs={{0,1},{1,0},{2,3},{3,2},{4,5},{5,4},{6,7},{7,6},{8,9},{9,8},{10,11... | collective-permute-start | bytes 1671176 | tf_op jit(solution)/shard_map/ppermute | solution.py:362
  44.1 3.9 %copy-start.1 = (bf16[8,272,128]{2,1,0:T(8,128)(2,1)}, bf16[8,272,128]{2,1,0:T(8,128)(2,1)S(1)}, u32[]{:S(2)}) copy-start(bf16[8,272,128]{2,1,0:T(8,128)(2,1)S(1)} %collective-permute-done.4.refs_4_) | copy-start | bytes 1671172
  44.1 9.0 %collective-permute-start.8 = (bf16[4,272,128]{2,1,0:T(8,128)(2,1)S(1)}, bf16[4,272,128]{2,1,0:T(8,128)(2,1)S(1)}, u32[]{:S(2)}, u32[]{:S(2)}) collective-permute-start(bf16[4,272,128]{2,1,0:T(8,128)(2,1)S(1)} %slice.41), channel_id=1, source_target_pairs={{0,48},{16,0},{32,16},{48,32},{1,49},{17,1},{33,17},{49,33},{2,50}... | collective-permute-start | bytes 835592 | tf_op jit(solution)/shard_map/ppermute | solution.py:353
  47.9 10.8 %copy-start.3 = (bf16[8,272,128]{2,1,0:T(8,128)(2,1)}, bf16[8,272,128]{2,1,0:T(8,128)(2,1)S(1)}, u32[]{:S(2)}) copy-start(bf16[8,272,128]{2,1,0:T(8,128)(2,1)S(1)} %collective-permute-done.2.refs_2_) | copy-start | bytes 1671172
  47.9 8.8 %collective-permute-start.6 = (bf16[4,272,128]{2,1,0:T(8,128)(2,1)S(1)}, bf16[4,272,128]{2,1,0:T(8,128)(2,1)}, u32[]{:S(2)}, u32[]{:S(2)}) collective-permute-start(bf16[4,272,128]{2,1,0:T(8,128)(2,1)S(1)} %slice.40), channel_id=1, source_target_pairs={{0,16},{16,32},{32,48},{48,0},{1,17},{17,33},{33,49},{49,1},{2,18}... | collective-permute-start | bytes 835592 | tf_op jit(solution)/shard_map/ppermute | solution.py:350
  48.0 10.7 %collective-permute-start.5 = (bf16[8,272,128]{2,1,0:T(8,128)(2,1)S(1)}, bf16[8,272,128]{2,1,0:T(8,128)(2,1)}, u32[]{:S(2)}, u32[]{:S(2)}) collective-permute-start(bf16[8,272,128]{2,1,0:T(8,128)(2,1)S(1)} %collective-permute-done.4.refs_4_), channel_id=1, source_target_pairs={{0,1},{1,0},{2,3},{3,2},{4,5},{5,4},{6,7},{7,6},{8,9},{9,8},{10,11... | collective-permute-start | bytes 1671176 | tf_op jit(solution)/shard_map/ppermute | solution.py:362
  48.1 10.6 %collective-permute-start.3 = (bf16[8,272,128]{2,1,0:T(8,128)(2,1)S(1)}, bf16[8,272,128]{2,1,0:T(8,128)(2,1)}, u32[]{:S(2)}, u32[]{:S(2)}) collective-permute-start(bf16[8,272,128]{2,1,0:T(8,128)(2,1)S(1)} %collective-permute-done.2.refs_2_), channel_id=1, source_target_pairs={{0,1},{1,0},{2,3},{3,2},{4,5},{5,4},{6,7},{7,6},{8,9},{9,8},{10,11... | collective-permute-start | bytes 1671176 | tf_op jit(solution)/shard_map/ppermute | solution.py:362
  53.1 4.5 %collective-permute-start.9 = (bf16[4,272,128]{2,1,0:T(8,128)(2,1)S(1)}, bf16[4,272,128]{2,1,0:T(8,128)(2,1)}, u32[]{:S(2)}, u32[]{:S(2)}) collective-permute-start(bf16[4,272,128]{2,1,0:T(8,128)(2,1)S(1)} %collective-permute-done.8.refs_8_), channel_id=1, source_target_pairs={{0,1},{1,0},{2,3},{3,2},{4,5},{5,4},{6,7},{7,6},{8,9},{9,8},{10,11... | collective-permute-start | bytes 835592 | tf_op jit(solution)/shard_map/ppermute | solution.py:362
  56.7 1.9 %collective-permute-start.7 = (bf16[4,272,128]{2,1,0:T(8,128)(2,1)}, bf16[4,272,128]{2,1,0:T(8,128)(2,1)}, u32[]{:S(2)}, u32[]{:S(2)}) collective-permute-start(bf16[4,272,128]{2,1,0:T(8,128)(2,1)} %collective-permute-done.6.refs_6_), channel_id=1, source_target_pairs={{0,1},{1,0},{2,3},{3,2},{4,5},{5,4},{6,7},{7,6},{8,9},{9,8},{10,11... | collective-permute-start | bytes 835592 | tf_op jit(solution)/shard_map/ppermute | solution.py:362
  58.6 1.1 copy-start.2
  59.7 1.1 copy-start.4
  94.5 6.9 %collective-permute-start.11 = (bf16[8,256,128]{2,1,0:T(8,128)(2,1)}, bf16[8,256,128]{2,1,0:T(8,128)(2,1)}, u32[]{:S(2)}, u32[]{:S(2)}) collective-permute-start(bf16[8,256,128]{2,1,0:T(8,128)(2,1)} %get-tuple-element.22), channel_id=1, source_target_pairs={{0,1},{1,0},{2,3},{3,2},{4,5},{5,4},{6,7},{7,6},{8,9},{9,8},{10,11... | collective-permute-start | bytes 1572872 | tf_op jit(solution)/shard_map/ppermute | solution.py:362
  94.6 8.9 %collective-permute-start.12 = (bf16[8,256,128]{2,1,0:T(8,128)(2,1)}, bf16[8,256,128]{2,1,0:T(8,128)(2,1)}, u32[]{:S(2)}, u32[]{:S(2)}) collective-permute-start(bf16[8,256,128]{2,1,0:T(8,128)(2,1)} %get-tuple-element.24), channel_id=1, source_target_pairs={{0,1},{1,0},{2,3},{3,2},{4,5},{5,4},{6,7},{7,6},{8,9},{9,8},{10,11... | collective-permute-start | bytes 1572872 | tf_op jit(solution)/shard_map/ppermute | solution.py:362
  95.0 5.8 %copy-start.8 = (bf16[8,256,128]{2,1,0:T(8,128)(2,1)S(1)}, bf16[8,256,128]{2,1,0:T(8,128)(2,1)}, u32[]{:S(2)}) copy-start(bf16[8,256,128]{2,1,0:T(8,128)(2,1)} %copy-done.7) | copy-start | bytes 1572868
  95.0 5.9 %copy-start.10 = (bf16[8,256,128]{2,1,0:T(8,128)(2,1)S(1)}, bf16[8,256,128]{2,1,0:T(8,128)(2,1)}, u32[]{:S(2)}) copy-start(bf16[8,256,128]{2,1,0:T(8,128)(2,1)} %copy-done.9) | copy-start | bytes 1572868
  95.0 36.4 %all-to-all-start.2 = ((bf16[8,256,128]{2,1,0:T(8,128)(2,1)}), bf16[8,256,128]{2,1,0:T(8,128)(2,1)}, u32[]{:S(2)}, u32[]{:S(2)}) async-start(bf16[8,256,128]{2,1,0:T(8,128)(2,1)} %copy-done), calls=%async_computation.2 | async-start | bytes 1048576 | tf_op jit(solution)/shard_map/all_to_all | solution.py:347
  100.8 22.4 %collective-permute-start.10 = (bf16[8,256,128]{2,1,0:T(8,128)(2,1)S(1)}, bf16[8,256,128]{2,1,0:T(8,128)(2,1)S(1)}, u32[]{:S(2)}, u32[]{:S(2)}) collective-permute-start(bf16[8,256,128]{2,1,0:T(8,128)(2,1)S(1)} %copy-done.8), channel_id=1, source_target_pairs={{0,1},{1,0},{2,3},{3,2},{4,5},{5,4},{6,7},{7,6},{8,9},{9,8},{10,11... | collective-permute-start | bytes 1572872 | tf_op jit(solution)/shard_map/ppermute | solution.py:362
  100.9 10.3 %collective-permute-start.15 = (bf16[8,256,128]{2,1,0:T(8,128)(2,1)S(1)}, bf16[8,256,128]{2,1,0:T(8,128)(2,1)S(1)}, u32[]{:S(2)}, u32[]{:S(2)}) collective-permute-start(bf16[8,256,128]{2,1,0:T(8,128)(2,1)S(1)} %copy-done.10), channel_id=1, source_target_pairs={{0,1},{1,0},{2,3},{3,2},{4,5},{5,4},{6,7},{7,6},{8,9},{9,8},{10,11... | collective-permute-start | bytes 1572872 | tf_op jit(solution)/shard_map/ppermute | solution.py:362
  102.6 20.7 %collective-permute-start.17 = (bf16[4,256,128]{2,1,0:T(8,128)(2,1)S(1)}, bf16[4,256,128]{2,1,0:T(8,128)(2,1)S(1)}, u32[]{:S(2)}, u32[]{:S(2)}) collective-permute-start(bf16[4,256,128]{2,1,0:T(8,128)(2,1)S(1)} %slice.47), channel_id=1, source_target_pairs={{0,16},{16,32},{32,48},{48,0},{1,17},{17,33},{33,49},{49,1},{2,18}... | collective-permute-start | bytes 786440 | tf_op jit(solution)/shard_map/ppermute | solution.py:350
  104.8 13.1 %collective-permute-start.13 = (bf16[4,256,128]{2,1,0:T(8,128)(2,1)S(1)}, bf16[4,256,128]{2,1,0:T(8,128)(2,1)S(1)}, u32[]{:S(2)}, u32[]{:S(2)}) collective-permute-start(bf16[4,256,128]{2,1,0:T(8,128)(2,1)S(1)} %get-tuple-element.32), channel_id=1, source_target_pairs={{0,16},{16,32},{32,48},{48,0},{1,17},{17,33},{33,49},{49,1},{2,18}... | collective-permute-start | bytes 786440 | tf_op jit(solution)/shard_map/ppermute | solution.py:350
  111.2 10.4 %collective-permute-start.18 = (bf16[4,256,128]{2,1,0:T(8,128)(2,1)S(1)}, bf16[4,256,128]{2,1,0:T(8,128)(2,1)S(1)}, u32[]{:S(2)}, u32[]{:S(2)}) collective-permute-start(bf16[4,256,128]{2,1,0:T(8,128)(2,1)S(1)} %get-tuple-element.33), channel_id=1, source_target_pairs={{0,48},{16,0},{32,16},{48,32},{1,49},{17,1},{33,17},{49,33},{2,50}... | collective-permute-start | bytes 786440 | tf_op jit(solution)/shard_map/ppermute | solution.py:353
  111.4 13.7 %collective-permute-start.16 = (bf16[4,256,128]{2,1,0:T(8,128)(2,1)S(1)}, bf16[4,256,128]{2,1,0:T(8,128)(2,1)S(1)}, u32[]{:S(2)}, u32[]{:S(2)}) collective-permute-start(bf16[4,256,128]{2,1,0:T(8,128)(2,1)S(1)} %slice.45), channel_id=1, source_target_pairs={{0,48},{16,0},{32,16},{48,32},{1,49},{17,1},{33,17},{49,33},{2,50}... | collective-permute-start | bytes 786440 | tf_op jit(solution)/shard_map/ppermute | solution.py:353
  117.9 11.2 %collective-permute-start.14 = (bf16[4,256,128]{2,1,0:T(8,128)(2,1)S(1)}, bf16[4,256,128]{2,1,0:T(8,128)(2,1)S(1)}, u32[]{:S(2)}, u32[]{:S(2)}) collective-permute-start(bf16[4,256,128]{2,1,0:T(8,128)(2,1)S(1)} %add_convert_fusion.7), channel_id=1, source_target_pairs={{0,16},{16,32},{32,48},{48,0},{1,17},{17,33},{33,49},{49,1},{2,18}... | collective-permute-start | bytes 786440 | tf_op jit(solution)/shard_map/ppermute | solution.py:350
  121.7 8.6 %collective-permute-start.19 = (bf16[4,256,128]{2,1,0:T(8,128)(2,1)S(1)}, bf16[4,256,128]{2,1,0:T(8,128)(2,1)S(1)}, u32[]{:S(2)}, u32[]{:S(2)}) collective-permute-start(bf16[4,256,128]{2,1,0:T(8,128)(2,1)S(1)} %add_convert_fusion.5), channel_id=1, source_target_pairs={{0,48},{16,0},{32,16},{48,32},{1,49},{17,1},{33,17},{49,33},{2,50}... | collective-permute-start | bytes 786440 | tf_op jit(solution)/shard_map/ppermute | solution.py:353
  131.4 23.6 %all-to-all-start.3 = ((bf16[8,256,128]{2,1,0:T(8,128)(2,1)}), bf16[8,256,128]{2,1,0:T(8,128)(2,1)S(1)}, u32[]{:S(2)}, u32[]{:S(2)}) async-start(bf16[8,256,128]{2,1,0:T(8,128)(2,1)} %pad_maximum_fusion), calls=%async_computation.3 | async-start | bytes 1048576 | tf_op jit(solution)/shard_map/all_to_all | solution.py:347
  138.4 1.7 %collective-permute-start.20 = (bf16[8,256,128]{2,1,0:T(8,128)(2,1)}, bf16[8,256,128]{2,1,0:T(8,128)(2,1)S(1)}, u32[]{:S(2)}, u32[]{:S(2)}) collective-permute-start(bf16[8,256,128]{2,1,0:T(8,128)(2,1)} %all-to-all-done.2), channel_id=1, source_target_pairs={{0,0},{2,2},{4,4},{6,6},{8,56},{10,58},{12,60},{14,62},{16,16},{18... | collective-permute-start | bytes 1572872 | tf_op jit(solution)/shard_map/ppermute | solution.py:359
  140.1 14.9 %copy-start.14 = (bf16[8,256,128]{2,1,0:T(8,128)(2,1)}, bf16[8,256,128]{2,1,0:T(8,128)(2,1)S(1)}, u32[]{:S(2)}) copy-start(bf16[8,256,128]{2,1,0:T(8,128)(2,1)S(1)} %collective-permute-done.20.ad_ref) | copy-start | bytes 1572868
  (8 other events, 6.8 us)

commit v9 on v7

--- a/solution.py
+++ b/solution.py
@@ -379,18 +379,18 @@
     far = add(grads[4], twin(grads[5]))
     far, *grads = lax.optimization_barrier((far, *grads))
     sums = {distance: add(grads[2 * distance], twin(grads[2 * distance + 1])) for distance in (3, 1, 0)}
-    ad, sums[1], sums[3] = lax.optimization_barrier((ad, sums[1], sums[3]))
-    ad_back = over_heads(ad)
     k, v = slice(0, ROWS), slice(ROWS, 2 * ROWS)
     key_left = left(sums[3][:, k])
     key_relay = add(sums[1][:, k], right(far[:, k]))
     value_relay = add(sums[3][:, v], left(far[:, v]))
+    ad, key_relay, value_relay = lax.optimization_barrier((ad, key_relay, value_relay))
+    ad_back = over_heads(ad)
     key_right, value_left = right(key_relay), left(value_relay)
     value_right = right(sums[1][:, v])
-    key_right, ad_back = lax.optimization_barrier((key_right, ad_back))
     key_sum = add(sums[0][:, k], key_right, key_left)
     value_sum = add(sums[0][:, v], value_right, value_left)
     sums = jnp.concatenate([key_sum, value_sum], axis=1)
+    sums, ad_back = lax.optimization_barrier((sums, ad_back))
     return unpack(swap(ad_back), over_heads(sums))
 
 

time: 157 us -> 155 us (0.987)
  the two profiles are of different devices: /device:TPU:24 before, /device:TPU:14 now
where the time goes in v9:
time: 155 us; the launch traced here: 153 us
  waiting for transfers between devices  55.5 us (36%)
  starting transfers between devices  53.8 us (35%)
  Pallas kernels  38.5 us (25%)
  local copies, waits for them, and re-layouts  2.58 us (2%)
  other arithmetic  1.84 us (1%)
    pallas_call x1, Pallas kernels, attention(): pl.pallas_call(attention_kernel, out_shape=outs, in_specs=[pl.BlockSpec(m...  32.4 us
    all_to_all x4, starting transfers between devices, over_heads(): return lax.all_to_all(arr, 'z', split_axis=0, concat_axis=0, tiled=True)  29.2 us
    all_to_all x4, waiting for transfers between devices, over_heads(): return lax.all_to_all(arr, 'z', split_axis=0, concat_axis=0, tiled=True)  26.3 us
    ppermute x5, waiting for transfers between devices, right(): return lax.ppermute(arr, 'x', [(i, (i + 1) % XS) for i in range(XS)])  13.9 us
    ppermute x5, waiting for transfers between devices, left(): return lax.ppermute(arr, 'x', [(i, (i + XS - 1) % XS) for i in range(XS)])  13.7 us
    ppermute x5, starting transfers between devices, right(): return lax.ppermute(arr, 'x', [(i, (i + 1) % XS) for i in range(XS)])  12.9 us
    ppermute x2, starting transfers between devices, swap(): return lax.ppermute(arr, ('x', 'z'), pairs)  6.52 us
    pallas_call x2, Pallas kernels, pack(): pl.pallas_call(pack_kernel, out_shape=jax.ShapeDtypeStruct((HEADS, 2 * RO...  3.88 us
  transfers between devices with their start and end apart: 25, of which 12 were waited for; matrix products, arithmetic and copies ran while one was open for 1% of the time, Pallas kernels for 1%

profile of v9, /device:TPU:14, one launch (start us, length us, event | category | flops | bytes accessed | tf_op | source)
XLA Modules:
  0.0 153.2 jit_solution(965419322326107229)
XLA Ops:
  0.6 1.9 %shard_map.84 = bf16[8,272,128]{2,1,0:T(8,128)(2,1)} custom-call(bf16[1,128,1024]{2,1,0:T(8,128)(2,1)} %a_ref.2, bf16[1,128,1024]{2,1,0:T(8,128)(2,1)} %b_ref.2, s32[1,128]{1,0:T(1,128)} %scale_ref.3), custom_call_target="tpu_custom_call" | custom-call | tf_op jit(solution)/shard_map/pallas_call | solution.py:301
  2.6 8.5 %all-to-all-start = ((bf16[8,272,128]{2,1,0:T(8,128)(2,1)}), bf16[8,272,128]{2,1,0:T(8,128)(2,1)S(1)}, u32[]{:S(2)}, u32[]{:S(2)}) async-start(bf16[8,272,128]{2,1,0:T(8,128)(2,1)} %shard_map.84), calls=%async_computation | async-start | bytes 1114112 | tf_op jit(solution)/shard_map/all_to_all | solution.py:347
  11.0 1.9 %shard_map.85 = bf16[8,272,128]{2,1,0:T(8,128)(2,1)} custom-call(bf16[1,128,1024]{2,1,0:T(8,128)(2,1)} %a_ref.3, bf16[1,128,1024]{2,1,0:T(8,128)(2,1)} %b_ref.3, s32[1,128]{1,0:T(1,128)} %scale_ref.3), custom_call_target="tpu_custom_call" | custom-call | tf_op jit(solution)/shard_map/pallas_call | solution.py:301
  13.0 5.8 %collective-permute-start = (bf16[8,272,128]{2,1,0:T(8,128)(2,1)}, bf16[8,272,128]{2,1,0:T(8,128)(2,1)}, u32[]{:S(2)}, u32[]{:S(2)}) collective-permute-start(bf16[8,272,128]{2,1,0:T(8,128)(2,1)} %shard_map.85), channel_id=1, source_target_pairs={{0,0},{2,2},{4,4},{6,6},{8,56},{10,58},{12,60},{14,62},{16,16},{18... | collective-permute-start | bytes 1671176 | tf_op jit(solution)/shard_map/ppermute | solution.py:359
  18.8 10.4 %all-to-all-done.refs_0_ = bf16[8,272,128]{2,1,0:T(8,128)(2,1)S(1)} async-done(((bf16[8,272,128]{2,1,0:T(8,128)(2,1)}), bf16[8,272,128]{2,1,0:T(8,128)(2,1)S(1)}, u32[]{:S(2)}, u32[]{:S(2)}) %all-to-all-start) | async-done | bytes 557088 | tf_op jit(solution)/shard_map/all_to_all | solution.py:347
  29.2 0.8 collective-permute-start.4
  30.1 2.4 %collective-permute-start.2 = (bf16[8,272,128]{2,1,0:T(8,128)(2,1)S(1)}, bf16[8,272,128]{2,1,0:T(8,128)(2,1)S(1)}, u32[]{:S(2)}, u32[]{:S(2)}) collective-permute-start(bf16[8,272,128]{2,1,0:T(8,128)(2,1)S(1)} %all-to-all-done.refs_0_), channel_id=1, source_target_pairs={{0,16},{16,32},{32,48},{48,0},{1,17},{17,33},{33,49},{49,1},{2,18}... | collective-permute-start | bytes 1671176 | tf_op jit(solution)/shard_map/ppermute | solution.py:350
  32.5 8.2 %all-to-all-start.1 = ((bf16[8,272,128]{2,1,0:T(8,128)(2,1)}), bf16[8,272,128]{2,1,0:T(8,128)(2,1)S(1)}, u32[]{:S(2)}, u32[]{:S(2)}) async-start(bf16[8,272,128]{2,1,0:T(8,128)(2,1)} %collective-permute-done), calls=%async_computation.1 | async-start | bytes 1114112 | tf_op jit(solution)/shard_map/all_to_all | solution.py:347
  40.6 4.3 %collective-permute-done.4.refs_4_ = bf16[8,272,128]{2,1,0:T(8,128)(2,1)S(1)} collective-permute-done((bf16[8,272,128]{2,1,0:T(8,128)(2,1)S(1)}, bf16[8,272,128]{2,1,0:T(8,128)(2,1)S(1)}, u32[]{:S(2)}, u32[]{:S(2)}) %collective-permute-start.4) | collective-permute-done | bytes 557088 | tf_op jit(solution)/shard_map/ppermute | solution.py:353
  45.1 3.3 %collective-permute-start.6 = (bf16[4,272,128]{2,1,0:T(8,128)(2,1)S(1)}, bf16[4,272,128]{2,1,0:T(8,128)(2,1)}, u32[]{:S(2)}, u32[]{:S(2)}) collective-permute-start(bf16[4,272,128]{2,1,0:T(8,128)(2,1)S(1)} %slice.40), channel_id=1, source_target_pairs={{0,16},{16,32},{32,48},{48,0},{1,17},{17,33},{33,49},{49,1},{2,18}... | collective-permute-start | bytes 835592 | tf_op jit(solution)/shard_map/ppermute | solution.py:350
  48.9 5.1 %collective-permute-done.8.refs_8_ = bf16[4,272,128]{2,1,0:T(8,128)(2,1)S(1)} collective-permute-done((bf16[4,272,128]{2,1,0:T(8,128)(2,1)S(1)}, bf16[4,272,128]{2,1,0:T(8,128)(2,1)S(1)}, u32[]{:S(2)}, u32[]{:S(2)}) %collective-permute-start.8) | collective-permute-done | bytes 278560 | tf_op jit(solution)/shard_map/ppermute | solution.py:353
  54.0 0.7 copy-done
  55.3 1.5 all-to-all-done.1.refs_10_
  56.8 0.9 copy-done.1
  57.8 32.4 %shard_map.86 = (bf16[8,256,128]{2,1,0:T(8,128)(2,1)}, bf16[8,256,128]{2,1,0:T(8,128)(2,1)S(1)}, bf16[8,256,128]{2,1,0:T(8,128)(2,1)}, bf16[8,256,128]{2,1,0:T(8...) custom-call(s32[2]{0:T(128)S(1)} %pad_add_fusion.at_ref, ...), custom_call_target="tpu_custom_call" | custom-call | flops 8000000000 | bytes 10485760 | tf_op jit(solution)/shard_map/pallas_call | solution.py:257
  90.2 1.0 collective-permute-start.10
  91.2 1.5 %collective-permute-done.10 = bf16[8,256,128]{2,1,0:T(8,128)(2,1)S(1)} collective-permute-done((bf16[8,256,128]{2,1,0:T(8,128)(2,1)S(1)}, bf16[8,256,128]{2,1,0:T(8,128)(2,1)S(1)}, u32[]{:S(2)}, u32[]{:S(2)}) %collective-permute-start.10) | collective-permute-done | bytes 524320 | tf_op jit(solution)/shard_map/ppermute | solution.py:362
  93.6 3.6 %collective-permute-start.13 = (bf16[8,128,128]{2,1,0:T(8,128)(2,1)S(1)}, bf16[8,128,128]{2,1,0:T(8,128)(2,1)S(1)}, u32[]{:S(2)}, u32[]{:S(2)}) collective-permute-start(bf16[8,128,128]{2,1,0:T(8,128)(2,1)S(1)} %get-tuple-element.53), channel_id=1, source_target_pairs={{0,16},{16,32},{32,48},{48,0},{1,17},{17,33},{33,49},{49,1},{2,18}... | collective-permute-start | bytes 786440 | tf_op jit(solution)/shard_map/ppermute | solution.py:350
  97.4 5.7 %collective-permute-done.13 = bf16[8,128,128]{2,1,0:T(8,128)(2,1)S(1)} collective-permute-done((bf16[8,128,128]{2,1,0:T(8,128)(2,1)S(1)}, bf16[8,128,128]{2,1,0:T(8,128)(2,1)S(1)}, u32[]{:S(2)}, u32[]{:S(2)}) %collective-permute-start.13) | collective-permute-done | bytes 262176 | tf_op jit(solution)/shard_map/ppermute | solution.py:350
  103.2 0.6 collective-permute-done.15
  103.8 5.6 %all-to-all-start.2 = ((bf16[8,256,128]{2,1,0:T(8,128)(2,1)}), bf16[8,256,128]{2,1,0:T(8,128)(2,1)S(1)}, u32[]{:S(2)}, u32[]{:S(2)}) async-start(bf16[8,256,128]{2,1,0:T(8,128)(2,1)} %get-tuple-element.47), calls=%async_computation.2 | async-start | bytes 1048576 | tf_op jit(solution)/shard_map/all_to_all | solution.py:347
  109.5 3.2 %collective-permute-start.18 = (bf16[8,128,128]{2,1,0:T(8,128)(2,1)S(1)}, bf16[8,128,128]{2,1,0:T(8,128)(2,1)S(1)}, u32[]{:S(2)}, u32[]{:S(2)}) collective-permute-start(bf16[8,128,128]{2,1,0:T(8,128)(2,1)S(1)} %slice.47), channel_id=1, source_target_pairs={{0,16},{16,32},{32,48},{48,0},{1,17},{17,33},{33,49},{49,1},{2,18}... | collective-permute-start | bytes 786440 | tf_op jit(solution)/shard_map/ppermute | solution.py:350
  113.1 1.6 %collective-permute-start.19 = (bf16[8,128,128]{2,1,0:T(8,128)(2,1)S(1)}, bf16[8,128,128]{2,1,0:T(8,128)(2,1)S(1)}, u32[]{:S(2)}, u32[]{:S(2)}) collective-permute-start(bf16[8,128,128]{2,1,0:T(8,128)(2,1)S(1)} %add_convert_fusion.6), channel_id=1, source_target_pairs={{0,48},{16,0},{32,16},{48,32},{1,49},{17,1},{33,17},{49,33},{2,50}... | collective-permute-start | bytes 786440 | tf_op jit(solution)/shard_map/ppermute | solution.py:353
  114.9 4.6 %collective-permute-done.18 = bf16[8,128,128]{2,1,0:T(8,128)(2,1)S(1)} collective-permute-done((bf16[8,128,128]{2,1,0:T(8,128)(2,1)S(1)}, bf16[8,128,128]{2,1,0:T(8,128)(2,1)S(1)}, u32[]{:S(2)}, u32[]{:S(2)}) %collective-permute-start.18) | collective-permute-done | bytes 262176 | tf_op jit(solution)/shard_map/ppermute | solution.py:350
  119.4 3.7 %collective-permute-done.16 = bf16[8,128,128]{2,1,0:T(8,128)(2,1)S(1)} collective-permute-done((bf16[8,128,128]{2,1,0:T(8,128)(2,1)S(1)}, bf16[8,128,128]{2,1,0:T(8,128)(2,1)S(1)}, u32[]{:S(2)}, u32[]{:S(2)}) %collective-permute-start.16) | collective-permute-done | bytes 262176 | tf_op jit(solution)/shard_map/ppermute | solution.py:350
  123.6 3.3 %collective-permute-done.17 = bf16[8,128,128]{2,1,0:T(8,128)(2,1)S(1)} collective-permute-done((bf16[8,128,128]{2,1,0:T(8,128)(2,1)S(1)}, bf16[8,128,128]{2,1,0:T(8,128)(2,1)S(1)}, u32[]{:S(2)}, u32[]{:S(2)}) %collective-permute-start.17) | collective-permute-done | bytes 262176 | tf_op jit(solution)/shard_map/ppermute | solution.py:353
  127.1 0.8 pad_maximum_fusion
  127.9 6.9 %all-to-all-start.3 = ((bf16[8,256,128]{2,1,0:T(8,128)(2,1)}), bf16[8,256,128]{2,1,0:T(8,128)(2,1)S(1)}, u32[]{:S(2)}, u32[]{:S(2)}) async-start(bf16[8,256,128]{2,1,0:T(8,128)(2,1)} %pad_maximum_fusion), calls=%async_computation.3 | async-start | bytes 1048576 | tf_op jit(solution)/shard_map/all_to_all | solution.py:347
  134.9 0.7 collective-permute-start.20
  135.6 14.4 %all-to-all-done.3.dkv_ref = bf16[8,256,128]{2,1,0:T(8,128)(2,1)S(1)} async-done(((bf16[8,256,128]{2,1,0:T(8,128)(2,1)}), bf16[8,256,128]{2,1,0:T(8,128)(2,1)S(1)}, u32[]{:S(2)}, u32[]{:S(2)}) %all-to-all-start.3) | async-done | bytes 524320 | tf_op jit(solution)/shard_map/all_to_all | solution.py:347
  150.0 0.8 copy-done.2
  150.8 2.2 %shard_map.87 = (bf16[1,128,1024]{2,1,0:T(8,128)(2,1)}, bf16[1,128,1024]{2,1,0:T(8,128)(2,1)}, bf16[1,128,1024]{2,1,0:T(8,128)(2,1)}, bf16[1,128,1024]{2,1,0:T(8,128)(2,1)}) custom-call(bf16[8,256,128]{2,1,0:T(8,128)(2,1)} %copy-done.3, bf16[8,256,128]{2,1,0:T(8,128)(2,1)} %copy-done.2), custom_call_target="tpu_custom_call" | custom-call | tf_op jit(solution)/shard_map/pallas_call | solution.py:326
  (44 shorter events, 3.9 us)
Async XLA Ops:
  2.6 26.7 %all-to-all-start = ((bf16[8,272,128]{2,1,0:T(8,128)(2,1)}), bf16[8,272,128]{2,1,0:T(8,128)(2,1)S(1)}, u32[]{:S(2)}, u32[]{:S(2)}) async-start(bf16[8,272,128]{2,1,0:T(8,128)(2,1)} %shard_map.84), calls=%async_computation | async-start | bytes 1114112 | tf_op jit(solution)/shard_map/all_to_all | solution.py:347
  13.0 5.8 %collective-permute-start = (bf16[8,272,128]{2,1,0:T(8,128)(2,1)}, bf16[8,272,128]{2,1,0:T(8,128)(2,1)}, u32[]{:S(2)}, u32[]{:S(2)}) collective-permute-start(bf16[8,272,128]{2,1,0:T(8,128)(2,1)} %shard_map.85), channel_id=1, source_target_pairs={{0,0},{2,2},{4,4},{6,6},{8,56},{10,58},{12,60},{14,62},{16,16},{18... | collective-permute-start | bytes 1671176 | tf_op jit(solution)/shard_map/ppermute | solution.py:359
  29.2 15.8 %collective-permute-start.4 = (bf16[8,272,128]{2,1,0:T(8,128)(2,1)S(1)}, bf16[8,272,128]{2,1,0:T(8,128)(2,1)S(1)}, u32[]{:S(2)}, u32[]{:S(2)}) collective-permute-start(bf16[8,272,128]{2,1,0:T(8,128)(2,1)S(1)} %all-to-all-done.refs_0_), channel_id=1, source_target_pairs={{0,48},{16,0},{32,16},{48,32},{1,49},{17,1},{33,17},{49,33},{2,50}... | collective-permute-start | bytes 1671176 | tf_op jit(solution)/shard_map/ppermute | solution.py:353
  30.1 15.0 %collective-permute-start.2 = (bf16[8,272,128]{2,1,0:T(8,128)(2,1)S(1)}, bf16[8,272,128]{2,1,0:T(8,128)(2,1)S(1)}, u32[]{:S(2)}, u32[]{:S(2)}) collective-permute-start(bf16[8,272,128]{2,1,0:T(8,128)(2,1)S(1)} %all-to-all-done.refs_0_), channel_id=1, source_target_pairs={{0,16},{16,32},{32,48},{48,0},{1,17},{17,33},{33,49},{49,1},{2,18}... | collective-permute-start | bytes 1671176 | tf_op jit(solution)/shard_map/ppermute | solution.py:350
  32.5 24.3 %all-to-all-start.1 = ((bf16[8,272,128]{2,1,0:T(8,128)(2,1)}), bf16[8,272,128]{2,1,0:T(8,128)(2,1)S(1)}, u32[]{:S(2)}, u32[]{:S(2)}) async-start(bf16[8,272,128]{2,1,0:T(8,128)(2,1)} %collective-permute-done), calls=%async_computation.1 | async-start | bytes 1114112 | tf_op jit(solution)/shard_map/all_to_all | solution.py:347
  40.6 14.7 %collective-permute-start.1 = (bf16[8,272,128]{2,1,0:T(8,128)(2,1)S(1)}, bf16[8,272,128]{2,1,0:T(8,128)(2,1)S(1)}, u32[]{:S(2)}, u32[]{:S(2)}) collective-permute-start(bf16[8,272,128]{2,1,0:T(8,128)(2,1)S(1)} %all-to-all-done.refs_0_), channel_id=1, source_target_pairs={{0,1},{1,0},{2,3},{3,2},{4,5},{5,4},{6,7},{7,6},{8,9},{9,8},{10,11... | collective-permute-start | bytes 1671176 | tf_op jit(solution)/shard_map/ppermute | solution.py:362
  45.0 9.0 %collective-permute-start.8 = (bf16[4,272,128]{2,1,0:T(8,128)(2,1)S(1)}, bf16[4,272,128]{2,1,0:T(8,128)(2,1)S(1)}, u32[]{:S(2)}, u32[]{:S(2)}) collective-permute-start(bf16[4,272,128]{2,1,0:T(8,128)(2,1)S(1)} %slice.41), channel_id=1, source_target_pairs={{0,48},{16,0},{32,16},{48,32},{1,49},{17,1},{33,17},{49,33},{2,50}... | collective-permute-start | bytes 835592 | tf_op jit(solution)/shard_map/ppermute | solution.py:353
  45.1 9.6 %collective-permute-start.6 = (bf16[4,272,128]{2,1,0:T(8,128)(2,1)S(1)}, bf16[4,272,128]{2,1,0:T(8,128)(2,1)}, u32[]{:S(2)}, u32[]{:S(2)}) collective-permute-start(bf16[4,272,128]{2,1,0:T(8,128)(2,1)S(1)} %slice.40), channel_id=1, source_target_pairs={{0,16},{16,32},{32,48},{48,0},{1,17},{17,33},{33,49},{49,1},{2,18}... | collective-permute-start | bytes 835592 | tf_op jit(solution)/shard_map/ppermute | solution.py:350
  48.4 8.4 %collective-permute-start.5 = (bf16[8,272,128]{2,1,0:T(8,128)(2,1)S(1)}, bf16[8,272,128]{2,1,0:T(8,128)(2,1)}, u32[]{:S(2)}, u32[]{:S(2)}) collective-permute-start(bf16[8,272,128]{2,1,0:T(8,128)(2,1)S(1)} %collective-permute-done.4.refs_4_), channel_id=1, source_target_pairs={{0,1},{1,0},{2,3},{3,2},{4,5},{5,4},{6,7},{7,6},{8,9},{9,8},{10,11... | collective-permute-start | bytes 1671176 | tf_op jit(solution)/shard_map/ppermute | solution.py:362
  48.4 8.4 %collective-permute-start.3 = (bf16[8,272,128]{2,1,0:T(8,128)(2,1)S(1)}, bf16[8,272,128]{2,1,0:T(8,128)(2,1)}, u32[]{:S(2)}, u32[]{:S(2)}) collective-permute-start(bf16[8,272,128]{2,1,0:T(8,128)(2,1)S(1)} %collective-permute-done.2.refs_2_), channel_id=1, source_target_pairs={{0,1},{1,0},{2,3},{3,2},{4,5},{5,4},{6,7},{7,6},{8,9},{9,8},{10,11... | collective-permute-start | bytes 1671176 | tf_op jit(solution)/shard_map/ppermute | solution.py:362
  54.0 2.8 %collective-permute-start.9 = (bf16[4,272,128]{2,1,0:T(8,128)(2,1)S(1)}, bf16[4,272,128]{2,1,0:T(8,128)(2,1)}, u32[]{:S(2)}, u32[]{:S(2)}) collective-permute-start(bf16[4,272,128]{2,1,0:T(8,128)(2,1)S(1)} %collective-permute-done.8.refs_8_), channel_id=1, source_target_pairs={{0,1},{1,0},{2,3},{3,2},{4,5},{5,4},{6,7},{7,6},{8,9},{9,8},{10,11... | collective-permute-start | bytes 835592 | tf_op jit(solution)/shard_map/ppermute | solution.py:362
  54.0 0.7 copy-start
  54.7 2.1 %collective-permute-start.7 = (bf16[4,272,128]{2,1,0:T(8,128)(2,1)}, bf16[4,272,128]{2,1,0:T(8,128)(2,1)}, u32[]{:S(2)}, u32[]{:S(2)}) collective-permute-start(bf16[4,272,128]{2,1,0:T(8,128)(2,1)} %collective-permute-done.6.refs_6_), channel_id=1, source_target_pairs={{0,1},{1,0},{2,3},{3,2},{4,5},{5,4},{6,7},{7,6},{8,9},{9,8},{10,11... | collective-permute-start | bytes 835592 | tf_op jit(solution)/shard_map/ppermute | solution.py:362
  56.8 1.0 copy-start.1
  90.2 2.5 %collective-permute-start.10 = (bf16[8,256,128]{2,1,0:T(8,128)(2,1)S(1)}, bf16[8,256,128]{2,1,0:T(8,128)(2,1)S(1)}, u32[]{:S(2)}, u32[]{:S(2)}) collective-permute-start(bf16[8,256,128]{2,1,0:T(8,128)(2,1)S(1)} %get-tuple-element.30), channel_id=1, source_target_pairs={{0,1},{1,0},{2,3},{3,2},{4,5},{5,4},{6,7},{7,6},{8,9},{9,8},{10,11... | collective-permute-start | bytes 1572872 | tf_op jit(solution)/shard_map/ppermute | solution.py:362
  92.8 4.3 %collective-permute-start.12 = (bf16[8,256,128]{2,1,0:T(8,128)(2,1)S(1)}, bf16[8,256,128]{2,1,0:T(8,128)(2,1)S(1)}, u32[]{:S(2)}, u32[]{:S(2)}) collective-permute-start(bf16[8,256,128]{2,1,0:T(8,128)(2,1)S(1)} %get-tuple-element.41), channel_id=1, source_target_pairs={{0,1},{1,0},{2,3},{3,2},{4,5},{5,4},{6,7},{7,6},{8,9},{9,8},{10,11... | collective-permute-start | bytes 1572872 | tf_op jit(solution)/shard_map/ppermute | solution.py:362
  93.3 4.0 %collective-permute-start.14 = (bf16[8,256,128]{2,1,0:T(8,128)(2,1)S(1)}, bf16[8,256,128]{2,1,0:T(8,128)(2,1)S(1)}, u32[]{:S(2)}, u32[]{:S(2)}) collective-permute-start(bf16[8,256,128]{2,1,0:T(8,128)(2,1)S(1)} %get-tuple-element.44), channel_id=1, source_target_pairs={{0,1},{1,0},{2,3},{3,2},{4,5},{5,4},{6,7},{7,6},{8,9},{9,8},{10,11... | collective-permute-start | bytes 1572872 | tf_op jit(solution)/shard_map/ppermute | solution.py:362
  93.5 10.3 %collective-permute-start.15 = (bf16[8,128,128]{2,1,0:T(8,128)(2,1)S(1)}, bf16[8,128,128]{2,1,0:T(8,128)(2,1)S(1)}, u32[]{:S(2)}, u32[]{:S(2)}) collective-permute-start(bf16[8,128,128]{2,1,0:T(8,128)(2,1)S(1)} %get-tuple-element.52), channel_id=1, source_target_pairs={{0,48},{16,0},{32,16},{48,32},{1,49},{17,1},{33,17},{49,33},{2,50}... | collective-permute-start | bytes 786440 | tf_op jit(solution)/shard_map/ppermute | solution.py:353
  93.6 9.5 %collective-permute-start.13 = (bf16[8,128,128]{2,1,0:T(8,128)(2,1)S(1)}, bf16[8,128,128]{2,1,0:T(8,128)(2,1)S(1)}, u32[]{:S(2)}, u32[]{:S(2)}) collective-permute-start(bf16[8,128,128]{2,1,0:T(8,128)(2,1)S(1)} %get-tuple-element.53), channel_id=1, source_target_pairs={{0,16},{16,32},{32,48},{48,0},{1,17},{17,33},{33,49},{49,1},{2,18}... | collective-permute-start | bytes 786440 | tf_op jit(solution)/shard_map/ppermute | solution.py:350
  97.1 17.6 %collective-permute-start.11 = (bf16[8,256,128]{2,1,0:T(8,128)(2,1)}, bf16[8,256,128]{2,1,0:T(8,128)(2,1)S(1)}, u32[]{:S(2)}, u32[]{:S(2)}) collective-permute-start(bf16[8,256,128]{2,1,0:T(8,128)(2,1)} %get-tuple-element.38), channel_id=1, source_target_pairs={{0,1},{1,0},{2,3},{3,2},{4,5},{5,4},{6,7},{7,6},{8,9},{9,8},{10,11... | collective-permute-start | bytes 1572872 | tf_op jit(solution)/shard_map/ppermute | solution.py:362
  103.8 24.1 %all-to-all-start.2 = ((bf16[8,256,128]{2,1,0:T(8,128)(2,1)}), bf16[8,256,128]{2,1,0:T(8,128)(2,1)S(1)}, u32[]{:S(2)}, u32[]{:S(2)}) async-start(bf16[8,256,128]{2,1,0:T(8,128)(2,1)} %get-tuple-element.47), calls=%async_computation.2 | async-start | bytes 1048576 | tf_op jit(solution)/shard_map/all_to_all | solution.py:347
  109.5 10.0 %collective-permute-start.18 = (bf16[8,128,128]{2,1,0:T(8,128)(2,1)S(1)}, bf16[8,128,128]{2,1,0:T(8,128)(2,1)S(1)}, u32[]{:S(2)}, u32[]{:S(2)}) collective-permute-start(bf16[8,128,128]{2,1,0:T(8,128)(2,1)S(1)} %slice.47), channel_id=1, source_target_pairs={{0,16},{16,32},{32,48},{48,0},{1,17},{17,33},{33,49},{49,1},{2,18}... | collective-permute-start | bytes 786440 | tf_op jit(solution)/shard_map/ppermute | solution.py:350
  112.7 10.5 %collective-permute-start.16 = (bf16[8,128,128]{2,1,0:T(8,128)(2,1)S(1)}, bf16[8,128,128]{2,1,0:T(8,128)(2,1)S(1)}, u32[]{:S(2)}, u32[]{:S(2)}) collective-permute-start(bf16[8,128,128]{2,1,0:T(8,128)(2,1)S(1)} %add_convert_fusion.7), channel_id=1, source_target_pairs={{0,16},{16,32},{32,48},{48,0},{1,17},{17,33},{33,49},{49,1},{2,18}... | collective-permute-start | bytes 786440 | tf_op jit(solution)/shard_map/ppermute | solution.py:350
  113.1 10.5 %collective-permute-start.19 = (bf16[8,128,128]{2,1,0:T(8,128)(2,1)S(1)}, bf16[8,128,128]{2,1,0:T(8,128)(2,1)S(1)}, u32[]{:S(2)}, u32[]{:S(2)}) collective-permute-start(bf16[8,128,128]{2,1,0:T(8,128)(2,1)S(1)} %add_convert_fusion.6), channel_id=1, source_target_pairs={{0,48},{16,0},{32,16},{48,32},{1,49},{17,1},{33,17},{49,33},{2,50}... | collective-permute-start | bytes 786440 | tf_op jit(solution)/shard_map/ppermute | solution.py:353
  114.7 12.2 %collective-permute-start.17 = (bf16[8,128,128]{2,1,0:T(8,128)(2,1)S(1)}, bf16[8,128,128]{2,1,0:T(8,128)(2,1)S(1)}, u32[]{:S(2)}, u32[]{:S(2)}) collective-permute-start(bf16[8,128,128]{2,1,0:T(8,128)(2,1)S(1)} %slice.45), channel_id=1, source_target_pairs={{0,48},{16,0},{32,16},{48,32},{1,49},{17,1},{33,17},{49,33},{2,50}... | collective-permute-start | bytes 786440 | tf_op jit(solution)/shard_map/ppermute | solution.py:353
  127.9 22.1 %all-to-all-start.3 = ((bf16[8,256,128]{2,1,0:T(8,128)(2,1)}), bf16[8,256,128]{2,1,0:T(8,128)(2,1)S(1)}, u32[]{:S(2)}, u32[]{:S(2)}) async-start(bf16[8,256,128]{2,1,0:T(8,128)(2,1)} %pad_maximum_fusion), calls=%async_computation.3 | async-start | bytes 1048576 | tf_op jit(solution)/shard_map/all_to_all | solution.py:347
  134.9 0.7 collective-permute-start.20
  135.6 14.5 %copy-start.3 = (bf16[8,256,128]{2,1,0:T(8,128)(2,1)}, bf16[8,256,128]{2,1,0:T(8,128)(2,1)S(1)}, u32[]{:S(2)}) copy-start(bf16[8,256,128]{2,1,0:T(8,128)(2,1)S(1)} %collective-permute-done.20.ad_ref) | copy-start | bytes 1572868
  150.0 0.8 copy-start.2
